TPU v7x, 256 devices: a whole 4x4x8 slice. The times are simulated.
256 devices in a mesh: seq: 64 (over y, z, core), batch: 4 (over x).
Axes of the slice: x: 4, y: 4, z: 8, core: 2. Of those that a mesh axis runs over, the one named last changes fastest.
Arguments:
- query: bfloat16 [65536, 512], P(('batch', 'seq')), parts along dimension 0, may hold values from -104 to 104
- key_rows: bfloat16 [65536, 512], P(('batch', 'seq')), parts along dimension 0, may hold values from -4 to 4
- value_rows: bfloat16 [65536, 512], P(('batch', 'seq')), parts along dimension 0, may hold values from -6 to 6
- out_grad: bfloat16 [65536, 512], P(('batch', 'seq')), parts along dimension 0, may hold values from -6 to 6
Outputs:
- attended: bfloat16 [65536, 512], P(('batch', 'seq')), parts along dimension 0
- query_grad: bfloat16 [65536, 512], P(('batch', 'seq')), parts along dimension 0
- key_grad: bfloat16 [65536, 512], P(('batch', 'seq')), parts along dimension 0
- value_grad: bfloat16 [65536, 512], P(('batch', 'seq')), parts along dimension 0
There are 4 independent parts, one for each index of `batch`. A program takes and returns all parts, laid end to end along the dimension named above; each array names one. Nothing has to cross between parts.
All inputs are finite; a program needn't handle non-finite values.
Results may differ from a plain program's by a relative error of at most 0.02.
Values may be sent and summed in bfloat16 or wider, within the bound.
No kernel may reach another device: no remote copies, remote signals or barrier semaphores. Data moves between devices by JAX's collectives and lax.ppermute only.
A program may use at most 128 MiB of HBM per device.

v0:
```python
import jax
import jax.numpy as jnp
from jax import lax
from jax.experimental import pallas as pl
from jax.experimental.pallas import tpu as pltpu
from jax.sharding import PartitionSpec as P

HEADS = 4
HEAD = 128
D = HEADS * HEAD
ROWS = 256
FULL = 2 * D
SCALE = HEAD**-0.5
LOG2E = 1.4426950408889634
EXP_SCALE = SCALE * LOG2E
NEG = -1e30
VMEM_LIMIT = 40 * 1024 * 1024
BF = jnp.bfloat16
F32 = jnp.float32

RUN = 16


def place():
    index = lax.axis_index("seq")
    return lax.rem(index, 2), lax.div(index, 2)


def part(number, size):
    return pl.ds(pl.multiple_of(number * size, size), size)


def head(h):
    return slice(h * HEAD, (h + 1) * HEAD)


def order_matrix(back=False):
    a = lax.broadcasted_iota(jnp.int32, (128, 128), 0)
    b = lax.broadcasted_iota(jnp.int32, (128, 128), 1)
    row, token = (b, a) if back else (a, b)
    hit = row == (token & 7) * RUN + lax.shift_right_logical(token, 3)
    return jnp.where(hit, 1.0, 0.0).astype(BF)


def reorder(matrix, x):
    blocks = [jnp.dot(matrix, x[i : i + 128], preferred_element_type=F32) for i in range(0, x.shape[0], 128)]
    return jnp.concatenate(blocks, axis=0).astype(BF)


def coarse(x):
    rows, lanes = x.shape
    y = x.astype(F32).reshape(rows // (2 * RUN), 2, RUN, lanes)
    return ((y[:, 0] + y[:, 1]) * 0.5).reshape(rows // 2, lanes).astype(BF)


def expand(x, level=1):
    rows, lanes = x.shape
    step = 2**level
    y = jnp.broadcast_to(x.reshape(rows // RUN, 1, RUN, lanes), (rows // RUN, step, RUN, lanes))
    return y.reshape(rows * step, lanes)


def fold(x, level):
    rows, lanes = x.shape
    step = 2**level
    y = x.reshape(rows // (step * RUN), step, RUN, lanes)
    total = y[:, 0]
    for s in range(1, step):
        total = total + y[:, s]
    return total.reshape(rows // step, lanes)


def nt(a, b):
    return lax.dot_general(a, b, (((1,), (1,)), ((), ())), preferred_element_type=F32)


def tn(a, b):
    return lax.dot_general(a, b, (((0,), (0,)), ((), ())), preferred_element_type=F32)


def nn(a, b):
    return jnp.dot(a, b, preferred_element_type=F32)


def lanes128(value):
    return jnp.broadcast_to(value, (value.shape[0], HEAD))


def wide(value, count):
    return value if count == 1 else jnp.concatenate([value] * count, axis=1)


def penalty(ok):
    return jnp.where(ok, 0.0, NEG).astype(F32)


def half_masks():
    row = lax.broadcasted_iota(jnp.int32, (128, 128), 0) >= 64
    key = lax.broadcasted_iota(jnp.int32, (128, 128), 1) >= 64
    left = jnp.where(jnp.logical_and(~row, key), NEG, 0.0).astype(F32)
    right = jnp.where(jnp.logical_and(row, ~key), NEG, 0.0).astype(F32)
    return left, right


def soft(units):
    scores = [nt(q, k) if bias is None else nt(q, k) + bias for q, k, _, bias in units]
    peaks = [jnp.max(s, axis=1, keepdims=True) for s in scores]
    weights = [jnp.exp2((s - peak) * EXP_SCALE) for s, peak in zip(scores, peaks)]
    rounded = [e.astype(BF) for e in weights]
    mixes = [nn(eb, v) for eb, (_, _, v, _) in zip(rounded, units)]
    sums = [jnp.sum(e, axis=1, keepdims=True) for e in weights]
    return [
        (eb, lanes128(peak * EXP_SCALE), lanes128(den), mix)
        for eb, peak, den, mix in zip(rounded, peaks, sums, mixes)
    ]


def backward(units):
    inners = [nt(grad, v) for _, _, v, _, grad, _ in units]
    dvs = [tn(eb, grad) for _, _, _, eb, grad, _ in units]
    dscores = [
        (eb.astype(F32) * (inner - wide(drift, eb.shape[1] // HEAD))).astype(BF)
        for inner, (_, _, _, eb, _, drift) in zip(inners, units)
    ]
    dqs = [nn(dscore, k) * SCALE for dscore, (_, k, _, _, _, _) in zip(dscores, units)]
    dks = [tn(dscore, q) * SCALE for dscore, (q, _, _, _, _, _) in zip(dscores, units)]
    return list(zip(dqs, dks, dvs))


def merge(top, z, y, pieces):
    best = top
    peaks = [expand(m, level) if level else m for m, _, _, level in pieces]
    for m in peaks:
        best = jnp.maximum(best, m)
    f = jnp.exp2(top - best)
    z, y = f * z, f * y
    factors = []
    for m, (_, d, n, level) in zip(peaks, pieces):
        f = jnp.exp2(m - best)
        if level:
            f = f * 2.0**level
            d, n = expand(d, level), expand(n, level)
        factors.append(f)
        z = z + f * d
        y = y + f * n
    return best, z, y, factors


def placed(value, first, rows):
    zeros = jnp.zeros((rows, value.shape[1]), F32)
    return jnp.concatenate([jnp.where(first, value, zeros), jnp.where(first, zeros, value)], axis=0)


def pre_kernel(raw, kv, l1, l2, l3, sib):
    core, _ = place()
    matrix = order_matrix()
    for i in range(2):
        lanes = slice(i * D, (i + 1) * D)
        fine = reorder(matrix, raw[:, lanes])
        kv[:, lanes] = fine
        fine = coarse(fine)
        l1[:, lanes] = fine
        fine = coarse(fine)
        l2[:, lanes] = fine
        l3[:, lanes] = coarse(fine)
    sib[:128] = kv[part(1 - core, 128), :]
    sib[128:] = l1[part(core, 64), :]


def pack_kernel(kv, l1, l3, s2, msg1, msg2):
    core, _ = place()
    msg1[:128] = kv[part(core, 128), :]
    msg1[128:192] = l1[part(1 - core, 64), :]
    msg1[192:] = s2[...]
    msg2[:32] = l3[...]
    msg2[32:] = coarse(s2[...])


def local_kernel(q_ref, g_ref, kv, sib, q0, g0, q1, q2, q3, win, s1, e0, e1, m0, m1, top, zsum, ysum, d1, n1):
    core, _ = place()
    matrix = order_matrix()
    q0[...] = reorder(matrix, q_ref[...])
    g0[...] = reorder(matrix, g_ref[...])
    q1[...] = coarse(q0[...])
    q2[...] = coarse(q1[...])
    q3[...] = coarse(q2[...])
    win[:256] = kv[...]
    win[256:] = sib[:128]
    s1[part(core, 64), :] = coarse(sib[:128])
    s1[part(1 - core, 64), :] = sib[128:]
    left, right = half_masks()
    bias = jnp.where(core == 0, right, left)
    for h in range(HEADS):
        kl, vl = head(h), head(HEADS + h)
        blocks = ((1 - core, 384), (core, 256))
        units = [(q1[:, kl], s1[:, kl], s1[:, vl], bias)]
        units += [(q0[part(n, 128), kl], win[:keys, kl], win[:keys, vl], None) for n, keys in blocks]
        first, *fine = soft(units)
        e1[h], m1[h], d1[h], n1[h] = first
        for i, (number, keys) in enumerate(blocks):
            rows, half = part(number, 128), part(number, 64)
            e, m, d, n = fine[i]
            e0[h, i * 128 : (i + 1) * 128, :keys] = e
            m0[h, i * 128 : (i + 1) * 128] = m
            top[h, rows], zsum[h, rows], ysum[h, rows], _ = merge(
                m, d, n, [(m1[h, half], d1[h, half], n1[h, half], 1)]
            )


def second_split_kernel(r1, after, l1, send):
    core, _ = place()
    l1[part(core, 64), :] = r1[128:192]
    l1[part(1 - core, 64), :] = coarse(r1[:128])
    send[:64] = coarse(l1[...])
    send[64:] = r1[192:]


def third_split_kernel(r2, r3, after, send):
    send[:64] = r2[...]
    send[64:] = r3[...]


def outer_kernel(q0, q1, r1, l1, top, zsum, ysum, top_out, z_out, y_out, e0, e1, m0, m1, d1, n1):
    core, chip = place()
    is0 = core == 0
    bad = penalty(jnp.where(is0, chip >= 1, chip <= 30))
    left, right = half_masks()
    bias = jnp.where(is0, left, right) + bad
    outer = part(core, 128)
    units = []
    for h in range(HEADS):
        kl, vl = head(h), head(HEADS + h)
        units.append((q1[:, kl], l1[:, kl], l1[:, vl], bias))
        units.append((q0[outer, kl], r1[:128, kl], r1[:128, vl], bad))
    results = soft(units)
    for h in range(HEADS):
        e1[h], m1[h], d1[h], n1[h] = results[2 * h]
        e0[h], m, d, n = results[2 * h + 1]
        m0[h] = m
        for number in (core, 1 - core):
            rows, half = part(number, 128), part(number, 64)
            pieces = [(m1[h, half], d1[h, half], n1[h, half], 1)]
            if number is core:
                pieces.append((m, d, n, 0))
            top_out[h, rows], z_out[h, rows], y_out[h, rows], _ = merge(
                top[h, rows], zsum[h, rows], ysum[h, rows], pieces
            )


def second_kernel(q2, r1, got, top, zsum, ysum, after, win, e2, m2, top_out, z_out, y_out):
    core, chip = place()
    is0 = core == 0
    win[:64] = r1[192:]
    win[64:192] = got[...]
    win[192:] = jnp.zeros((64, FULL), BF)
    lane = lax.broadcasted_iota(jnp.int32, (1, 256), 1)
    left_ok, right_ok = chip >= 1, chip <= 30
    own_bad = penalty(jnp.where(is0, left_ok, right_ok))
    sib_bad = penalty(jnp.where(is0, right_ok, left_ok))
    bias = jnp.where(lane < 64, own_bad, jnp.where(lane < 192, sib_bad, NEG))
    results = soft([(q2[:, head(h)], win[:, head(h)], win[:, head(HEADS + h)], bias) for h in range(HEADS)])
    for h in range(HEADS):
        e2[h], m2[h], d, n = results[h]
        for c in range(2):
            r, a = slice(c * 128, (c + 1) * 128), slice(c * 32, (c + 1) * 32)
            top_out[h, r], z_out[h, r], y_out[h, r], _ = merge(
                top[h, r], zsum[h, r], ysum[h, r], [(m2[h, a], d[a], n[a], 2)]
            )


def far_kernel(
    q2, q3, g_ref, top, zsum, ysum, w2, e2, m2, r2, r3, got,
    att, best_out, inv_out, delta_out, dq2, dq3, own2, own3, cross3, send,
    w3,
):
    core, chip = place()
    is0 = core == 0
    w3[:64] = r2[...]
    w3[64:128] = got[:64]
    w3[128:160] = r3[...]
    w3[160:192] = got[64:]
    w3[192:] = jnp.zeros((64, FULL), BF)
    low2, high2 = chip >= 2, chip <= 29
    even = lax.rem(chip, 2) == 0
    cross_bad = penalty(jnp.where(even, chip <= 28, chip >= 3))
    lane = lax.broadcasted_iota(jnp.int32, (1, 256), 1)
    own_bad = penalty(jnp.where(is0, low2, high2))
    sib_bad = penalty(jnp.where(is0, high2, low2))
    bias3 = jnp.where(
        lane < 64, own_bad, jnp.where(lane < 128, sib_bad, jnp.where(lane < 192, cross_bad, NEG))
    )
    third = soft([(q3[:, head(h)], w3[:, head(h)], w3[:, head(HEADS + h)], bias3) for h in range(HEADS)])
    units = []
    for h in range(HEADS):
        kl, vl = head(h), head(HEADS + h)
        e3, m3, d3, n3 = third[h]
        grads = ([], [])
        drifts = ([], [])
        for c in range(2):
            r = slice(c * 128, (c + 1) * 128)
            a, b = slice(c * 32, (c + 1) * 32), slice(c * 16, (c + 1) * 16)
            best, z, y, factors = merge(top[h, r], zsum[h, r], ysum[h, r], [(m3[b], d3[b], n3[b], 3)])
            inv = 1.0 / z
            y = y * inv
            att[r, kl] = y.astype(BF)
            g = g_ref[r, kl].astype(F32)
            delta = lanes128(jnp.sum(g * y, axis=1, keepdims=True))
            best_out[h, r] = best
            inv_out[h, r] = inv
            delta_out[h, r] = delta
            factors = [4.0 * jnp.exp2(expand(m2[h, a], 2) - best)] + factors
            for i in range(2):
                share = factors[i] * inv
                grads[i].append(fold(share * g, i + 2))
                drifts[i].append(fold(share * delta, i + 2))
        for i, (q, w, e) in enumerate(((q2, w2, e2[h]), (q3, w3, e3))):
            grad = jnp.concatenate(grads[i], axis=0).astype(BF)
            units.append((q[:, kl], w[:, kl], w[:, vl], e, grad, jnp.concatenate(drifts[i], axis=0)))
    results = backward(units)
    for h in range(HEADS):
        for i in range(2):
            dq, dk, dv = results[2 * h + i]
            (dq2, dq3)[i][h] = dq
            for lanes, value in ((head(h), dk), (head(HEADS + h), dv)):
                if i == 0:
                    own2[:, lanes] = value[:64]
                    send[:128, lanes] = value[64:192].astype(BF)
                else:
                    own3[:, lanes] = value[:64]
                    send[128:192, lanes] = value[64:128].astype(BF)
                    cross3[:, lanes] = value[128:160]
                    send[192:, lanes] = value[160:192].astype(BF)


def coarse_grad(m, best, inv, g, delta):
    grads, drifts = [], []
    for c in range(2):
        r, half = slice(c * 128, (c + 1) * 128), slice(c * 64, (c + 1) * 64)
        share = jnp.exp2(expand(m[half]) - best[r]) * (2.0 * inv[r])
        grads.append(fold(share * g[r].astype(F32), 1))
        drifts.append(fold(share * delta[r], 1))
    return jnp.concatenate(grads, axis=0).astype(BF), jnp.concatenate(drifts, axis=0)


def outer_back_kernel(
    q0, q1, g_ref, r1, l1, e0, e1, m0, m1, best, inv_ref, delta_ref,
    dq0, dq1, d0, d1,
):
    core, _ = place()
    outer = part(core, 128)
    units = []
    for h in range(HEADS):
        kl, vl = head(h), head(HEADS + h)
        share = jnp.exp2(m0[h] - best[h, outer]) * inv_ref[h, outer]
        grad = (share * g_ref[outer, kl].astype(F32)).astype(BF)
        drift = share * delta_ref[h, outer]
        units.append((q0[outer, kl], r1[:128, kl], r1[:128, vl], e0[h], grad, drift))
        grad, drift = coarse_grad(m1[h], best[h], inv_ref[h], g_ref[:, kl], delta_ref[h])
        units.append((q1[:, kl], l1[:, kl], l1[:, vl], e1[h], grad, drift))
    results = backward(units)
    for h in range(HEADS):
        kl, vl = head(h), head(HEADS + h)
        dq0[h], d0[:, kl], d0[:, vl] = results[2 * h]
        dq1[h], d1[:, kl], d1[:, vl] = results[2 * h + 1]


def join_kernel(own2, own3, cross3, d0, d1, got, msg1, msg2, msg3):
    core, _ = place()
    is0 = core == 0
    for j in range(2 * HEADS):
        lanes = head(j)
        msg1[192:, lanes] = (own2[:, lanes] + got[64:128, lanes].astype(F32)).astype(BF)
        first = d1[:, lanes] + expand(0.5 * got[:64, lanes].astype(F32))
        low, high = first[:64], first[64:]
        msg1[128:192, lanes] = jnp.where(is0, low, high).astype(BF)
        msg1[:128, lanes] = (d0[:, lanes] + expand(0.5 * jnp.where(is0, high, low))).astype(BF)
        msg2[:, lanes] = (own3[:, lanes] + got[128:192, lanes].astype(F32)).astype(BF)
        msg3[:, lanes] = (cross3[:, lanes] + got[192:, lanes].astype(F32)).astype(BF)


def rest_kernel(
    q0, q1, g_ref, win, s1, e0, e1, m0, m1, best, inv_ref, delta_ref, dqo0, dqo1, dq2, dq3, att_ref, after,
    att, dq_out, acc, send,
    t0,
):
    core, _ = place()
    is0 = core == 0
    matrix = order_matrix(back=True)
    att[...] = reorder(matrix, att_ref[...])
    for h in range(HEADS):
        kl, vl = head(h), head(HEADS + h)
        grad, drift = coarse_grad(m1[h], best[h], inv_ref[h], g_ref[:, kl], delta_ref[h])
        units = [(q1[:, kl], s1[:, kl], s1[:, vl], e1[h], grad, drift)]
        for i, (number, keys) in enumerate(((1 - core, 384), (core, 256))):
            rows, kept = part(number, 128), slice(i * 128, (i + 1) * 128)
            share = jnp.exp2(m0[h, kept] - best[h, rows]) * inv_ref[h, rows]
            grad = (share * g_ref[rows, kl].astype(F32)).astype(BF)
            drift = share * delta_ref[h, rows]
            units.append((q0[rows, kl], win[:keys, kl], win[:keys, vl], e0[h, kept, :keys], grad, drift))
        (dq, dk, dv), (dq_in, dk_in, dv_in), (dq_out0, dk_out, dv_out) = backward(units)
        t0[h, part(1 - core, 128)] = dq_in
        t0[h, part(core, 128)] = dq_out0 + dqo0[h]
        acc[:, kl] = dk_in[:256] + dk_out
        acc[:, vl] = dv_in[:256] + dv_out
        dq = dq + dqo1[h] + expand(0.5 * (dq2[h] + expand(0.5 * dq3[h])))
        dq_out[:, kl] = reorder(matrix, (t0[h] + expand(0.5 * dq)).astype(BF))
        for lanes, value, fine in ((kl, dk, dk_in), (vl, dv, dv_in)):
            low, high = value[:64], value[64:]
            send[:128, lanes] = (fine[256:] + expand(0.5 * jnp.where(is0, low, high))).astype(BF)
            send[128:, lanes] = jnp.where(is0, high, low).astype(BF)


def add_kernel(own, r1, r2, r3, acc, send):
    core, _ = place()
    is0 = core == 0
    for j in range(2 * HEADS):
        lanes = head(j)
        sib3 = r2[32:, lanes].astype(F32)
        send[:, lanes] = (r1[192:, lanes].astype(F32) + expand(0.5 * sib3)).astype(BF)
        own3 = r2[:32, lanes].astype(F32) + r3[:, lanes].astype(F32)
        first = expand(0.25 * own3, 2) + placed(r1[128:192, lanes].astype(F32), ~is0, 64)
        acc[:, lanes] = own[:, lanes] + expand(0.5 * first) + placed(r1[:128, lanes].astype(F32), is0, 128)


def final_kernel(acc, near, got, dk, dv):
    core, _ = place()
    is0 = core == 0
    matrix = order_matrix(back=True)
    for j in range(2 * HEADS):
        lanes = head(j)
        first = expand(0.5 * got[:, lanes].astype(F32)) + placed(near[128:, lanes].astype(F32), is0, 64)
        total = acc[:, lanes] + expand(0.5 * first) + placed(near[:128, lanes].astype(F32), ~is0, 128)
        (dk if j < HEADS else dv)[:, head(j % HEADS)] = reorder(matrix, total.astype(BF))


SPACES = {"v": pltpu.VMEM, "a": pl.ANY}


def call(kernel, outs, scratch=(), flops=0, specs=None):
    extra = {"in_specs": [pl.BlockSpec(memory_space=SPACES[s]) for s in specs]} if specs else {}
    if flops:
        extra["cost_estimate"] = pl.CostEstimate(flops=flops, bytes_accessed=1 << 20, transcendentals=0)
    return pl.pallas_call(
        kernel,
        out_shape=[jax.ShapeDtypeStruct(shape, dtype) for shape, dtype in outs],
        out_specs=[pl.BlockSpec(memory_space=pltpu.VMEM)] * len(outs),
        scratch_shapes=[s if not isinstance(s, tuple) else pltpu.VMEM(*s) for s in scratch],
        compiler_params=pltpu.CompilerParams(vmem_limit_bytes=VMEM_LIMIT),
        **extra,
    )


def per_device(query, key_rows, value_rows, out_grad):
    count = lax.axis_size("seq")
    sibling = [(i, i + 1) for i in range(0, count, 2)]
    next1 = [(i, i + 1) for i in range(1, count - 1, 2)]
    next2 = [(i, i + 3) for i in range(1, count - 3, 2)]
    next3 = [(i, i + 6) for i in range(count - 6) if (i // 2) % 2 == 0]

    def swap(value, pairs):
        return lax.ppermute(value, "seq", pairs + [(b, a) for a, b in pairs])

    def rows(n, dtype=BF):
        return ((n, FULL), dtype)

    def heads(n, dtype=F32, lanes=HEAD):
        return ((HEADS, n, lanes), dtype)

    stat = heads(256)
    out = ((ROWS, D), BF)
    kv, l1, l2, l3, near = call(
        pre_kernel,
        [rows(256), rows(128), rows(64), rows(32), rows(192)],
    )(jnp.concatenate([key_rows, value_rows], axis=1))
    s2 = swap(l2, sibling)
    r3 = swap(l3, next3)
    msg1, msg2 = call(pack_kernel, [rows(256), rows(64)])(kv, l1, l3, s2)
    r1 = swap(msg1, next1)
    r2 = swap(msg2, next2)
    near = swap(near, sibling)
    q0, g0, q1, q2, q3, win, s1, e0, e1, m0, m1, top, zsum, ysum = call(
        local_kernel,
        [out, out, ((128, D), BF), ((64, D), BF), ((32, D), BF), rows(384), rows(128)]
        + [heads(256, BF, 384), heads(128, BF), stat, heads(128), stat, stat, stat],
        [heads(128), heads(128)],
        flops=1 << 31,
    )(query, out_grad, kv, near)
    outer1, send = call(second_split_kernel, [rows(128), rows(128)], specs="va")(r1, top)
    got2 = swap(send, sibling)
    top, zsum, ysum, eo0, eo1, mo0, mo1 = call(
        outer_kernel,
        [stat] * 3 + [heads(128, BF), heads(128, BF), heads(128), heads(128)],
        [heads(128), heads(128)],
        flops=1 << 30,
    )(q0, q1, r1, outer1, top, zsum, ysum)
    (send,) = call(third_split_kernel, [rows(96)], specs="vva")(r2, r3, top)
    got3 = swap(send, sibling)
    w2, e2, m2, top, zsum, ysum = call(
        second_kernel,
        [rows(256), heads(64, BF, 256), heads(64), stat, stat, stat],
        flops=1 << 28,
        specs="v" * 6 + "a",
    )(q2, r1, got2, top, zsum, ysum, send)
    att, best, inv, delta, dq2, dq3, own2, own3, cross3, send = call(
        far_kernel,
        [out, stat, stat, stat, heads(64), heads(32), rows(64, F32), rows(64, F32), rows(32, F32), rows(224)],
        [rows(256)],
    )(q2, q3, g0, top, zsum, ysum, w2, e2, m2, r2, r3, got3)
    got = swap(send, sibling)
    dqo0, dqo1, d0, d1 = call(
        outer_back_kernel, [heads(128), heads(128), rows(128, F32), rows(128, F32)], flops=1 << 30
    )(q0, q1, g0, r1, outer1, eo0, eo1, mo0, mo1, best, inv, delta)
    msg1, msg2, msg3 = call(join_kernel, [rows(256), rows(64), rows(32)])(own2, own3, cross3, d0, d1, got)
    r1 = swap(msg1, next1)
    r2 = swap(msg2, next2)
    r3 = swap(msg3, next3)
    attended, query_grad, acc, send = call(
        rest_kernel,
        [out, out, rows(256, F32), rows(192)],
        [stat],
        flops=1 << 31,
        specs="v" * 17 + "a",
    )(q0, q1, g0, win, s1, e0, e1, m0, m1, best, inv, delta, dqo0, dqo1, dq2, dq3, att, msg1)
    near = swap(send, sibling)
    acc, send = call(add_kernel, [rows(256, F32), rows(64)], flops=1 << 34)(acc, r1, r2, r3)
    got = swap(send, sibling)
    key_grad, value_grad = call(final_kernel, [out, out])(acc, near, got)
    return attended, query_grad, key_grad, value_grad


def solution(mesh):
    spec = P(("batch", "seq"), None)
    return jax.shard_map(
        per_device, mesh=mesh, in_specs=(spec,) * 4, out_specs=(spec,) * 4, check_vma=False
    )
```

profile of v0, /device:TPU:11, one launch (start us, length us, event | category | flops | bytes accessed | tf_op | source)
XLA Modules:
  0.0 50.3 jit_solution(1800994871427297278)
XLA Ops:
  0.6 1.1 %pad_maximum_fusion.raw = bf16[256,1024]{1,0:T(8,128)(2,1)S(1)} fusion(bf16[256,512]{1,0:T(8,128)(2,1)} %param.6, bf16[256,512]{1,0:T(8,128)(2,1)} %param.5), kind=kLoop, calls=%fused_computation | loop fusion | flops 1048576 | bytes 1048576 | tf_op jit(solution)/shard_map/concatenate | solution.py:474
  1.7 0.4 shard_map.75
  2.1 0.8 %collective-permute-start.1 = (bf16[64,1024]{1,0:T(8,128)(2,1)S(1)}, bf16[64,1024]{1,0:T(8,128)(2,1)S(1)}, u32[]{:S(2)}, u32[]{:S(2)}) collective-permute-start(bf16[64,1024]{1,0:T(8,128)(2,1)S(1)} %get-tuple-element.80), channel_id=1, source_target_pairs={{0,4},{8,12},{16,20},{24,28},{32,36},{40,44},{48,52},{56,60},{64,6... | collective-permute-start | bytes 393224 | tf_op jit(solution)/shard_map/ppermute | solution.py:461
  2.9 0.1 collective-permute-start
  3.0 0.9 %collective-permute-done.1.s2 = bf16[64,1024]{1,0:T(8,128)(2,1)S(1)} collective-permute-done((bf16[64,1024]{1,0:T(8,128)(2,1)S(1)}, bf16[64,1024]{1,0:T(8,128)(2,1)S(1)}, u32[]{:S(2)}, u32[]{:S(2)}) %collective-permute-start.1) | collective-permute-done | bytes 131104 | tf_op jit(solution)/shard_map/ppermute | solution.py:461
  3.9 3.9 %collective-permute-start.2 = (bf16[256,1024]{1,0:T(8,128)(2,1)S(1)}, bf16[256,1024]{1,0:T(8,128)(2,1)S(1)}, u32[]{:S(2)}, u32[]{:S(2)}) collective-permute-start(bf16[256,1024]{1,0:T(8,128)(2,1)S(1)} %get-tuple-element.81), channel_id=1, source_target_pairs={{4,8},{12,16},{20,24},{28,32},{36,40},{44,48},{52,56},{60,64},{68,... | collective-permute-start | bytes 1572872 | tf_op jit(solution)/shard_map/ppermute | solution.py:461
  7.8 7.5 %collective-permute-start.5 = (bf16[32,1024]{1,0:T(8,128)(2,1)S(1)}, bf16[32,1024]{1,0:T(8,128)(2,1)S(1)}, u32[]{:S(2)}, u32[]{:S(2)}) collective-permute-start(bf16[32,1024]{1,0:T(8,128)(2,1)S(1)} %get-tuple-element.79.l3), channel_id=1, source_target_pairs={{0,24},{4,28},{16,40},{20,44},{32,56},{36,60},{48,72},{52,76},{64,... | collective-permute-start | bytes 196616 | tf_op jit(solution)/shard_map/ppermute | solution.py:461
  15.3 3.4 %collective-permute-start.4 = (bf16[64,1024]{1,0:T(8,128)(2,1)S(1)}, bf16[64,1024]{1,0:T(8,128)(2,1)S(1)}, u32[]{:S(2)}, u32[]{:S(2)}) collective-permute-start(bf16[64,1024]{1,0:T(8,128)(2,1)S(1)} %get-tuple-element.90), channel_id=1, source_target_pairs={{4,16},{12,24},{20,32},{28,40},{36,48},{44,56},{52,64},{60,72},{68... | collective-permute-start | bytes 393224 | tf_op jit(solution)/shard_map/ppermute | solution.py:461
  18.8 1.6 %shard_map.76 = (bf16[256,512]{1,0:T(8,128)(2,1)S(1)}, bf16[256,512]{1,0:T(8,128)(2,1)S(1)}, bf16[128,512]{1,0:T(8,128)(2,1)S(1)}, bf16[64,512]{1,0:T(8,128)(2,1...) custom-call(bf16[256,512]{1,0:T(8,128)(2,1)S(1)} %copy-done, ...), custom_call_target="tpu_custom_call" | custom-call | flops 2147483648 | bytes 1048576 | tf_op jit(solution)/shard_map/pallas_call | solution.py:481
  20.4 0.1 shard_map.78
  20.5 0.1 collective-permute-start.3
  20.6 0.8 %shard_map.79 = (f32[4,256,128]{2,1,0:T(8,128)S(1)}, f32[4,256,128]{2,1,0:T(8,128)S(1)}, f32[4,256,128]{2,1,0:T(8,128)S(1)}, bf16[4,128,128]{2,1,0:T(8,128)(2,1)...) custom-call(bf16[256,512]{1,0:T(8,128)(2,1)S(1)} %get-tuple-element.67.q0, ...), custom_call_target="tpu_custom_call" | custom-call | flops 1073741824 | bytes 1048576 | tf_op jit(solution)/shard_map/pallas_call | solution.py:490
  21.4 0.0 collective-permute-done.5.r3
  21.4 2.8 %collective-permute-done.4.r2 = bf16[64,1024]{1,0:T(8,128)(2,1)S(1)} collective-permute-done((bf16[64,1024]{1,0:T(8,128)(2,1)S(1)}, bf16[64,1024]{1,0:T(8,128)(2,1)S(1)}, u32[]{:S(2)}, u32[]{:S(2)}) %collective-permute-start.4) | collective-permute-done | bytes 131104 | tf_op jit(solution)/shard_map/ppermute | solution.py:461
  24.2 1.7 %collective-permute-start.6 = (bf16[96,1024]{1,0:T(8,128)(2,1)S(1)}, bf16[96,1024]{1,0:T(8,128)(2,1)S(1)}, u32[]{:S(2)}, u32[]{:S(2)}) collective-permute-start(bf16[96,1024]{1,0:T(8,128)(2,1)S(1)} %shard_map.80.after), channel_id=1, source_target_pairs={{0,4},{8,12},{16,20},{24,28},{32,36},{40,44},{48,52},{56,60},{64,6... | collective-permute-start | bytes 589832 | tf_op jit(solution)/shard_map/ppermute | solution.py:461
  25.9 0.6 %shard_map.81 = (bf16[256,1024]{1,0:T(8,128)(2,1)S(1)}, bf16[4,64,256]{2,1,0:T(8,128)(2,1)S(1)}, f32[4,64,128]{2,1,0:T(8,128)S(1)}, f32[4,256,128]{2,1,0:T(8,128...) custom-call(bf16[64,512]{1,0:T(8,128)(2,1)S(1)} %get-tuple-element.76.q2, ...), custom_call_target="tpu_custom_call" | custom-call | flops 268435456 | bytes 1048576 | tf_op jit(solution)/shard_map/pallas_call | solution.py:498
  26.5 0.5 collective-permute-done.6.got
  27.0 1.4 %shard_map.82 = (bf16[256,512]{1,0:T(8,128)(2,1)S(1)}, f32[4,256,128]{2,1,0:T(8,128)S(1)}, f32[4,256,128]{2,1,0:T(8,128)S(1)}, f32[4,256,128]{2,1,0:T(8,128)S(1)...) custom-call(bf16[64,512]{1,0:T(8,128)(2,1)S(1)} %get-tuple-element.7, ...), custom_call_target="tpu_custom_call" | custom-call | tf_op jit(solution)/shard_map/pallas_call | solution.py:504
  28.4 0.5 collective-permute-start.7
  28.9 0.6 %shard_map.83 = (f32[4,128,128]{2,1,0:T(8,128)S(1)}, f32[4,128,128]{2,1,0:T(8,128)S(1)}, f32[128,1024]{1,0:T(8,128)S(1)}, f32[128,1024]{1,0:T(8,128)S(1)}) custom-call(bf16[256,512]{1,0:T(8,128)(2,1)S(1)} %get-tuple-element.67.q0, bf16[128,512]{1,0:T(8,128)(2,1)S(1)} %get-tuple-element.68.q1, bf16[256,512]{1,0:T(8,128)(2,1)S(1)} %get-tuple-element.69.g_ref, ...), custom_call_target="tpu_custom_call" | custom-call | flops 1073741824 | bytes 1048576 | tf_op jit(solution)/shard_map/pallas_call | solution.py:510
  29.4 0.9 %collective-permute-done.7.got = bf16[224,1024]{1,0:T(8,128)(2,1)S(1)} collective-permute-done((bf16[224,1024]{1,0:T(8,128)(2,1)S(1)}, bf16[224,1024]{1,0:T(8,128)(2,1)S(1)}, u32[]{:S(2)}, u32[]{:S(2)}) %collective-permute-start.7) | collective-permute-done | bytes 458784 | tf_op jit(solution)/shard_map/ppermute | solution.py:461
  30.3 0.2 shard_map.84
  30.6 4.0 %collective-permute-start.8 = (bf16[256,1024]{1,0:T(8,128)(2,1)S(1)}, bf16[256,1024]{1,0:T(8,128)(2,1)S(1)}, u32[]{:S(2)}, u32[]{:S(2)}) collective-permute-start(bf16[256,1024]{1,0:T(8,128)(2,1)S(1)} %get-tuple-element.115.after), channel_id=1, source_target_pairs={{4,8},{12,16},{20,24},{28,32},{36,40},{44,48},{52,56},{60,64},{68,... | collective-permute-start | bytes 1572872 | tf_op jit(solution)/shard_map/ppermute | solution.py:461
  34.6 1.9 %collective-permute-start.10 = (bf16[32,1024]{1,0:T(8,128)(2,1)S(1)}, bf16[32,1024]{1,0:T(8,128)(2,1)S(1)}, u32[]{:S(2)}, u32[]{:S(2)}) collective-permute-start(bf16[32,1024]{1,0:T(8,128)(2,1)S(1)} %get-tuple-element.120), channel_id=1, source_target_pairs={{0,24},{4,28},{16,40},{20,44},{32,56},{36,60},{48,72},{52,76},{64,... | collective-permute-start | bytes 196616 | tf_op jit(solution)/shard_map/ppermute | solution.py:461
  36.5 3.1 %collective-permute-start.9 = (bf16[64,1024]{1,0:T(8,128)(2,1)S(1)}, bf16[64,1024]{1,0:T(8,128)(2,1)S(1)}, u32[]{:S(2)}, u32[]{:S(2)}) collective-permute-start(bf16[64,1024]{1,0:T(8,128)(2,1)S(1)} %get-tuple-element.119), channel_id=1, source_target_pairs={{4,16},{12,24},{20,32},{28,40},{36,48},{44,56},{52,64},{60,72},{68... | collective-permute-start | bytes 393224 | tf_op jit(solution)/shard_map/ppermute | solution.py:461
  39.6 2.7 %shard_map.85 = (bf16[256,512]{1,0:T(8,128)(2,1)}, bf16[256,512]{1,0:T(8,128)(2,1)}, f32[256,1024]{1,0:T(8,128)S(1)}, bf16[192,1024]{1,0:T(8,128)(2,1)S(1)}) custom-call(bf16[256,512]{1,0:T(8,128)(2,1)S(1)} %get-tuple-element.67.q0, bf16[128,512]{1,0:T(8,128)(2,1)S(1)} %get-tuple-element.68.q1, bf16[256,512]{1,0:T(8,128)(2,1)S(1)} %get-tuple-element.69.g_ref, ...), custom_call_target="tpu_custom_call" | custom-call | flops 2147483648 | bytes 1048576 | tf_op jit(solution)/shard_map/pallas_call | solution.py:517
  42.3 3.1 %collective-permute-start.11 = (bf16[192,1024]{1,0:T(8,128)(2,1)S(1)}, bf16[192,1024]{1,0:T(8,128)(2,1)S(1)}, u32[]{:S(2)}, u32[]{:S(2)}) collective-permute-start(bf16[192,1024]{1,0:T(8,128)(2,1)S(1)} %get-tuple-element.122), channel_id=1, source_target_pairs={{0,4},{8,12},{16,20},{24,28},{32,36},{40,44},{48,52},{56,60},{64,6... | collective-permute-start | bytes 1179656 | tf_op jit(solution)/shard_map/ppermute | solution.py:461
  45.4 1.7 %collective-permute-done.9.r2 = bf16[64,1024]{1,0:T(8,128)(2,1)S(1)} collective-permute-done((bf16[64,1024]{1,0:T(8,128)(2,1)S(1)}, bf16[64,1024]{1,0:T(8,128)(2,1)S(1)}, u32[]{:S(2)}, u32[]{:S(2)}) %collective-permute-start.9) | collective-permute-done | bytes 131104 | tf_op jit(solution)/shard_map/ppermute | solution.py:461
  47.1 0.3 shard_map.86
  47.4 0.7 %collective-permute-start.12 = (bf16[64,1024]{1,0:T(8,128)(2,1)S(1)}, bf16[64,1024]{1,0:T(8,128)(2,1)S(1)}, u32[]{:S(2)}, u32[]{:S(2)}) collective-permute-start(bf16[64,1024]{1,0:T(8,128)(2,1)S(1)} %get-tuple-element.123), channel_id=1, source_target_pairs={{0,4},{8,12},{16,20},{24,28},{32,36},{40,44},{48,52},{56,60},{64,6... | collective-permute-start | bytes 393224 | tf_op jit(solution)/shard_map/ppermute | solution.py:461
  48.1 1.0 %collective-permute-done.12.got = bf16[64,1024]{1,0:T(8,128)(2,1)S(1)} collective-permute-done((bf16[64,1024]{1,0:T(8,128)(2,1)S(1)}, bf16[64,1024]{1,0:T(8,128)(2,1)S(1)}, u32[]{:S(2)}, u32[]{:S(2)}) %collective-permute-start.12) | collective-permute-done | bytes 131104 | tf_op jit(solution)/shard_map/ppermute | solution.py:461
  49.1 1.1 %shard_map.87 = (bf16[256,512]{1,0:T(8,128)(2,1)}, bf16[256,512]{1,0:T(8,128)(2,1)}) custom-call(f32[256,1024]{1,0:T(8,128)S(1)} %get-tuple-element.121.acc, bf16[192,1024]{1,0:T(8,128)(2,1)S(1)} %collective-permute-done.11.near, bf16[64,1024]{1,0:T(8,128)(2,1)S(1)} %collective-permute-done.12.got), custom_call_target="tpu_custom_call" | custom-call | tf_op jit(solution)/shard_map/pallas_call | solution.py:527
  (12 shorter events, 0.1 us)
Async XLA Ops:
  2.1 1.8 %collective-permute-start.1 = (bf16[64,1024]{1,0:T(8,128)(2,1)S(1)}, bf16[64,1024]{1,0:T(8,128)(2,1)S(1)}, u32[]{:S(2)}, u32[]{:S(2)}) collective-permute-start(bf16[64,1024]{1,0:T(8,128)(2,1)S(1)} %get-tuple-element.80), channel_id=1, source_target_pairs={{0,4},{8,12},{16,20},{24,28},{32,36},{40,44},{48,52},{56,60},{64,6... | collective-permute-start | bytes 393224 | tf_op jit(solution)/shard_map/ppermute | solution.py:461
  2.9 15.9 %collective-permute-start = (bf16[192,1024]{1,0:T(8,128)(2,1)S(1)}, bf16[192,1024]{1,0:T(8,128)(2,1)S(1)}, u32[]{:S(2)}, u32[]{:S(2)}) collective-permute-start(bf16[192,1024]{1,0:T(8,128)(2,1)S(1)} %get-tuple-element.66), channel_id=1, source_target_pairs={{0,4},{8,12},{16,20},{24,28},{32,36},{40,44},{48,52},{56,60},{64,6... | collective-permute-start | bytes 1179656 | tf_op jit(solution)/shard_map/ppermute | solution.py:461
  3.8 14.9 %copy-start = (bf16[256,512]{1,0:T(8,128)(2,1)S(1)}, bf16[256,512]{1,0:T(8,128)(2,1)}, u32[]{:S(2)}) copy-start(bf16[256,512]{1,0:T(8,128)(2,1)} %q_ref.1) | copy-start | bytes 786436
  3.9 14.9 %copy-start.1 = (bf16[256,512]{1,0:T(8,128)(2,1)S(1)}, bf16[256,512]{1,0:T(8,128)(2,1)}, u32[]{:S(2)}) copy-start(bf16[256,512]{1,0:T(8,128)(2,1)} %g_ref.1) | copy-start | bytes 786436
  3.9 16.5 %collective-permute-start.2 = (bf16[256,1024]{1,0:T(8,128)(2,1)S(1)}, bf16[256,1024]{1,0:T(8,128)(2,1)S(1)}, u32[]{:S(2)}, u32[]{:S(2)}) collective-permute-start(bf16[256,1024]{1,0:T(8,128)(2,1)S(1)} %get-tuple-element.81), channel_id=1, source_target_pairs={{4,8},{12,16},{20,24},{28,32},{36,40},{44,48},{52,56},{60,64},{68,... | collective-permute-start | bytes 1572872 | tf_op jit(solution)/shard_map/ppermute | solution.py:461
  7.8 13.6 %collective-permute-start.5 = (bf16[32,1024]{1,0:T(8,128)(2,1)S(1)}, bf16[32,1024]{1,0:T(8,128)(2,1)S(1)}, u32[]{:S(2)}, u32[]{:S(2)}) collective-permute-start(bf16[32,1024]{1,0:T(8,128)(2,1)S(1)} %get-tuple-element.79.l3), channel_id=1, source_target_pairs={{0,24},{4,28},{16,40},{20,44},{32,56},{36,60},{48,72},{52,76},{64,... | collective-permute-start | bytes 196616 | tf_op jit(solution)/shard_map/ppermute | solution.py:461
  15.3 8.9 %collective-permute-start.4 = (bf16[64,1024]{1,0:T(8,128)(2,1)S(1)}, bf16[64,1024]{1,0:T(8,128)(2,1)S(1)}, u32[]{:S(2)}, u32[]{:S(2)}) collective-permute-start(bf16[64,1024]{1,0:T(8,128)(2,1)S(1)} %get-tuple-element.90), channel_id=1, source_target_pairs={{4,16},{12,24},{20,32},{28,40},{36,48},{44,56},{52,64},{60,72},{68... | collective-permute-start | bytes 393224 | tf_op jit(solution)/shard_map/ppermute | solution.py:461
  20.5 5.4 %collective-permute-start.3 = (bf16[128,1024]{1,0:T(8,128)(2,1)S(1)}, bf16[128,1024]{1,0:T(8,128)(2,1)S(1)}, u32[]{:S(2)}, u32[]{:S(2)}) collective-permute-start(bf16[128,1024]{1,0:T(8,128)(2,1)S(1)} %get-tuple-element.83), channel_id=1, source_target_pairs={{0,4},{8,12},{16,20},{24,28},{32,36},{40,44},{48,52},{56,60},{64,6... | collective-permute-start | bytes 786440 | tf_op jit(solution)/shard_map/ppermute | solution.py:461
  24.2 2.8 %collective-permute-start.6 = (bf16[96,1024]{1,0:T(8,128)(2,1)S(1)}, bf16[96,1024]{1,0:T(8,128)(2,1)S(1)}, u32[]{:S(2)}, u32[]{:S(2)}) collective-permute-start(bf16[96,1024]{1,0:T(8,128)(2,1)S(1)} %shard_map.80.after), channel_id=1, source_target_pairs={{0,4},{8,12},{16,20},{24,28},{32,36},{40,44},{48,52},{56,60},{64,6... | collective-permute-start | bytes 589832 | tf_op jit(solution)/shard_map/ppermute | solution.py:461
  28.4 1.9 %collective-permute-start.7 = (bf16[224,1024]{1,0:T(8,128)(2,1)S(1)}, bf16[224,1024]{1,0:T(8,128)(2,1)S(1)}, u32[]{:S(2)}, u32[]{:S(2)}) collective-permute-start(bf16[224,1024]{1,0:T(8,128)(2,1)S(1)} %get-tuple-element.114), channel_id=1, source_target_pairs={{0,4},{8,12},{16,20},{24,28},{32,36},{40,44},{48,52},{56,60},{64,6... | collective-permute-start | bytes 1376264 | tf_op jit(solution)/shard_map/ppermute | solution.py:461
  30.6 16.6 %collective-permute-start.8 = (bf16[256,1024]{1,0:T(8,128)(2,1)S(1)}, bf16[256,1024]{1,0:T(8,128)(2,1)S(1)}, u32[]{:S(2)}, u32[]{:S(2)}) collective-permute-start(bf16[256,1024]{1,0:T(8,128)(2,1)S(1)} %get-tuple-element.115.after), channel_id=1, source_target_pairs={{4,8},{12,16},{20,24},{28,32},{36,40},{44,48},{52,56},{60,64},{68,... | collective-permute-start | bytes 1572872 | tf_op jit(solution)/shard_map/ppermute | solution.py:461
  34.6 10.9 %collective-permute-start.10 = (bf16[32,1024]{1,0:T(8,128)(2,1)S(1)}, bf16[32,1024]{1,0:T(8,128)(2,1)S(1)}, u32[]{:S(2)}, u32[]{:S(2)}) collective-permute-start(bf16[32,1024]{1,0:T(8,128)(2,1)S(1)} %get-tuple-element.120), channel_id=1, source_target_pairs={{0,24},{4,28},{16,40},{20,44},{32,56},{36,60},{48,72},{52,76},{64,... | collective-permute-start | bytes 196616 | tf_op jit(solution)/shard_map/ppermute | solution.py:461
  36.5 10.6 %collective-permute-start.9 = (bf16[64,1024]{1,0:T(8,128)(2,1)S(1)}, bf16[64,1024]{1,0:T(8,128)(2,1)S(1)}, u32[]{:S(2)}, u32[]{:S(2)}) collective-permute-start(bf16[64,1024]{1,0:T(8,128)(2,1)S(1)} %get-tuple-element.119), channel_id=1, source_target_pairs={{4,16},{12,24},{20,32},{28,40},{36,48},{44,56},{52,64},{60,72},{68... | collective-permute-start | bytes 393224 | tf_op jit(solution)/shard_map/ppermute | solution.py:461
  42.3 5.8 %collective-permute-start.11 = (bf16[192,1024]{1,0:T(8,128)(2,1)S(1)}, bf16[192,1024]{1,0:T(8,128)(2,1)S(1)}, u32[]{:S(2)}, u32[]{:S(2)}) collective-permute-start(bf16[192,1024]{1,0:T(8,128)(2,1)S(1)} %get-tuple-element.122), channel_id=1, source_target_pairs={{0,4},{8,12},{16,20},{24,28},{32,36},{40,44},{48,52},{56,60},{64,6... | collective-permute-start | bytes 1179656 | tf_op jit(solution)/shard_map/ppermute | solution.py:461
  47.4 1.7 %collective-permute-start.12 = (bf16[64,1024]{1,0:T(8,128)(2,1)S(1)}, bf16[64,1024]{1,0:T(8,128)(2,1)S(1)}, u32[]{:S(2)}, u32[]{:S(2)}) collective-permute-start(bf16[64,1024]{1,0:T(8,128)(2,1)S(1)} %get-tuple-element.123), channel_id=1, source_target_pairs={{0,4},{8,12},{16,20},{24,28},{32,36},{40,44},{48,52},{56,60},{64,6... | collective-permute-start | bytes 393224 | tf_op jit(solution)/shard_map/ppermute | solution.py:461
where the time goes:
time: 50.9 us; the launch traced here: 50.3 us
  starting transfers between devices  30.8 us (61%)
  Pallas kernels  9.91 us (19%)
  waiting for transfers between devices  7.64 us (15%)
  other arithmetic  1.08 us (2%)
  between operations  0.82 us (2%)
    ppermute x13, starting transfers between devices, swap(): return lax.ppermute(value, 'seq', pairs + [(b, a) for a, b in pairs])  30.8 us
    ppermute x13, waiting for transfers between devices, swap(): return lax.ppermute(value, 'seq', pairs + [(b, a) for a, b in pairs])  7.64 us
    pallas_call x1, Pallas kernels, per_device(): call(rest_kernel, [out, out, rows(256, F32), rows(192)], [stat], flops=1...  2.68 us
    pallas_call x1, Pallas kernels, per_device(): call(local_kernel, [out, out, ((128, D), BF), ((64, D), BF), ((32, D), BF...  1.58 us
    pallas_call x1, Pallas kernels, per_device(): call(far_kernel, [out, stat, stat, stat, heads(64), heads(32), rows(64, F...  1.42 us
    pallas_call x1, Pallas kernels, per_device(): key_grad, value_grad = call(final_kernel, [out, out])(acc, near, got)  1.15 us
    concatenate x1, other arithmetic, per_device(): jnp.concatenate([key_rows, value_rows], axis=1)  1.08 us
  transfers between devices with their start and end apart: 13, of which 6 were waited for; matrix products, arithmetic and copies ran while one was open for 0% of the time, Pallas kernels for 13%

commit v1 on v0

--- a/solution.py
+++ b/solution.py
@@ -151,8 +151,7 @@
     return jnp.concatenate([jnp.where(first, value, zeros), jnp.where(first, zeros, value)], axis=0)
 
 
-def pre_kernel(raw, kv, l1, l2, l3, sib):
-    core, _ = place()
+def pre_kernel(raw, kv, l1, l3):
     matrix = order_matrix()
     for i in range(2):
         lanes = slice(i * D, (i + 1) * D)
@@ -160,23 +159,27 @@
         kv[:, lanes] = fine
         fine = coarse(fine)
         l1[:, lanes] = fine
-        fine = coarse(fine)
-        l2[:, lanes] = fine
-        l3[:, lanes] = coarse(fine)
-    sib[:128] = kv[part(1 - core, 128), :]
-    sib[128:] = l1[part(core, 64), :]
-
-
-def pack_kernel(kv, l1, l3, s2, msg1, msg2):
-    core, _ = place()
+        l3[:, lanes] = coarse(coarse(fine))
+
+
+def pack_kernel(kv, l1, l3, ks, vs, near, s1, msg1, msg2):
+    core, _ = place()
+    matrix = order_matrix()
+    for i, raw in enumerate((ks, vs)):
+        lanes = slice(i * D, (i + 1) * D)
+        fine = reorder(matrix, raw[...])
+        near[:, lanes] = jnp.where(core == 0, fine[:128], fine[128:])
+        first = coarse(fine)
+        s1[:, lanes] = first
+        second = coarse(first)
+        msg1[192:, lanes] = second
+        msg2[32:, lanes] = coarse(second)
     msg1[:128] = kv[part(core, 128), :]
     msg1[128:192] = l1[part(1 - core, 64), :]
-    msg1[192:] = s2[...]
     msg2[:32] = l3[...]
-    msg2[32:] = coarse(s2[...])
-
-
-def local_kernel(q_ref, g_ref, kv, sib, q0, g0, q1, q2, q3, win, s1, e0, e1, m0, m1, top, zsum, ysum, d1, n1):
+
+
+def local_kernel(q_ref, g_ref, kv, near, s1, q0, g0, q1, q2, q3, win, e0, e1, m0, m1, top, zsum, ysum, d1, n1):
     core, _ = place()
     matrix = order_matrix()
     q0[...] = reorder(matrix, q_ref[...])
@@ -185,9 +188,7 @@
     q2[...] = coarse(q1[...])
     q3[...] = coarse(q2[...])
     win[:256] = kv[...]
-    win[256:] = sib[:128]
-    s1[part(core, 64), :] = coarse(sib[:128])
-    s1[part(1 - core, 64), :] = sib[128:]
+    win[256:] = near[...]
     left, right = half_masks()
     bias = jnp.where(core == 0, right, left)
     for h in range(HEADS):
@@ -247,7 +248,7 @@
             )
 
 
-def second_kernel(q2, r1, got, top, zsum, ysum, after, win, e2, m2, top_out, z_out, y_out):
+def second_kernel(q2, r1, got, top, zsum, ysum, win, e2, m2, top_out, z_out, y_out):
     core, chip = place()
     is0 = core == 0
     win[:64] = r1[192:]
@@ -277,15 +278,15 @@
     is0 = core == 0
     w3[:64] = r2[...]
     w3[64:128] = got[:64]
-    w3[128:160] = r3[...]
-    w3[160:192] = got[64:]
+    w3[128:192] = jnp.where(lax.rem(core + chip, 2) == 1, r3[...], got[64:])
     w3[192:] = jnp.zeros((64, FULL), BF)
+    holder = lax.rem(core + chip, 2) == 1
     low2, high2 = chip >= 2, chip <= 29
     even = lax.rem(chip, 2) == 0
     cross_bad = penalty(jnp.where(even, chip <= 28, chip >= 3))
     lane = lax.broadcasted_iota(jnp.int32, (1, 256), 1)
-    own_bad = penalty(jnp.where(is0, low2, high2))
-    sib_bad = penalty(jnp.where(is0, high2, low2))
+    own_bad = penalty(jnp.where(is0, high2, low2))
+    sib_bad = penalty(jnp.where(is0, low2, high2))
     bias3 = jnp.where(
         lane < 64, own_bad, jnp.where(lane < 128, sib_bad, jnp.where(lane < 192, cross_bad, NEG))
     )
@@ -328,8 +329,8 @@
                 else:
                     own3[:, lanes] = value[:64]
                     send[128:192, lanes] = value[64:128].astype(BF)
-                    cross3[:, lanes] = value[128:160]
-                    send[192:, lanes] = value[160:192].astype(BF)
+                    cross3[:, lanes] = jnp.where(holder, value[128:160], value[160:192])
+                    send[192:, lanes] = jnp.where(holder, value[160:192], value[128:160]).astype(BF)
 
 
 def coarse_grad(m, best, inv, g, delta):
@@ -454,7 +455,8 @@
     count = lax.axis_size("seq")
     sibling = [(i, i + 1) for i in range(0, count, 2)]
     next1 = [(i, i + 1) for i in range(1, count - 1, 2)]
-    next2 = [(i, i + 3) for i in range(1, count - 3, 2)]
+    next2 = [(i, i + 5) for i in range(0, count - 5, 2)]
+    forward = [(i, i + 1) for i in range(1, count, 4)]
     next3 = [(i, i + 6) for i in range(count - 6) if (i // 2) % 2 == 0]
 
     def swap(value, pairs):
@@ -468,24 +470,27 @@
 
     stat = heads(256)
     out = ((ROWS, D), BF)
-    kv, l1, l2, l3, near = call(
-        pre_kernel,
-        [rows(256), rows(128), rows(64), rows(32), rows(192)],
-    )(jnp.concatenate([key_rows, value_rows], axis=1))
-    s2 = swap(l2, sibling)
-    r3 = swap(l3, next3)
-    msg1, msg2 = call(pack_kernel, [rows(256), rows(64)])(kv, l1, l3, s2)
+    key_sib = swap(key_rows, sibling)
+    value_sib = swap(value_rows, sibling)
+    kv, l1, l3 = call(pre_kernel, [rows(256), rows(128), rows(32)])(
+        jnp.concatenate([key_rows, value_rows], axis=1)
+    )
+    near, s1, msg1, msg2 = call(pack_kernel, [rows(128), rows(128), rows(256), rows(64)])(
+        kv, l1, l3, key_sib, value_sib
+    )
+    r2 = swap(msg2, next2)
     r1 = swap(msg1, next1)
-    r2 = swap(msg2, next2)
-    near = swap(near, sibling)
-    q0, g0, q1, q2, q3, win, s1, e0, e1, m0, m1, top, zsum, ysum = call(
+    r3 = swap(r2, forward)
+    q0, g0, q1, q2, q3, win, e0, e1, m0, m1, top, zsum, ysum = call(
         local_kernel,
-        [out, out, ((128, D), BF), ((64, D), BF), ((32, D), BF), rows(384), rows(128)]
+        [out, out, ((128, D), BF), ((64, D), BF), ((32, D), BF), rows(384)]
         + [heads(256, BF, 384), heads(128, BF), stat, heads(128), stat, stat, stat],
         [heads(128), heads(128)],
-        flops=1 << 31,
-    )(query, out_grad, kv, near)
-    outer1, send = call(second_split_kernel, [rows(128), rows(128)], specs="va")(r1, top)
+        flops=1 << 33,
+    )(query, out_grad, kv, near, s1)
+    (send,) = call(third_split_kernel, [rows(128)], specs="vva")(r2, r3, top)
+    got3 = swap(send, sibling)
+    outer1, send = call(second_split_kernel, [rows(128), rows(128)], specs="va")(r1, send)
     got2 = swap(send, sibling)
     top, zsum, ysum, eo0, eo1, mo0, mo1 = call(
         outer_kernel,
@@ -493,14 +498,11 @@
         [heads(128), heads(128)],
         flops=1 << 30,
     )(q0, q1, r1, outer1, top, zsum, ysum)
-    (send,) = call(third_split_kernel, [rows(96)], specs="vva")(r2, r3, top)
-    got3 = swap(send, sibling)
     w2, e2, m2, top, zsum, ysum = call(
         second_kernel,
         [rows(256), heads(64, BF, 256), heads(64), stat, stat, stat],
         flops=1 << 28,
-        specs="v" * 6 + "a",
-    )(q2, r1, got2, top, zsum, ysum, send)
+    )(q2, r1, got2, top, zsum, ysum)
     att, best, inv, delta, dq2, dq3, own2, own3, cross3, send = call(
         far_kernel,
         [out, stat, stat, stat, heads(64), heads(32), rows(64, F32), rows(64, F32), rows(32, F32), rows(224)],

time: 50.9 us -> 49.6 us (0.974)
  starting transfers between devices: 30.8 us -> 26 us
  waiting for transfers between devices: 7.64 us -> 11 us
    ppermute x13, starting transfers between devices: 30.8 us -> 26 us  [swap(): return lax.ppermute(value, 'seq', pairs + [(b, a) for a, b in pairs])]
    ppermute x13, waiting for transfers between devices: 7.64 us -> 11 us  [swap(): return lax.ppermute(value, 'seq', pairs + [(b, a) for a, b in pairs])]
  transfers between devices with their start and end apart: 13 -> 13, of which waited for: 6 -> 7; matrix products, arithmetic and copies ran while one was open for 0% -> 2% of each run, Pallas kernels for 13% -> 14%
where the time goes in v1:
time: 49.6 us; the launch traced here: 49.1 us
  starting transfers between devices  26 us (52%)
  waiting for transfers between devices  11 us (22%)
  Pallas kernels  10.2 us (21%)
  other arithmetic  1.08 us (2%)
  between operations  0.83 us (2%)
    ppermute x13, starting transfers between devices, swap(): return lax.ppermute(value, 'seq', pairs + [(b, a) for a, b in pairs])  26 us
    ppermute x13, waiting for transfers between devices, swap(): return lax.ppermute(value, 'seq', pairs + [(b, a) for a, b in pairs])  11 us
    pallas_call x1, Pallas kernels, per_device(): call(rest_kernel, [out, out, rows(256, F32), rows(192)], [stat], flops=1...  2.68 us
    pallas_call x1, Pallas kernels, per_device(): call(local_kernel, [out, out, ((128, D), BF), ((64, D), BF), ((32, D), BF...  1.6 us
    pallas_call x1, Pallas kernels, per_device(): call(far_kernel, [out, stat, stat, stat, heads(64), heads(32), rows(64, F...  1.42 us
    pallas_call x1, Pallas kernels, per_device(): key_grad, value_grad = call(final_kernel, [out, out])(acc, near, got)  1.15 us
    concatenate x1, other arithmetic, per_device(): jnp.concatenate([key_rows, value_rows], axis=1)  1.08 us
  transfers between devices with their start and end apart: 13, of which 7 were waited for; matrix products, arithmetic and copies ran while one was open for 2% of the time, Pallas kernels for 14%

profile of v1, /device:TPU:11, one launch (start us, length us, event | category | flops | bytes accessed | tf_op | source)
XLA Modules:
  0.0 49.1 jit_solution(16770970712540865049)
XLA Ops:
  0.6 0.8 %collective-permute-start = (bf16[256,512]{1,0:T(8,128)(2,1)}, bf16[256,512]{1,0:T(8,128)(2,1)S(1)}, u32[]{:S(2)}, u32[]{:S(2)}) collective-permute-start(bf16[256,512]{1,0:T(8,128)(2,1)} %param.5), channel_id=1, source_target_pairs={{0,4},{8,12},{16,20},{24,28},{32,36},{40,44},{48,52},{56,60},{64,6... | collective-permute-start | bytes 786440 | tf_op jit(solution)/shard_map/ppermute | solution.py:463
  1.4 0.1 collective-permute-start.1
  1.5 1.1 %pad_maximum_fusion.raw = bf16[256,1024]{1,0:T(8,128)(2,1)S(1)} fusion(bf16[256,512]{1,0:T(8,128)(2,1)} %param.6, bf16[256,512]{1,0:T(8,128)(2,1)} %param.5), kind=kLoop, calls=%fused_computation | loop fusion | flops 1048576 | bytes 1048576 | tf_op jit(solution)/shard_map/concatenate | solution.py:476
  2.6 0.3 shard_map.75
  2.9 0.2 collective-permute-done.1.vs
  3.1 0.4 shard_map.76
  3.5 8.1 %collective-permute-start.3 = (bf16[64,1024]{1,0:T(8,128)(2,1)S(1)}, bf16[64,1024]{1,0:T(8,128)(2,1)S(1)}, u32[]{:S(2)}, u32[]{:S(2)}) collective-permute-start(bf16[64,1024]{1,0:T(8,128)(2,1)S(1)} %get-tuple-element.80), channel_id=1, source_target_pairs={{0,20},{8,28},{16,36},{24,44},{32,52},{40,60},{48,68},{56,76},{64,... | collective-permute-start | bytes 393224 | tf_op jit(solution)/shard_map/ppermute | solution.py:463
  11.6 1.9 %collective-permute-start.2 = (bf16[256,1024]{1,0:T(8,128)(2,1)S(1)}, bf16[256,1024]{1,0:T(8,128)(2,1)S(1)}, u32[]{:S(2)}, u32[]{:S(2)}) collective-permute-start(bf16[256,1024]{1,0:T(8,128)(2,1)S(1)} %get-tuple-element.79), channel_id=1, source_target_pairs={{4,8},{12,16},{20,24},{28,32},{36,40},{44,48},{52,56},{60,64},{68,... | collective-permute-start | bytes 1572872 | tf_op jit(solution)/shard_map/ppermute | solution.py:463
  13.5 1.4 %collective-permute-done.3.r2 = bf16[64,1024]{1,0:T(8,128)(2,1)S(1)} collective-permute-done((bf16[64,1024]{1,0:T(8,128)(2,1)S(1)}, bf16[64,1024]{1,0:T(8,128)(2,1)S(1)}, u32[]{:S(2)}, u32[]{:S(2)}) %collective-permute-start.3) | collective-permute-done | bytes 131104 | tf_op jit(solution)/shard_map/ppermute | solution.py:463
  14.9 2.3 %collective-permute-start.4 = (bf16[64,1024]{1,0:T(8,128)(2,1)S(1)}, bf16[64,1024]{1,0:T(8,128)(2,1)S(1)}, u32[]{:S(2)}, u32[]{:S(2)}) collective-permute-start(bf16[64,1024]{1,0:T(8,128)(2,1)S(1)} %collective-permute-done.3.r2), channel_id=1, source_target_pairs={{4,8},{20,24},{36,40},{52,56},{68,72},{84,88},{100,104},{116,120},... | collective-permute-start | bytes 393224 | tf_op jit(solution)/shard_map/ppermute | solution.py:463
  17.2 1.6 %shard_map.77 = (bf16[256,512]{1,0:T(8,128)(2,1)S(1)}, bf16[256,512]{1,0:T(8,128)(2,1)S(1)}, bf16[128,512]{1,0:T(8,128)(2,1)S(1)}, bf16[64,512]{1,0:T(8,128)(2,1...) custom-call(bf16[256,512]{1,0:T(8,128)(2,1)S(1)} %copy-done, ...), custom_call_target="tpu_custom_call" | custom-call | flops 8589934592 | bytes 1048576 | tf_op jit(solution)/shard_map/pallas_call | solution.py:484
  18.8 4.7 %collective-permute-done.4.r3 = bf16[64,1024]{1,0:T(8,128)(2,1)S(1)} collective-permute-done((bf16[64,1024]{1,0:T(8,128)(2,1)S(1)}, bf16[64,1024]{1,0:T(8,128)(2,1)S(1)}, u32[]{:S(2)}, u32[]{:S(2)}) %collective-permute-start.4) | collective-permute-done | bytes 131104 | tf_op jit(solution)/shard_map/ppermute | solution.py:463
  23.5 0.1 shard_map.79
  23.7 0.1 collective-permute-start.5
  23.8 0.5 %collective-permute-start.6 = (bf16[128,1024]{1,0:T(8,128)(2,1)S(1)}, bf16[128,1024]{1,0:T(8,128)(2,1)S(1)}, u32[]{:S(2)}, u32[]{:S(2)}) collective-permute-start(bf16[128,1024]{1,0:T(8,128)(2,1)S(1)} %shard_map.78.after), channel_id=1, source_target_pairs={{0,4},{8,12},{16,20},{24,28},{32,36},{40,44},{48,52},{56,60},{64,6... | collective-permute-start | bytes 786440 | tf_op jit(solution)/shard_map/ppermute | solution.py:463
  24.3 0.8 %shard_map.80 = (f32[4,256,128]{2,1,0:T(8,128)S(1)}, f32[4,256,128]{2,1,0:T(8,128)S(1)}, f32[4,256,128]{2,1,0:T(8,128)S(1)}, bf16[4,128,128]{2,1,0:T(8,128)(2,1)...) custom-call(bf16[256,512]{1,0:T(8,128)(2,1)S(1)} %get-tuple-element.69.q0, ...), custom_call_target="tpu_custom_call" | custom-call | flops 1073741824 | bytes 1048576 | tf_op jit(solution)/shard_map/pallas_call | solution.py:495
  25.1 0.2 collective-permute-done.5.got
  25.3 0.6 %shard_map.81 = (bf16[256,1024]{1,0:T(8,128)(2,1)S(1)}, bf16[4,64,256]{2,1,0:T(8,128)(2,1)S(1)}, f32[4,64,128]{2,1,0:T(8,128)S(1)}, f32[4,256,128]{2,1,0:T(8,128...) custom-call(bf16[64,512]{1,0:T(8,128)(2,1)S(1)} %get-tuple-element.77.q2, ...), custom_call_target="tpu_custom_call" | custom-call | flops 268435456 | bytes 1048576 | tf_op jit(solution)/shard_map/pallas_call | solution.py:501
  25.9 1.4 %shard_map.82 = (bf16[256,512]{1,0:T(8,128)(2,1)S(1)}, f32[4,256,128]{2,1,0:T(8,128)S(1)}, f32[4,256,128]{2,1,0:T(8,128)S(1)}, f32[4,256,128]{2,1,0:T(8,128)S(1)...) custom-call(bf16[64,512]{1,0:T(8,128)(2,1)S(1)} %get-tuple-element.7, ...), custom_call_target="tpu_custom_call" | custom-call | tf_op jit(solution)/shard_map/pallas_call | solution.py:506
  27.3 0.2 collective-permute-start.7
  27.5 0.6 %shard_map.83 = (f32[4,128,128]{2,1,0:T(8,128)S(1)}, f32[4,128,128]{2,1,0:T(8,128)S(1)}, f32[128,1024]{1,0:T(8,128)S(1)}, f32[128,1024]{1,0:T(8,128)S(1)}) custom-call(bf16[256,512]{1,0:T(8,128)(2,1)S(1)} %get-tuple-element.69.q0, bf16[128,512]{1,0:T(8,128)(2,1)S(1)} %get-tuple-element.70.q1, bf16[256,512]{1,0:T(8,128)(2,1)S(1)} %get-tuple-element.71.g_ref, ...), custom_call_target="tpu_custom_call" | custom-call | flops 1073741824 | bytes 1048576 | tf_op jit(solution)/shard_map/pallas_call | solution.py:512
  28.1 1.1 %collective-permute-done.7.got = bf16[224,1024]{1,0:T(8,128)(2,1)S(1)} collective-permute-done((bf16[224,1024]{1,0:T(8,128)(2,1)S(1)}, bf16[224,1024]{1,0:T(8,128)(2,1)S(1)}, u32[]{:S(2)}, u32[]{:S(2)}) %collective-permute-start.7) | collective-permute-done | bytes 458784 | tf_op jit(solution)/shard_map/ppermute | solution.py:463
  29.2 0.2 shard_map.84
  29.5 2.5 %collective-permute-start.8 = (bf16[256,1024]{1,0:T(8,128)(2,1)S(1)}, bf16[256,1024]{1,0:T(8,128)(2,1)S(1)}, u32[]{:S(2)}, u32[]{:S(2)}) collective-permute-start(bf16[256,1024]{1,0:T(8,128)(2,1)S(1)} %get-tuple-element.113.after), channel_id=1, source_target_pairs={{4,8},{12,16},{20,24},{28,32},{36,40},{44,48},{52,56},{60,64},{68,... | collective-permute-start | bytes 1572872 | tf_op jit(solution)/shard_map/ppermute | solution.py:463
  32.0 4.1 %collective-permute-start.10 = (bf16[32,1024]{1,0:T(8,128)(2,1)S(1)}, bf16[32,1024]{1,0:T(8,128)(2,1)S(1)}, u32[]{:S(2)}, u32[]{:S(2)}) collective-permute-start(bf16[32,1024]{1,0:T(8,128)(2,1)S(1)} %get-tuple-element.118), channel_id=1, source_target_pairs={{0,24},{4,28},{16,40},{20,44},{32,56},{36,60},{48,72},{52,76},{64,... | collective-permute-start | bytes 196616 | tf_op jit(solution)/shard_map/ppermute | solution.py:463
  36.0 5.4 %collective-permute-start.9 = (bf16[64,1024]{1,0:T(8,128)(2,1)S(1)}, bf16[64,1024]{1,0:T(8,128)(2,1)S(1)}, u32[]{:S(2)}, u32[]{:S(2)}) collective-permute-start(bf16[64,1024]{1,0:T(8,128)(2,1)S(1)} %get-tuple-element.117), channel_id=1, source_target_pairs={{0,20},{8,28},{16,36},{24,44},{32,52},{40,60},{48,68},{56,76},{64,... | collective-permute-start | bytes 393224 | tf_op jit(solution)/shard_map/ppermute | solution.py:463
  41.4 2.7 %shard_map.85 = (bf16[256,512]{1,0:T(8,128)(2,1)}, bf16[256,512]{1,0:T(8,128)(2,1)}, f32[256,1024]{1,0:T(8,128)S(1)}, bf16[192,1024]{1,0:T(8,128)(2,1)S(1)}) custom-call(bf16[256,512]{1,0:T(8,128)(2,1)S(1)} %get-tuple-element.69.q0, bf16[128,512]{1,0:T(8,128)(2,1)S(1)} %get-tuple-element.70.q1, bf16[256,512]{1,0:T(8,128)(2,1)S(1)} %get-tuple-element.71.g_ref, ...), custom_call_target="tpu_custom_call" | custom-call | flops 2147483648 | bytes 1048576 | tf_op jit(solution)/shard_map/pallas_call | solution.py:519
  44.1 2.1 %collective-permute-done.9.r2 = bf16[64,1024]{1,0:T(8,128)(2,1)S(1)} collective-permute-done((bf16[64,1024]{1,0:T(8,128)(2,1)S(1)}, bf16[64,1024]{1,0:T(8,128)(2,1)S(1)}, u32[]{:S(2)}, u32[]{:S(2)}) %collective-permute-start.9) | collective-permute-done | bytes 131104 | tf_op jit(solution)/shard_map/ppermute | solution.py:463
  46.2 0.3 shard_map.86
  46.5 0.1 collective-permute-start.12
  46.6 1.3 %collective-permute-done.12.got = bf16[64,1024]{1,0:T(8,128)(2,1)S(1)} collective-permute-done((bf16[64,1024]{1,0:T(8,128)(2,1)S(1)}, bf16[64,1024]{1,0:T(8,128)(2,1)S(1)}, u32[]{:S(2)}, u32[]{:S(2)}) %collective-permute-start.12) | collective-permute-done | bytes 131104 | tf_op jit(solution)/shard_map/ppermute | solution.py:463
  47.9 1.1 %shard_map.87 = (bf16[256,512]{1,0:T(8,128)(2,1)}, bf16[256,512]{1,0:T(8,128)(2,1)}) custom-call(f32[256,1024]{1,0:T(8,128)S(1)} %get-tuple-element.119.acc, bf16[192,1024]{1,0:T(8,128)(2,1)S(1)} %collective-permute-done.11.near, bf16[64,1024]{1,0:T(8,128)(2,1)S(1)} %collective-permute-done.12.got), custom_call_target="tpu_custom_call" | custom-call | tf_op jit(solution)/shard_map/pallas_call | solution.py:529
  (12 shorter events, 0.0 us)
Async XLA Ops:
  0.6 2.3 %collective-permute-start = (bf16[256,512]{1,0:T(8,128)(2,1)}, bf16[256,512]{1,0:T(8,128)(2,1)S(1)}, u32[]{:S(2)}, u32[]{:S(2)}) collective-permute-start(bf16[256,512]{1,0:T(8,128)(2,1)} %param.5), channel_id=1, source_target_pairs={{0,4},{8,12},{16,20},{24,28},{32,36},{40,44},{48,52},{56,60},{64,6... | collective-permute-start | bytes 786440 | tf_op jit(solution)/shard_map/ppermute | solution.py:463
  1.4 1.7 %collective-permute-start.1 = (bf16[256,512]{1,0:T(8,128)(2,1)}, bf16[256,512]{1,0:T(8,128)(2,1)S(1)}, u32[]{:S(2)}, u32[]{:S(2)}) collective-permute-start(bf16[256,512]{1,0:T(8,128)(2,1)} %param.6), channel_id=1, source_target_pairs={{0,4},{8,12},{16,20},{24,28},{32,36},{40,44},{48,52},{56,60},{64,6... | collective-permute-start | bytes 786440 | tf_op jit(solution)/shard_map/ppermute | solution.py:463
  3.1 14.0 %copy-start = (bf16[256,512]{1,0:T(8,128)(2,1)S(1)}, bf16[256,512]{1,0:T(8,128)(2,1)}, u32[]{:S(2)}) copy-start(bf16[256,512]{1,0:T(8,128)(2,1)} %q_ref.1) | copy-start | bytes 786436
  3.1 14.0 %copy-start.1 = (bf16[256,512]{1,0:T(8,128)(2,1)S(1)}, bf16[256,512]{1,0:T(8,128)(2,1)}, u32[]{:S(2)}) copy-start(bf16[256,512]{1,0:T(8,128)(2,1)} %g_ref.1) | copy-start | bytes 786436
  3.5 11.4 %collective-permute-start.3 = (bf16[64,1024]{1,0:T(8,128)(2,1)S(1)}, bf16[64,1024]{1,0:T(8,128)(2,1)S(1)}, u32[]{:S(2)}, u32[]{:S(2)}) collective-permute-start(bf16[64,1024]{1,0:T(8,128)(2,1)S(1)} %get-tuple-element.80), channel_id=1, source_target_pairs={{0,20},{8,28},{16,36},{24,44},{32,52},{40,60},{48,68},{56,76},{64,... | collective-permute-start | bytes 393224 | tf_op jit(solution)/shard_map/ppermute | solution.py:463
  11.6 11.9 %collective-permute-start.2 = (bf16[256,1024]{1,0:T(8,128)(2,1)S(1)}, bf16[256,1024]{1,0:T(8,128)(2,1)S(1)}, u32[]{:S(2)}, u32[]{:S(2)}) collective-permute-start(bf16[256,1024]{1,0:T(8,128)(2,1)S(1)} %get-tuple-element.79), channel_id=1, source_target_pairs={{4,8},{12,16},{20,24},{28,32},{36,40},{44,48},{52,56},{60,64},{68,... | collective-permute-start | bytes 1572872 | tf_op jit(solution)/shard_map/ppermute | solution.py:463
  14.9 8.6 %collective-permute-start.4 = (bf16[64,1024]{1,0:T(8,128)(2,1)S(1)}, bf16[64,1024]{1,0:T(8,128)(2,1)S(1)}, u32[]{:S(2)}, u32[]{:S(2)}) collective-permute-start(bf16[64,1024]{1,0:T(8,128)(2,1)S(1)} %collective-permute-done.3.r2), channel_id=1, source_target_pairs={{4,8},{20,24},{36,40},{52,56},{68,72},{84,88},{100,104},{116,120},... | collective-permute-start | bytes 393224 | tf_op jit(solution)/shard_map/ppermute | solution.py:463
  23.7 1.6 %collective-permute-start.5 = (bf16[128,1024]{1,0:T(8,128)(2,1)S(1)}, bf16[128,1024]{1,0:T(8,128)(2,1)S(1)}, u32[]{:S(2)}, u32[]{:S(2)}) collective-permute-start(bf16[128,1024]{1,0:T(8,128)(2,1)S(1)} %get-tuple-element.82), channel_id=1, source_target_pairs={{0,4},{8,12},{16,20},{24,28},{32,36},{40,44},{48,52},{56,60},{64,6... | collective-permute-start | bytes 786440 | tf_op jit(solution)/shard_map/ppermute | solution.py:463
  23.8 2.1 %collective-permute-start.6 = (bf16[128,1024]{1,0:T(8,128)(2,1)S(1)}, bf16[128,1024]{1,0:T(8,128)(2,1)S(1)}, u32[]{:S(2)}, u32[]{:S(2)}) collective-permute-start(bf16[128,1024]{1,0:T(8,128)(2,1)S(1)} %shard_map.78.after), channel_id=1, source_target_pairs={{0,4},{8,12},{16,20},{24,28},{32,36},{40,44},{48,52},{56,60},{64,6... | collective-permute-start | bytes 786440 | tf_op jit(solution)/shard_map/ppermute | solution.py:463
  27.3 1.9 %collective-permute-start.7 = (bf16[224,1024]{1,0:T(8,128)(2,1)S(1)}, bf16[224,1024]{1,0:T(8,128)(2,1)S(1)}, u32[]{:S(2)}, u32[]{:S(2)}) collective-permute-start(bf16[224,1024]{1,0:T(8,128)(2,1)S(1)} %get-tuple-element.112), channel_id=1, source_target_pairs={{0,4},{8,12},{16,20},{24,28},{32,36},{40,44},{48,52},{56,60},{64,6... | collective-permute-start | bytes 1376264 | tf_op jit(solution)/shard_map/ppermute | solution.py:463
  29.5 16.7 %collective-permute-start.8 = (bf16[256,1024]{1,0:T(8,128)(2,1)S(1)}, bf16[256,1024]{1,0:T(8,128)(2,1)S(1)}, u32[]{:S(2)}, u32[]{:S(2)}) collective-permute-start(bf16[256,1024]{1,0:T(8,128)(2,1)S(1)} %get-tuple-element.113.after), channel_id=1, source_target_pairs={{4,8},{12,16},{20,24},{28,32},{36,40},{44,48},{52,56},{60,64},{68,... | collective-permute-start | bytes 1572872 | tf_op jit(solution)/shard_map/ppermute | solution.py:463
  32.0 12.2 %collective-permute-start.10 = (bf16[32,1024]{1,0:T(8,128)(2,1)S(1)}, bf16[32,1024]{1,0:T(8,128)(2,1)S(1)}, u32[]{:S(2)}, u32[]{:S(2)}) collective-permute-start(bf16[32,1024]{1,0:T(8,128)(2,1)S(1)} %get-tuple-element.118), channel_id=1, source_target_pairs={{0,24},{4,28},{16,40},{20,44},{32,56},{36,60},{48,72},{52,76},{64,... | collective-permute-start | bytes 196616 | tf_op jit(solution)/shard_map/ppermute | solution.py:463
  36.0 10.2 %collective-permute-start.9 = (bf16[64,1024]{1,0:T(8,128)(2,1)S(1)}, bf16[64,1024]{1,0:T(8,128)(2,1)S(1)}, u32[]{:S(2)}, u32[]{:S(2)}) collective-permute-start(bf16[64,1024]{1,0:T(8,128)(2,1)S(1)} %get-tuple-element.117), channel_id=1, source_target_pairs={{0,20},{8,28},{16,36},{24,44},{32,52},{40,60},{48,68},{56,76},{64,... | collective-permute-start | bytes 393224 | tf_op jit(solution)/shard_map/ppermute | solution.py:463
  44.1 2.5 %collective-permute-start.11 = (bf16[192,1024]{1,0:T(8,128)(2,1)S(1)}, bf16[192,1024]{1,0:T(8,128)(2,1)S(1)}, u32[]{:S(2)}, u32[]{:S(2)}) collective-permute-start(bf16[192,1024]{1,0:T(8,128)(2,1)S(1)} %get-tuple-element.120), channel_id=1, source_target_pairs={{0,4},{8,12},{16,20},{24,28},{32,36},{40,44},{48,52},{56,60},{64,6... | collective-permute-start | bytes 1179656 | tf_op jit(solution)/shard_map/ppermute | solution.py:463
  46.5 1.4 %collective-permute-start.12 = (bf16[64,1024]{1,0:T(8,128)(2,1)S(1)}, bf16[64,1024]{1,0:T(8,128)(2,1)S(1)}, u32[]{:S(2)}, u32[]{:S(2)}) collective-permute-start(bf16[64,1024]{1,0:T(8,128)(2,1)S(1)} %get-tuple-element.121), channel_id=1, source_target_pairs={{0,4},{8,12},{16,20},{24,28},{32,36},{40,44},{48,52},{56,60},{64,6... | collective-permute-start | bytes 393224 | tf_op jit(solution)/shard_map/ppermute | solution.py:463

commit v2 on v1

--- a/solution.py
+++ b/solution.py
@@ -216,6 +216,10 @@
     send[64:] = r1[192:]
 
 
+def forward_kernel(r2, after, send):
+    send[...] = r2[...]
+
+
 def third_split_kernel(r2, r3, after, send):
     send[:64] = r2[...]
     send[64:] = r3[...]
@@ -248,7 +252,7 @@
             )
 
 
-def second_kernel(q2, r1, got, top, zsum, ysum, win, e2, m2, top_out, z_out, y_out):
+def second_kernel(q2, r1, got, top, zsum, ysum, after, win, e2, m2, top_out, z_out, y_out):
     core, chip = place()
     is0 = core == 0
     win[:64] = r1[192:]
@@ -480,17 +484,16 @@
     )
     r2 = swap(msg2, next2)
     r1 = swap(msg1, next1)
-    r3 = swap(r2, forward)
     q0, g0, q1, q2, q3, win, e0, e1, m0, m1, top, zsum, ysum = call(
         local_kernel,
         [out, out, ((128, D), BF), ((64, D), BF), ((32, D), BF), rows(384)]
         + [heads(256, BF, 384), heads(128, BF), stat, heads(128), stat, stat, stat],
         [heads(128), heads(128)],
-        flops=1 << 33,
+        flops=1 << 31,
     )(query, out_grad, kv, near, s1)
-    (send,) = call(third_split_kernel, [rows(128)], specs="vva")(r2, r3, top)
-    got3 = swap(send, sibling)
-    outer1, send = call(second_split_kernel, [rows(128), rows(128)], specs="va")(r1, send)
+    (send,) = call(forward_kernel, [rows(64)], specs="va")(r2, top)
+    r3 = swap(send, forward)
+    outer1, send = call(second_split_kernel, [rows(128), rows(128)], specs="va")(r1, top)
     got2 = swap(send, sibling)
     top, zsum, ysum, eo0, eo1, mo0, mo1 = call(
         outer_kernel,
@@ -498,11 +501,14 @@
         [heads(128), heads(128)],
         flops=1 << 30,
     )(q0, q1, r1, outer1, top, zsum, ysum)
+    (send,) = call(third_split_kernel, [rows(128)], specs="vva")(r2, r3, top)
+    got3 = swap(send, sibling)
     w2, e2, m2, top, zsum, ysum = call(
         second_kernel,
         [rows(256), heads(64, BF, 256), heads(64), stat, stat, stat],
         flops=1 << 28,
-    )(q2, r1, got2, top, zsum, ysum)
+        specs="v" * 6 + "a",
+    )(q2, r1, got2, top, zsum, ysum, send)
     att, best, inv, delta, dq2, dq3, own2, own3, cross3, send = call(
         far_kernel,
         [out, stat, stat, stat, heads(64), heads(32), rows(64, F32), rows(64, F32), rows(32, F32), rows(224)],

time: 49.6 us -> 53.3 us (1.075)
  waiting for transfers between devices: 11 us -> 13.5 us
  starting transfers between devices: 26 us -> 26.7 us
    ppermute x13, waiting for transfers between devices: 11 us -> 13.5 us  [swap(): return lax.ppermute(value, 'seq', pairs + [(b, a) for a, b in pairs])]
    ppermute x13, starting transfers between devices: 26 us -> 26.7 us  [swap(): return lax.ppermute(value, 'seq', pairs + [(b, a) for a, b in pairs])]
  transfers between devices with their start and end apart: 13 -> 13, of which waited for: 7 -> 7; matrix products, arithmetic and copies ran while one was open for 2% -> 2% of each run, Pallas kernels for 14% -> 13%
where the time goes in v2:
time: 53.3 us; the launch traced here: 52.4 us
  starting transfers between devices  26.7 us (50%)
  waiting for transfers between devices  13.5 us (25%)
  Pallas kernels  10.2 us (19%)
  other arithmetic  1.08 us (2%)
  between operations  0.84 us (2%)
    ppermute x13, starting transfers between devices, swap(): return lax.ppermute(value, 'seq', pairs + [(b, a) for a, b in pairs])  26.7 us
    ppermute x13, waiting for transfers between devices, swap(): return lax.ppermute(value, 'seq', pairs + [(b, a) for a, b in pairs])  13.5 us
    pallas_call x1, Pallas kernels, per_device(): call(rest_kernel, [out, out, rows(256, F32), rows(192)], [stat], flops=1...  2.69 us
    pallas_call x1, Pallas kernels, per_device(): call(local_kernel, [out, out, ((128, D), BF), ((64, D), BF), ((32, D), BF...  1.6 us
    pallas_call x1, Pallas kernels, per_device(): call(far_kernel, [out, stat, stat, stat, heads(64), heads(32), rows(64, F...  1.41 us
    pallas_call x1, Pallas kernels, per_device(): key_grad, value_grad = call(final_kernel, [out, out])(acc, near, got)  1.15 us
    concatenate x1, other arithmetic, per_device(): jnp.concatenate([key_rows, value_rows], axis=1)  1.08 us
  transfers between devices with their start and end apart: 13, of which 7 were waited for; matrix products, arithmetic and copies ran while one was open for 2% of the time, Pallas kernels for 13%

profile of v2, /device:TPU:11, one launch (start us, length us, event | category | flops | bytes accessed | tf_op | source)
XLA Modules:
  0.0 52.4 jit_solution(858125217314183790)
XLA Ops:
  0.6 0.8 %collective-permute-start = (bf16[256,512]{1,0:T(8,128)(2,1)}, bf16[256,512]{1,0:T(8,128)(2,1)S(1)}, u32[]{:S(2)}, u32[]{:S(2)}) collective-permute-start(bf16[256,512]{1,0:T(8,128)(2,1)} %param.5), channel_id=1, source_target_pairs={{0,4},{8,12},{16,20},{24,28},{32,36},{40,44},{48,52},{56,60},{64,6... | collective-permute-start | bytes 786440 | tf_op jit(solution)/shard_map/ppermute | solution.py:467
  1.4 0.1 collective-permute-start.1
  1.5 1.1 %pad_maximum_fusion.raw = bf16[256,1024]{1,0:T(8,128)(2,1)S(1)} fusion(bf16[256,512]{1,0:T(8,128)(2,1)} %param.6, bf16[256,512]{1,0:T(8,128)(2,1)} %param.5), kind=kLoop, calls=%fused_computation | loop fusion | flops 1048576 | bytes 1048576 | tf_op jit(solution)/shard_map/concatenate | solution.py:480
  2.6 0.3 shard_map.75
  2.9 0.2 collective-permute-done.1.vs
  3.1 0.4 shard_map.76
  3.5 3.8 %collective-permute-start.2 = (bf16[256,1024]{1,0:T(8,128)(2,1)S(1)}, bf16[256,1024]{1,0:T(8,128)(2,1)S(1)}, u32[]{:S(2)}, u32[]{:S(2)}) collective-permute-start(bf16[256,1024]{1,0:T(8,128)(2,1)S(1)} %get-tuple-element.79), channel_id=1, source_target_pairs={{4,8},{12,16},{20,24},{28,32},{36,40},{44,48},{52,56},{60,64},{68,... | collective-permute-start | bytes 1572872 | tf_op jit(solution)/shard_map/ppermute | solution.py:467
  7.3 6.9 %collective-permute-start.4 = (bf16[64,1024]{1,0:T(8,128)(2,1)S(1)}, bf16[64,1024]{1,0:T(8,128)(2,1)S(1)}, u32[]{:S(2)}, u32[]{:S(2)}) collective-permute-start(bf16[64,1024]{1,0:T(8,128)(2,1)S(1)} %get-tuple-element.88), channel_id=1, source_target_pairs={{0,20},{8,28},{16,36},{24,44},{32,52},{40,60},{48,68},{56,76},{64,... | collective-permute-start | bytes 393224 | tf_op jit(solution)/shard_map/ppermute | solution.py:467
  14.3 1.6 %shard_map.77 = (bf16[256,512]{1,0:T(8,128)(2,1)S(1)}, bf16[256,512]{1,0:T(8,128)(2,1)S(1)}, bf16[128,512]{1,0:T(8,128)(2,1)S(1)}, bf16[64,512]{1,0:T(8,128)(2,1...) custom-call(bf16[256,512]{1,0:T(8,128)(2,1)S(1)} %copy-done, ...), custom_call_target="tpu_custom_call" | custom-call | flops 2147483648 | bytes 1048576 | tf_op jit(solution)/shard_map/pallas_call | solution.py:487
  15.9 3.6 %collective-permute-done.4.r2 = bf16[64,1024]{1,0:T(8,128)(2,1)S(1)} collective-permute-done((bf16[64,1024]{1,0:T(8,128)(2,1)S(1)}, bf16[64,1024]{1,0:T(8,128)(2,1)S(1)}, u32[]{:S(2)}, u32[]{:S(2)}) %collective-permute-start.4) | collective-permute-done | bytes 131104 | tf_op jit(solution)/shard_map/ppermute | solution.py:467
  19.5 2.7 %collective-permute-start.5 = (bf16[64,1024]{1,0:T(8,128)(2,1)S(1)}, bf16[64,1024]{1,0:T(8,128)(2,1)S(1)}, u32[]{:S(2)}, u32[]{:S(2)}) collective-permute-start(bf16[64,1024]{1,0:T(8,128)(2,1)S(1)} %shard_map.80), channel_id=1, source_target_pairs={{4,8},{20,24},{36,40},{52,56},{68,72},{84,88},{100,104},{116,120},... | collective-permute-start | bytes 393224 | tf_op jit(solution)/shard_map/ppermute | solution.py:467
  22.1 0.1 shard_map.78
  22.3 0.1 collective-permute-start.3
  22.4 0.8 %shard_map.79 = (f32[4,256,128]{2,1,0:T(8,128)S(1)}, f32[4,256,128]{2,1,0:T(8,128)S(1)}, f32[4,256,128]{2,1,0:T(8,128)S(1)}, bf16[4,128,128]{2,1,0:T(8,128)(2,1)...) custom-call(bf16[256,512]{1,0:T(8,128)(2,1)S(1)} %get-tuple-element.69.q0, ...), custom_call_target="tpu_custom_call" | custom-call | flops 1073741824 | bytes 1048576 | tf_op jit(solution)/shard_map/pallas_call | solution.py:498
  23.2 2.6 %collective-permute-done.5.r3 = bf16[64,1024]{1,0:T(8,128)(2,1)S(1)} collective-permute-done((bf16[64,1024]{1,0:T(8,128)(2,1)S(1)}, bf16[64,1024]{1,0:T(8,128)(2,1)S(1)}, u32[]{:S(2)}, u32[]{:S(2)}) %collective-permute-start.5) | collective-permute-done | bytes 131104 | tf_op jit(solution)/shard_map/ppermute | solution.py:467
  25.8 0.1 collective-permute-start.6
  25.9 0.6 %shard_map.82 = (bf16[256,1024]{1,0:T(8,128)(2,1)S(1)}, bf16[4,64,256]{2,1,0:T(8,128)(2,1)S(1)}, f32[4,64,128]{2,1,0:T(8,128)S(1)}, f32[4,256,128]{2,1,0:T(8,128...) custom-call(bf16[64,512]{1,0:T(8,128)(2,1)S(1)} %get-tuple-element.77.q2, ...), custom_call_target="tpu_custom_call" | custom-call | flops 268435456 | bytes 1048576 | tf_op jit(solution)/shard_map/pallas_call | solution.py:506
  26.5 0.9 %collective-permute-done.6.got = bf16[128,1024]{1,0:T(8,128)(2,1)S(1)} collective-permute-done((bf16[128,1024]{1,0:T(8,128)(2,1)S(1)}, bf16[128,1024]{1,0:T(8,128)(2,1)S(1)}, u32[]{:S(2)}, u32[]{:S(2)}) %collective-permute-start.6) | collective-permute-done | bytes 262176 | tf_op jit(solution)/shard_map/ppermute | solution.py:467
  27.4 1.4 %shard_map.83 = (bf16[256,512]{1,0:T(8,128)(2,1)S(1)}, f32[4,256,128]{2,1,0:T(8,128)S(1)}, f32[4,256,128]{2,1,0:T(8,128)S(1)}, f32[4,256,128]{2,1,0:T(8,128)S(1)...) custom-call(bf16[64,512]{1,0:T(8,128)(2,1)S(1)} %get-tuple-element.7, ...), custom_call_target="tpu_custom_call" | custom-call | tf_op jit(solution)/shard_map/pallas_call | solution.py:512
  28.8 0.2 collective-permute-start.7
  29.1 0.6 %shard_map.84 = (f32[4,128,128]{2,1,0:T(8,128)S(1)}, f32[4,128,128]{2,1,0:T(8,128)S(1)}, f32[128,1024]{1,0:T(8,128)S(1)}, f32[128,1024]{1,0:T(8,128)S(1)}) custom-call(bf16[256,512]{1,0:T(8,128)(2,1)S(1)} %get-tuple-element.69.q0, bf16[128,512]{1,0:T(8,128)(2,1)S(1)} %get-tuple-element.70.q1, bf16[256,512]{1,0:T(8,128)(2,1)S(1)} %get-tuple-element.71.g_ref, ...), custom_call_target="tpu_custom_call" | custom-call | flops 1073741824 | bytes 1048576 | tf_op jit(solution)/shard_map/pallas_call | solution.py:518
  29.6 1.1 %collective-permute-done.7.got = bf16[224,1024]{1,0:T(8,128)(2,1)S(1)} collective-permute-done((bf16[224,1024]{1,0:T(8,128)(2,1)S(1)}, bf16[224,1024]{1,0:T(8,128)(2,1)S(1)}, u32[]{:S(2)}, u32[]{:S(2)}) %collective-permute-start.7) | collective-permute-done | bytes 458784 | tf_op jit(solution)/shard_map/ppermute | solution.py:467
  30.7 0.2 shard_map.85
  31.0 2.7 %collective-permute-start.8 = (bf16[256,1024]{1,0:T(8,128)(2,1)S(1)}, bf16[256,1024]{1,0:T(8,128)(2,1)S(1)}, u32[]{:S(2)}, u32[]{:S(2)}) collective-permute-start(bf16[256,1024]{1,0:T(8,128)(2,1)S(1)} %get-tuple-element.113.after), channel_id=1, source_target_pairs={{4,8},{12,16},{20,24},{28,32},{36,40},{44,48},{52,56},{60,64},{68,... | collective-permute-start | bytes 1572872 | tf_op jit(solution)/shard_map/ppermute | solution.py:467
  33.6 5.2 %collective-permute-start.10 = (bf16[32,1024]{1,0:T(8,128)(2,1)S(1)}, bf16[32,1024]{1,0:T(8,128)(2,1)S(1)}, u32[]{:S(2)}, u32[]{:S(2)}) collective-permute-start(bf16[32,1024]{1,0:T(8,128)(2,1)S(1)} %get-tuple-element.118), channel_id=1, source_target_pairs={{0,24},{4,28},{16,40},{20,44},{32,56},{36,60},{48,72},{52,76},{64,... | collective-permute-start | bytes 196616 | tf_op jit(solution)/shard_map/ppermute | solution.py:467
  38.9 4.0 %collective-permute-start.9 = (bf16[64,1024]{1,0:T(8,128)(2,1)S(1)}, bf16[64,1024]{1,0:T(8,128)(2,1)S(1)}, u32[]{:S(2)}, u32[]{:S(2)}) collective-permute-start(bf16[64,1024]{1,0:T(8,128)(2,1)S(1)} %get-tuple-element.117), channel_id=1, source_target_pairs={{0,20},{8,28},{16,36},{24,44},{32,52},{40,60},{48,68},{56,76},{64,... | collective-permute-start | bytes 393224 | tf_op jit(solution)/shard_map/ppermute | solution.py:467
  42.9 2.7 %shard_map.86 = (bf16[256,512]{1,0:T(8,128)(2,1)}, bf16[256,512]{1,0:T(8,128)(2,1)}, f32[256,1024]{1,0:T(8,128)S(1)}, bf16[192,1024]{1,0:T(8,128)(2,1)S(1)}) custom-call(bf16[256,512]{1,0:T(8,128)(2,1)S(1)} %get-tuple-element.69.q0, bf16[128,512]{1,0:T(8,128)(2,1)S(1)} %get-tuple-element.70.q1, bf16[256,512]{1,0:T(8,128)(2,1)S(1)} %get-tuple-element.71.g_ref, ...), custom_call_target="tpu_custom_call" | custom-call | flops 2147483648 | bytes 1048576 | tf_op jit(solution)/shard_map/pallas_call | solution.py:525
  45.6 3.8 %collective-permute-done.9.r2 = bf16[64,1024]{1,0:T(8,128)(2,1)S(1)} collective-permute-done((bf16[64,1024]{1,0:T(8,128)(2,1)S(1)}, bf16[64,1024]{1,0:T(8,128)(2,1)S(1)}, u32[]{:S(2)}, u32[]{:S(2)}) %collective-permute-start.9) | collective-permute-done | bytes 131104 | tf_op jit(solution)/shard_map/ppermute | solution.py:467
  49.5 0.3 shard_map.87
  49.8 0.1 collective-permute-start.12
  49.9 1.3 %collective-permute-done.12.got = bf16[64,1024]{1,0:T(8,128)(2,1)S(1)} collective-permute-done((bf16[64,1024]{1,0:T(8,128)(2,1)S(1)}, bf16[64,1024]{1,0:T(8,128)(2,1)S(1)}, u32[]{:S(2)}, u32[]{:S(2)}) %collective-permute-start.12) | collective-permute-done | bytes 131104 | tf_op jit(solution)/shard_map/ppermute | solution.py:467
  51.2 1.2 %shard_map.88 = (bf16[256,512]{1,0:T(8,128)(2,1)}, bf16[256,512]{1,0:T(8,128)(2,1)}) custom-call(f32[256,1024]{1,0:T(8,128)S(1)} %get-tuple-element.119.acc, bf16[192,1024]{1,0:T(8,128)(2,1)S(1)} %collective-permute-done.11.near, bf16[64,1024]{1,0:T(8,128)(2,1)S(1)} %collective-permute-done.12.got), custom_call_target="tpu_custom_call" | custom-call | tf_op jit(solution)/shard_map/pallas_call | solution.py:535
  (13 shorter events, 0.1 us)
Async XLA Ops:
  0.6 2.3 %collective-permute-start = (bf16[256,512]{1,0:T(8,128)(2,1)}, bf16[256,512]{1,0:T(8,128)(2,1)S(1)}, u32[]{:S(2)}, u32[]{:S(2)}) collective-permute-start(bf16[256,512]{1,0:T(8,128)(2,1)} %param.5), channel_id=1, source_target_pairs={{0,4},{8,12},{16,20},{24,28},{32,36},{40,44},{48,52},{56,60},{64,6... | collective-permute-start | bytes 786440 | tf_op jit(solution)/shard_map/ppermute | solution.py:467
  1.4 1.7 %collective-permute-start.1 = (bf16[256,512]{1,0:T(8,128)(2,1)}, bf16[256,512]{1,0:T(8,128)(2,1)S(1)}, u32[]{:S(2)}, u32[]{:S(2)}) collective-permute-start(bf16[256,512]{1,0:T(8,128)(2,1)} %param.6), channel_id=1, source_target_pairs={{0,4},{8,12},{16,20},{24,28},{32,36},{40,44},{48,52},{56,60},{64,6... | collective-permute-start | bytes 786440 | tf_op jit(solution)/shard_map/ppermute | solution.py:467
  3.1 11.1 %copy-start = (bf16[256,512]{1,0:T(8,128)(2,1)S(1)}, bf16[256,512]{1,0:T(8,128)(2,1)}, u32[]{:S(2)}) copy-start(bf16[256,512]{1,0:T(8,128)(2,1)} %q_ref.1) | copy-start | bytes 786436
  3.1 11.1 %copy-start.1 = (bf16[256,512]{1,0:T(8,128)(2,1)S(1)}, bf16[256,512]{1,0:T(8,128)(2,1)}, u32[]{:S(2)}) copy-start(bf16[256,512]{1,0:T(8,128)(2,1)} %g_ref.1) | copy-start | bytes 786436
  3.5 18.6 %collective-permute-start.2 = (bf16[256,1024]{1,0:T(8,128)(2,1)S(1)}, bf16[256,1024]{1,0:T(8,128)(2,1)S(1)}, u32[]{:S(2)}, u32[]{:S(2)}) collective-permute-start(bf16[256,1024]{1,0:T(8,128)(2,1)S(1)} %get-tuple-element.79), channel_id=1, source_target_pairs={{4,8},{12,16},{20,24},{28,32},{36,40},{44,48},{52,56},{60,64},{68,... | collective-permute-start | bytes 1572872 | tf_op jit(solution)/shard_map/ppermute | solution.py:467
  7.3 12.1 %collective-permute-start.4 = (bf16[64,1024]{1,0:T(8,128)(2,1)S(1)}, bf16[64,1024]{1,0:T(8,128)(2,1)S(1)}, u32[]{:S(2)}, u32[]{:S(2)}) collective-permute-start(bf16[64,1024]{1,0:T(8,128)(2,1)S(1)} %get-tuple-element.88), channel_id=1, source_target_pairs={{0,20},{8,28},{16,36},{24,44},{32,52},{40,60},{48,68},{56,76},{64,... | collective-permute-start | bytes 393224 | tf_op jit(solution)/shard_map/ppermute | solution.py:467
  19.5 6.3 %collective-permute-start.5 = (bf16[64,1024]{1,0:T(8,128)(2,1)S(1)}, bf16[64,1024]{1,0:T(8,128)(2,1)S(1)}, u32[]{:S(2)}, u32[]{:S(2)}) collective-permute-start(bf16[64,1024]{1,0:T(8,128)(2,1)S(1)} %shard_map.80), channel_id=1, source_target_pairs={{4,8},{20,24},{36,40},{52,56},{68,72},{84,88},{100,104},{116,120},... | collective-permute-start | bytes 393224 | tf_op jit(solution)/shard_map/ppermute | solution.py:467
  22.3 3.6 %collective-permute-start.3 = (bf16[128,1024]{1,0:T(8,128)(2,1)S(1)}, bf16[128,1024]{1,0:T(8,128)(2,1)S(1)}, u32[]{:S(2)}, u32[]{:S(2)}) collective-permute-start(bf16[128,1024]{1,0:T(8,128)(2,1)S(1)} %get-tuple-element.81), channel_id=1, source_target_pairs={{0,4},{8,12},{16,20},{24,28},{32,36},{40,44},{48,52},{56,60},{64,6... | collective-permute-start | bytes 786440 | tf_op jit(solution)/shard_map/ppermute | solution.py:467
  25.8 1.6 %collective-permute-start.6 = (bf16[128,1024]{1,0:T(8,128)(2,1)S(1)}, bf16[128,1024]{1,0:T(8,128)(2,1)S(1)}, u32[]{:S(2)}, u32[]{:S(2)}) collective-permute-start(bf16[128,1024]{1,0:T(8,128)(2,1)S(1)} %shard_map.81.after), channel_id=1, source_target_pairs={{0,4},{8,12},{16,20},{24,28},{32,36},{40,44},{48,52},{56,60},{64,6... | collective-permute-start | bytes 786440 | tf_op jit(solution)/shard_map/ppermute | solution.py:467
  28.8 1.9 %collective-permute-start.7 = (bf16[224,1024]{1,0:T(8,128)(2,1)S(1)}, bf16[224,1024]{1,0:T(8,128)(2,1)S(1)}, u32[]{:S(2)}, u32[]{:S(2)}) collective-permute-start(bf16[224,1024]{1,0:T(8,128)(2,1)S(1)} %get-tuple-element.112), channel_id=1, source_target_pairs={{0,4},{8,12},{16,20},{24,28},{32,36},{40,44},{48,52},{56,60},{64,6... | collective-permute-start | bytes 1376264 | tf_op jit(solution)/shard_map/ppermute | solution.py:467
  31.0 18.5 %collective-permute-start.8 = (bf16[256,1024]{1,0:T(8,128)(2,1)S(1)}, bf16[256,1024]{1,0:T(8,128)(2,1)S(1)}, u32[]{:S(2)}, u32[]{:S(2)}) collective-permute-start(bf16[256,1024]{1,0:T(8,128)(2,1)S(1)} %get-tuple-element.113.after), channel_id=1, source_target_pairs={{4,8},{12,16},{20,24},{28,32},{36,40},{44,48},{52,56},{60,64},{68,... | collective-permute-start | bytes 1572872 | tf_op jit(solution)/shard_map/ppermute | solution.py:467
  33.6 12.0 %collective-permute-start.10 = (bf16[32,1024]{1,0:T(8,128)(2,1)S(1)}, bf16[32,1024]{1,0:T(8,128)(2,1)S(1)}, u32[]{:S(2)}, u32[]{:S(2)}) collective-permute-start(bf16[32,1024]{1,0:T(8,128)(2,1)S(1)} %get-tuple-element.118), channel_id=1, source_target_pairs={{0,24},{4,28},{16,40},{20,44},{32,56},{36,60},{48,72},{52,76},{64,... | collective-permute-start | bytes 196616 | tf_op jit(solution)/shard_map/ppermute | solution.py:467
  38.9 10.6 %collective-permute-start.9 = (bf16[64,1024]{1,0:T(8,128)(2,1)S(1)}, bf16[64,1024]{1,0:T(8,128)(2,1)S(1)}, u32[]{:S(2)}, u32[]{:S(2)}) collective-permute-start(bf16[64,1024]{1,0:T(8,128)(2,1)S(1)} %get-tuple-element.117), channel_id=1, source_target_pairs={{0,20},{8,28},{16,36},{24,44},{32,52},{40,60},{48,68},{56,76},{64,... | collective-permute-start | bytes 393224 | tf_op jit(solution)/shard_map/ppermute | solution.py:467
  45.6 4.3 %collective-permute-start.11 = (bf16[192,1024]{1,0:T(8,128)(2,1)S(1)}, bf16[192,1024]{1,0:T(8,128)(2,1)S(1)}, u32[]{:S(2)}, u32[]{:S(2)}) collective-permute-start(bf16[192,1024]{1,0:T(8,128)(2,1)S(1)} %get-tuple-element.120), channel_id=1, source_target_pairs={{0,4},{8,12},{16,20},{24,28},{32,36},{40,44},{48,52},{56,60},{64,6... | collective-permute-start | bytes 1179656 | tf_op jit(solution)/shard_map/ppermute | solution.py:467
  49.8 1.4 %collective-permute-start.12 = (bf16[64,1024]{1,0:T(8,128)(2,1)S(1)}, bf16[64,1024]{1,0:T(8,128)(2,1)S(1)}, u32[]{:S(2)}, u32[]{:S(2)}) collective-permute-start(bf16[64,1024]{1,0:T(8,128)(2,1)S(1)} %get-tuple-element.121), channel_id=1, source_target_pairs={{0,4},{8,12},{16,20},{24,28},{32,36},{40,44},{48,52},{56,60},{64,6... | collective-permute-start | bytes 393224 | tf_op jit(solution)/shard_map/ppermute | solution.py:467

commit v3 on v2

--- a/solution.py
+++ b/solution.py
@@ -220,9 +220,30 @@
     send[...] = r2[...]
 
 
-def third_split_kernel(r2, r3, after, send):
-    send[:64] = r2[...]
-    send[64:] = r3[...]
+def third_kernel(q3, r2, got2, r3, got3, top, zsum, ysum, w3, e3, m3, top_out, z_out, y_out):
+    core, chip = place()
+    is0 = core == 0
+    w3[:64] = r2[...]
+    w3[64:128] = got2[...]
+    w3[128:192] = jnp.where(lax.rem(core + chip, 2) == 1, r3[...], got3[...])
+    w3[192:] = jnp.zeros((64, FULL), BF)
+    low2, high2 = chip >= 2, chip <= 29
+    even = lax.rem(chip, 2) == 0
+    cross_bad = penalty(jnp.where(even, chip <= 28, chip >= 3))
+    lane = lax.broadcasted_iota(jnp.int32, (1, 256), 1)
+    own_bad = penalty(jnp.where(is0, high2, low2))
+    sib_bad = penalty(jnp.where(is0, low2, high2))
+    bias = jnp.where(
+        lane < 64, own_bad, jnp.where(lane < 128, sib_bad, jnp.where(lane < 192, cross_bad, NEG))
+    )
+    results = soft([(q3[:, head(h)], w3[:, head(h)], w3[:, head(HEADS + h)], bias) for h in range(HEADS)])
+    for h in range(HEADS):
+        e3[h], m3[h], d, n = results[h]
+        for c in range(2):
+            r, a = slice(c * 128, (c + 1) * 128), slice(c * 16, (c + 1) * 16)
+            top_out[h, r], z_out[h, r], y_out[h, r], _ = merge(
+                top[h, r], zsum[h, r], ysum[h, r], [(m3[h, a], d[a], n[a], 3)]
+            )
 
 
 def outer_kernel(q0, q1, r1, l1, top, zsum, ysum, top_out, z_out, y_out, e0, e1, m0, m1, d1, n1):
@@ -252,7 +273,7 @@
             )
 
 
-def second_kernel(q2, r1, got, top, zsum, ysum, after, win, e2, m2, top_out, z_out, y_out):
+def second_kernel(q2, r1, got, top, zsum, ysum, win, e2, m2, top_out, z_out, y_out):
     core, chip = place()
     is0 = core == 0
     win[:64] = r1[192:]
@@ -274,51 +295,32 @@
 
 
 def far_kernel(
-    q2, q3, g_ref, top, zsum, ysum, w2, e2, m2, r2, r3, got,
-    att, best_out, inv_out, delta_out, dq2, dq3, own2, own3, cross3, send,
-    w3,
+    q2, q3, g_ref, top, zsum, ysum, w2, e2, m2, w3, e3, m3,
+    att, inv_out, delta_out, dq2, dq3, own2, own3, cross3, send,
 ):
     core, chip = place()
-    is0 = core == 0
-    w3[:64] = r2[...]
-    w3[64:128] = got[:64]
-    w3[128:192] = jnp.where(lax.rem(core + chip, 2) == 1, r3[...], got[64:])
-    w3[192:] = jnp.zeros((64, FULL), BF)
     holder = lax.rem(core + chip, 2) == 1
-    low2, high2 = chip >= 2, chip <= 29
-    even = lax.rem(chip, 2) == 0
-    cross_bad = penalty(jnp.where(even, chip <= 28, chip >= 3))
-    lane = lax.broadcasted_iota(jnp.int32, (1, 256), 1)
-    own_bad = penalty(jnp.where(is0, high2, low2))
-    sib_bad = penalty(jnp.where(is0, low2, high2))
-    bias3 = jnp.where(
-        lane < 64, own_bad, jnp.where(lane < 128, sib_bad, jnp.where(lane < 192, cross_bad, NEG))
-    )
-    third = soft([(q3[:, head(h)], w3[:, head(h)], w3[:, head(HEADS + h)], bias3) for h in range(HEADS)])
     units = []
     for h in range(HEADS):
         kl, vl = head(h), head(HEADS + h)
-        e3, m3, d3, n3 = third[h]
         grads = ([], [])
         drifts = ([], [])
         for c in range(2):
             r = slice(c * 128, (c + 1) * 128)
             a, b = slice(c * 32, (c + 1) * 32), slice(c * 16, (c + 1) * 16)
-            best, z, y, factors = merge(top[h, r], zsum[h, r], ysum[h, r], [(m3[b], d3[b], n3[b], 3)])
-            inv = 1.0 / z
-            y = y * inv
+            best = top[h, r]
+            inv = 1.0 / zsum[h, r]
+            y = ysum[h, r] * inv
             att[r, kl] = y.astype(BF)
             g = g_ref[r, kl].astype(F32)
             delta = lanes128(jnp.sum(g * y, axis=1, keepdims=True))
-            best_out[h, r] = best
             inv_out[h, r] = inv
             delta_out[h, r] = delta
-            factors = [4.0 * jnp.exp2(expand(m2[h, a], 2) - best)] + factors
-            for i in range(2):
-                share = factors[i] * inv
+            for i, (m, rows) in enumerate(((m2, a), (m3, b))):
+                share = jnp.exp2(expand(m[h, rows], i + 2) - best) * (2.0 ** (i + 2) * inv)
                 grads[i].append(fold(share * g, i + 2))
                 drifts[i].append(fold(share * delta, i + 2))
-        for i, (q, w, e) in enumerate(((q2, w2, e2[h]), (q3, w3, e3))):
+        for i, (q, w, e) in enumerate(((q2, w2, e2[h]), (q3, w3, e3[h]))):
             grad = jnp.concatenate(grads[i], axis=0).astype(BF)
             units.append((q[:, kl], w[:, kl], w[:, vl], e, grad, jnp.concatenate(drifts[i], axis=0)))
     results = backward(units)
@@ -489,10 +491,17 @@
         [out, out, ((128, D), BF), ((64, D), BF), ((32, D), BF), rows(384)]
         + [heads(256, BF, 384), heads(128, BF), stat, heads(128), stat, stat, stat],
         [heads(128), heads(128)],
-        flops=1 << 31,
+        flops=1 << 33,
     )(query, out_grad, kv, near, s1)
     (send,) = call(forward_kernel, [rows(64)], specs="va")(r2, top)
     r3 = swap(send, forward)
+    got2 = swap(send, sibling)
+    got3 = swap(r3, sibling)
+    w3, e3, m3, top, zsum, ysum = call(
+        third_kernel,
+        [rows(256), heads(32, BF, 256), heads(32), stat, stat, stat],
+        flops=1 << 28,
+    )(q3, r2, got2, r3, got3, top, zsum, ysum)
     outer1, send = call(second_split_kernel, [rows(128), rows(128)], specs="va")(r1, top)
     got2 = swap(send, sibling)
     top, zsum, ysum, eo0, eo1, mo0, mo1 = call(
@@ -501,23 +510,19 @@
         [heads(128), heads(128)],
         flops=1 << 30,
     )(q0, q1, r1, outer1, top, zsum, ysum)
-    (send,) = call(third_split_kernel, [rows(128)], specs="vva")(r2, r3, top)
-    got3 = swap(send, sibling)
     w2, e2, m2, top, zsum, ysum = call(
         second_kernel,
         [rows(256), heads(64, BF, 256), heads(64), stat, stat, stat],
         flops=1 << 28,
-        specs="v" * 6 + "a",
-    )(q2, r1, got2, top, zsum, ysum, send)
-    att, best, inv, delta, dq2, dq3, own2, own3, cross3, send = call(
+    )(q2, r1, got2, top, zsum, ysum)
+    att, inv, delta, dq2, dq3, own2, own3, cross3, send = call(
         far_kernel,
-        [out, stat, stat, stat, heads(64), heads(32), rows(64, F32), rows(64, F32), rows(32, F32), rows(224)],
-        [rows(256)],
-    )(q2, q3, g0, top, zsum, ysum, w2, e2, m2, r2, r3, got3)
+        [out, stat, stat, heads(64), heads(32), rows(64, F32), rows(64, F32), rows(32, F32), rows(224)],
+    )(q2, q3, g0, top, zsum, ysum, w2, e2, m2, w3, e3, m3)
     got = swap(send, sibling)
     dqo0, dqo1, d0, d1 = call(
         outer_back_kernel, [heads(128), heads(128), rows(128, F32), rows(128, F32)], flops=1 << 30
-    )(q0, q1, g0, r1, outer1, eo0, eo1, mo0, mo1, best, inv, delta)
+    )(q0, q1, g0, r1, outer1, eo0, eo1, mo0, mo1, top, inv, delta)
     msg1, msg2, msg3 = call(join_kernel, [rows(256), rows(64), rows(32)])(own2, own3, cross3, d0, d1, got)
     r1 = swap(msg1, next1)
     r2 = swap(msg2, next2)
@@ -528,7 +533,7 @@
         [stat],
         flops=1 << 31,
         specs="v" * 17 + "a",
-    )(q0, q1, g0, win, s1, e0, e1, m0, m1, best, inv, delta, dqo0, dqo1, dq2, dq3, att, msg1)
+    )(q0, q1, g0, win, s1, e0, e1, m0, m1, top, inv, delta, dqo0, dqo1, dq2, dq3, att, msg1)
     near = swap(send, sibling)
     acc, send = call(add_kernel, [rows(256, F32), rows(64)], flops=1 << 34)(acc, r1, r2, r3)
     got = swap(send, sibling)

time: 53.3 us -> 51.1 us (0.959)
  waiting for transfers between devices: 13.5 us -> 11.2 us
    ppermute x13 -> x14, waiting for transfers between devices: 13.5 us -> 11.2 us  [swap(): return lax.ppermute(value, 'seq', pairs + [(b, a) for a, b in pairs])]
    ppermute x13 -> x14, starting transfers between devices: 26.7 us -> 27.1 us  [swap(): return lax.ppermute(value, 'seq', pairs + [(b, a) for a, b in pairs])]
  transfers between devices with their start and end apart: 13 -> 14, of which waited for: 7 -> 7; matrix products, arithmetic and copies ran while one was open for 2% -> 2% of each run, Pallas kernels for 13% -> 14%
where the time goes in v3:
time: 51.1 us; the launch traced here: 50.5 us
  starting transfers between devices  27.1 us (53%)
  waiting for transfers between devices  11.2 us (22%)
  Pallas kernels  10.3 us (20%)
  other arithmetic  1.08 us (2%)
  between operations  0.85 us (2%)
    ppermute x14, starting transfers between devices, swap(): return lax.ppermute(value, 'seq', pairs + [(b, a) for a, b in pairs])  27.1 us
    ppermute x14, waiting for transfers between devices, swap(): return lax.ppermute(value, 'seq', pairs + [(b, a) for a, b in pairs])  11.2 us
    pallas_call x1, Pallas kernels, per_device(): call(rest_kernel, [out, out, rows(256, F32), rows(192)], [stat], flops=1...  2.68 us
    pallas_call x1, Pallas kernels, per_device(): call(local_kernel, [out, out, ((128, D), BF), ((64, D), BF), ((32, D), BF...  1.6 us
    pallas_call x1, Pallas kernels, per_device(): key_grad, value_grad = call(final_kernel, [out, out])(acc, near, got)  1.15 us
    concatenate x1, other arithmetic, per_device(): jnp.concatenate([key_rows, value_rows], axis=1)  1.08 us
  transfers between devices with their start and end apart: 14, of which 7 were waited for; matrix products, arithmetic and copies ran while one was open for 2% of the time, Pallas kernels for 14%

profile of v3, /device:TPU:11, one launch (start us, length us, event | category | flops | bytes accessed | tf_op | source)
XLA Modules:
  0.0 50.5 jit_solution(5378922521918310845)
XLA Ops:
  0.6 0.8 %collective-permute-start = (bf16[256,512]{1,0:T(8,128)(2,1)}, bf16[256,512]{1,0:T(8,128)(2,1)S(1)}, u32[]{:S(2)}, u32[]{:S(2)}) collective-permute-start(bf16[256,512]{1,0:T(8,128)(2,1)} %param.5), channel_id=1, source_target_pairs={{0,4},{8,12},{16,20},{24,28},{32,36},{40,44},{48,52},{56,60},{64,6... | collective-permute-start | bytes 786440 | tf_op jit(solution)/shard_map/ppermute | solution.py:469
  1.4 0.1 collective-permute-start.1
  1.5 1.1 %pad_maximum_fusion.raw = bf16[256,1024]{1,0:T(8,128)(2,1)S(1)} fusion(bf16[256,512]{1,0:T(8,128)(2,1)} %param.6, bf16[256,512]{1,0:T(8,128)(2,1)} %param.5), kind=kLoop, calls=%fused_computation | loop fusion | flops 1048576 | bytes 1048576 | tf_op jit(solution)/shard_map/concatenate | solution.py:482
  2.6 0.3 shard_map.75
  2.9 0.2 collective-permute-done.1.vs
  3.1 0.4 shard_map.76
  3.5 8.1 %collective-permute-start.3 = (bf16[64,1024]{1,0:T(8,128)(2,1)S(1)}, bf16[64,1024]{1,0:T(8,128)(2,1)S(1)}, u32[]{:S(2)}, u32[]{:S(2)}) collective-permute-start(bf16[64,1024]{1,0:T(8,128)(2,1)S(1)} %get-tuple-element.85), channel_id=1, source_target_pairs={{0,20},{8,28},{16,36},{24,44},{32,52},{40,60},{48,68},{56,76},{64,... | collective-permute-start | bytes 393224 | tf_op jit(solution)/shard_map/ppermute | solution.py:469
  11.6 1.9 %collective-permute-start.2 = (bf16[256,1024]{1,0:T(8,128)(2,1)S(1)}, bf16[256,1024]{1,0:T(8,128)(2,1)S(1)}, u32[]{:S(2)}, u32[]{:S(2)}) collective-permute-start(bf16[256,1024]{1,0:T(8,128)(2,1)S(1)} %get-tuple-element.83), channel_id=1, source_target_pairs={{4,8},{12,16},{20,24},{28,32},{36,40},{44,48},{52,56},{60,64},{68,... | collective-permute-start | bytes 1572872 | tf_op jit(solution)/shard_map/ppermute | solution.py:469
  13.5 1.6 %shard_map.77 = (bf16[256,512]{1,0:T(8,128)(2,1)S(1)}, bf16[256,512]{1,0:T(8,128)(2,1)S(1)}, bf16[128,512]{1,0:T(8,128)(2,1)S(1)}, bf16[64,512]{1,0:T(8,128)(2,1...) custom-call(bf16[256,512]{1,0:T(8,128)(2,1)S(1)} %copy-done, ...), custom_call_target="tpu_custom_call" | custom-call | flops 8589934592 | bytes 1048576 | tf_op jit(solution)/shard_map/pallas_call | solution.py:489
  15.2 3.6 %collective-permute-start.5 = (bf16[64,1024]{1,0:T(8,128)(2,1)S(1)}, bf16[64,1024]{1,0:T(8,128)(2,1)S(1)}, u32[]{:S(2)}, u32[]{:S(2)}) collective-permute-start(bf16[64,1024]{1,0:T(8,128)(2,1)S(1)} %shard_map.78), channel_id=1, source_target_pairs={{4,8},{20,24},{36,40},{52,56},{68,72},{84,88},{100,104},{116,120},... | collective-permute-start | bytes 393224 | tf_op jit(solution)/shard_map/ppermute | solution.py:469
  18.8 0.1 collective-permute-start.4
  18.9 4.6 %collective-permute-done.5.r3 = bf16[64,1024]{1,0:T(8,128)(2,1)S(1)} collective-permute-done((bf16[64,1024]{1,0:T(8,128)(2,1)S(1)}, bf16[64,1024]{1,0:T(8,128)(2,1)S(1)}, u32[]{:S(2)}, u32[]{:S(2)}) %collective-permute-start.5) | collective-permute-done | bytes 131104 | tf_op jit(solution)/shard_map/ppermute | solution.py:469
  23.5 1.3 %collective-permute-done.6.got3 = bf16[64,1024]{1,0:T(8,128)(2,1)S(1)} collective-permute-done((bf16[64,1024]{1,0:T(8,128)(2,1)S(1)}, bf16[64,1024]{1,0:T(8,128)(2,1)S(1)}, u32[]{:S(2)}, u32[]{:S(2)}) %collective-permute-start.6) | collective-permute-done | bytes 131104 | tf_op jit(solution)/shard_map/ppermute | solution.py:469
  24.8 0.6 %shard_map.79 = (bf16[256,1024]{1,0:T(8,128)(2,1)S(1)}, bf16[4,32,256]{2,1,0:T(8,128)(2,1)S(1)}, f32[4,32,128]{2,1,0:T(8,128)S(1)}, f32[4,256,128]{2,1,0:T(8,128...) custom-call(bf16[32,512]{1,0:T(8,128)(2,1)S(1)} %get-tuple-element.84.q3, ...), custom_call_target="tpu_custom_call" | custom-call | flops 268435456 | bytes 1048576 | tf_op jit(solution)/shard_map/pallas_call | solution.py:500
  25.4 0.1 shard_map.80
  25.6 0.2 collective-permute-start.7
  25.8 0.8 %shard_map.81 = (f32[4,256,128]{2,1,0:T(8,128)S(1)}, f32[4,256,128]{2,1,0:T(8,128)S(1)}, f32[4,256,128]{2,1,0:T(8,128)S(1)}, bf16[4,128,128]{2,1,0:T(8,128)(2,1)...) custom-call(bf16[256,512]{1,0:T(8,128)(2,1)S(1)} %get-tuple-element.74.q0, ...), custom_call_target="tpu_custom_call" | custom-call | flops 1073741824 | bytes 1048576 | tf_op jit(solution)/shard_map/pallas_call | solution.py:507
  26.6 0.6 %collective-permute-done.7.got = bf16[128,1024]{1,0:T(8,128)(2,1)S(1)} collective-permute-done((bf16[128,1024]{1,0:T(8,128)(2,1)S(1)}, bf16[128,1024]{1,0:T(8,128)(2,1)S(1)}, u32[]{:S(2)}, u32[]{:S(2)}) %collective-permute-start.7) | collective-permute-done | bytes 262176 | tf_op jit(solution)/shard_map/ppermute | solution.py:469
  27.2 0.6 %shard_map.82 = (bf16[256,1024]{1,0:T(8,128)(2,1)S(1)}, bf16[4,64,256]{2,1,0:T(8,128)(2,1)S(1)}, f32[4,64,128]{2,1,0:T(8,128)S(1)}, f32[4,256,128]{2,1,0:T(8,128...) custom-call(bf16[64,512]{1,0:T(8,128)(2,1)S(1)} %get-tuple-element.82.q2, ...), custom_call_target="tpu_custom_call" | custom-call | flops 268435456 | bytes 1048576 | tf_op jit(solution)/shard_map/pallas_call | solution.py:513
  27.8 1.0 %shard_map.83 = (bf16[256,512]{1,0:T(8,128)(2,1)S(1)}, f32[4,256,128]{2,1,0:T(8,128)S(1)}, f32[4,256,128]{2,1,0:T(8,128)S(1)}, f32[4,64,128]{2,1,0:T(8,128)S(1)}...) custom-call(bf16[64,512]{1,0:T(8,128)(2,1)S(1)} %get-tuple-element.8, ...), custom_call_target="tpu_custom_call" | custom-call | tf_op jit(solution)/shard_map/pallas_call | solution.py:518
  28.8 0.2 collective-permute-start.8
  29.0 0.6 %shard_map.84 = (f32[4,128,128]{2,1,0:T(8,128)S(1)}, f32[4,128,128]{2,1,0:T(8,128)S(1)}, f32[128,1024]{1,0:T(8,128)S(1)}, f32[128,1024]{1,0:T(8,128)S(1)}) custom-call(bf16[256,512]{1,0:T(8,128)(2,1)S(1)} %get-tuple-element.74.q0, bf16[128,512]{1,0:T(8,128)(2,1)S(1)} %get-tuple-element.75.q1, bf16[256,512]{1,0:T(8,128)(2,1)S(1)} %get-tuple-element.76.g_ref, ...), custom_call_target="tpu_custom_call" | custom-call | flops 1073741824 | bytes 1048576 | tf_op jit(solution)/shard_map/pallas_call | solution.py:523
  29.6 1.1 %collective-permute-done.8.got = bf16[224,1024]{1,0:T(8,128)(2,1)S(1)} collective-permute-done((bf16[224,1024]{1,0:T(8,128)(2,1)S(1)}, bf16[224,1024]{1,0:T(8,128)(2,1)S(1)}, u32[]{:S(2)}, u32[]{:S(2)}) %collective-permute-start.8) | collective-permute-done | bytes 458784 | tf_op jit(solution)/shard_map/ppermute | solution.py:469
  30.7 0.2 shard_map.85
  30.9 2.5 %collective-permute-start.9 = (bf16[256,1024]{1,0:T(8,128)(2,1)S(1)}, bf16[256,1024]{1,0:T(8,128)(2,1)S(1)}, u32[]{:S(2)}, u32[]{:S(2)}) collective-permute-start(bf16[256,1024]{1,0:T(8,128)(2,1)S(1)} %get-tuple-element.123.after), channel_id=1, source_target_pairs={{4,8},{12,16},{20,24},{28,32},{36,40},{44,48},{52,56},{60,64},{68,... | collective-permute-start | bytes 1572872 | tf_op jit(solution)/shard_map/ppermute | solution.py:469
  33.4 4.0 %collective-permute-start.11 = (bf16[32,1024]{1,0:T(8,128)(2,1)S(1)}, bf16[32,1024]{1,0:T(8,128)(2,1)S(1)}, u32[]{:S(2)}, u32[]{:S(2)}) collective-permute-start(bf16[32,1024]{1,0:T(8,128)(2,1)S(1)} %get-tuple-element.128), channel_id=1, source_target_pairs={{0,24},{4,28},{16,40},{20,44},{32,56},{36,60},{48,72},{52,76},{64,... | collective-permute-start | bytes 196616 | tf_op jit(solution)/shard_map/ppermute | solution.py:469
  37.5 5.4 %collective-permute-start.10 = (bf16[64,1024]{1,0:T(8,128)(2,1)S(1)}, bf16[64,1024]{1,0:T(8,128)(2,1)S(1)}, u32[]{:S(2)}, u32[]{:S(2)}) collective-permute-start(bf16[64,1024]{1,0:T(8,128)(2,1)S(1)} %get-tuple-element.127), channel_id=1, source_target_pairs={{0,20},{8,28},{16,36},{24,44},{32,52},{40,60},{48,68},{56,76},{64,... | collective-permute-start | bytes 393224 | tf_op jit(solution)/shard_map/ppermute | solution.py:469
  42.9 2.7 %shard_map.86 = (bf16[256,512]{1,0:T(8,128)(2,1)}, bf16[256,512]{1,0:T(8,128)(2,1)}, f32[256,1024]{1,0:T(8,128)S(1)}, bf16[192,1024]{1,0:T(8,128)(2,1)S(1)}) custom-call(bf16[256,512]{1,0:T(8,128)(2,1)S(1)} %get-tuple-element.74.q0, bf16[128,512]{1,0:T(8,128)(2,1)S(1)} %get-tuple-element.75.q1, bf16[256,512]{1,0:T(8,128)(2,1)S(1)} %get-tuple-element.76.g_ref, ...), custom_call_target="tpu_custom_call" | custom-call | flops 2147483648 | bytes 1048576 | tf_op jit(solution)/shard_map/pallas_call | solution.py:530
  45.6 2.0 %collective-permute-done.10.r2 = bf16[64,1024]{1,0:T(8,128)(2,1)S(1)} collective-permute-done((bf16[64,1024]{1,0:T(8,128)(2,1)S(1)}, bf16[64,1024]{1,0:T(8,128)(2,1)S(1)}, u32[]{:S(2)}, u32[]{:S(2)}) %collective-permute-start.10) | collective-permute-done | bytes 131104 | tf_op jit(solution)/shard_map/ppermute | solution.py:469
  47.6 0.3 shard_map.87
  48.1 1.3 %collective-permute-done.13.got = bf16[64,1024]{1,0:T(8,128)(2,1)S(1)} collective-permute-done((bf16[64,1024]{1,0:T(8,128)(2,1)S(1)}, bf16[64,1024]{1,0:T(8,128)(2,1)S(1)}, u32[]{:S(2)}, u32[]{:S(2)}) %collective-permute-start.13) | collective-permute-done | bytes 131104 | tf_op jit(solution)/shard_map/ppermute | solution.py:469
  49.4 1.2 %shard_map.88 = (bf16[256,512]{1,0:T(8,128)(2,1)}, bf16[256,512]{1,0:T(8,128)(2,1)}) custom-call(f32[256,1024]{1,0:T(8,128)S(1)} %get-tuple-element.129.acc, bf16[192,1024]{1,0:T(8,128)(2,1)S(1)} %collective-permute-done.12.near, bf16[64,1024]{1,0:T(8,128)(2,1)S(1)} %collective-permute-done.13.got), custom_call_target="tpu_custom_call" | custom-call | tf_op jit(solution)/shard_map/pallas_call | solution.py:540
  (15 shorter events, 0.1 us)
Async XLA Ops:
  0.6 2.3 %collective-permute-start = (bf16[256,512]{1,0:T(8,128)(2,1)}, bf16[256,512]{1,0:T(8,128)(2,1)S(1)}, u32[]{:S(2)}, u32[]{:S(2)}) collective-permute-start(bf16[256,512]{1,0:T(8,128)(2,1)} %param.5), channel_id=1, source_target_pairs={{0,4},{8,12},{16,20},{24,28},{32,36},{40,44},{48,52},{56,60},{64,6... | collective-permute-start | bytes 786440 | tf_op jit(solution)/shard_map/ppermute | solution.py:469
  1.4 1.7 %collective-permute-start.1 = (bf16[256,512]{1,0:T(8,128)(2,1)}, bf16[256,512]{1,0:T(8,128)(2,1)S(1)}, u32[]{:S(2)}, u32[]{:S(2)}) collective-permute-start(bf16[256,512]{1,0:T(8,128)(2,1)} %param.6), channel_id=1, source_target_pairs={{0,4},{8,12},{16,20},{24,28},{32,36},{40,44},{48,52},{56,60},{64,6... | collective-permute-start | bytes 786440 | tf_op jit(solution)/shard_map/ppermute | solution.py:469
  3.1 10.4 %copy-start = (bf16[256,512]{1,0:T(8,128)(2,1)S(1)}, bf16[256,512]{1,0:T(8,128)(2,1)}, u32[]{:S(2)}) copy-start(bf16[256,512]{1,0:T(8,128)(2,1)} %q_ref.1) | copy-start | bytes 786436
  3.1 10.4 %copy-start.1 = (bf16[256,512]{1,0:T(8,128)(2,1)S(1)}, bf16[256,512]{1,0:T(8,128)(2,1)}, u32[]{:S(2)}) copy-start(bf16[256,512]{1,0:T(8,128)(2,1)} %g_ref.1) | copy-start | bytes 786436
  3.5 11.6 %collective-permute-start.3 = (bf16[64,1024]{1,0:T(8,128)(2,1)S(1)}, bf16[64,1024]{1,0:T(8,128)(2,1)S(1)}, u32[]{:S(2)}, u32[]{:S(2)}) collective-permute-start(bf16[64,1024]{1,0:T(8,128)(2,1)S(1)} %get-tuple-element.85), channel_id=1, source_target_pairs={{0,20},{8,28},{16,36},{24,44},{32,52},{40,60},{48,68},{56,76},{64,... | collective-permute-start | bytes 393224 | tf_op jit(solution)/shard_map/ppermute | solution.py:469
  11.6 13.9 %collective-permute-start.2 = (bf16[256,1024]{1,0:T(8,128)(2,1)S(1)}, bf16[256,1024]{1,0:T(8,128)(2,1)S(1)}, u32[]{:S(2)}, u32[]{:S(2)}) collective-permute-start(bf16[256,1024]{1,0:T(8,128)(2,1)S(1)} %get-tuple-element.83), channel_id=1, source_target_pairs={{4,8},{12,16},{20,24},{28,32},{36,40},{44,48},{52,56},{60,64},{68,... | collective-permute-start | bytes 1572872 | tf_op jit(solution)/shard_map/ppermute | solution.py:469
  15.2 8.3 %collective-permute-start.5 = (bf16[64,1024]{1,0:T(8,128)(2,1)S(1)}, bf16[64,1024]{1,0:T(8,128)(2,1)S(1)}, u32[]{:S(2)}, u32[]{:S(2)}) collective-permute-start(bf16[64,1024]{1,0:T(8,128)(2,1)S(1)} %shard_map.78), channel_id=1, source_target_pairs={{4,8},{20,24},{36,40},{52,56},{68,72},{84,88},{100,104},{116,120},... | collective-permute-start | bytes 393224 | tf_op jit(solution)/shard_map/ppermute | solution.py:469
  18.8 4.7 %collective-permute-start.4 = (bf16[64,1024]{1,0:T(8,128)(2,1)S(1)}, bf16[64,1024]{1,0:T(8,128)(2,1)S(1)}, u32[]{:S(2)}, u32[]{:S(2)}) collective-permute-start(bf16[64,1024]{1,0:T(8,128)(2,1)S(1)} %shard_map.78), channel_id=1, source_target_pairs={{0,4},{8,12},{16,20},{24,28},{32,36},{40,44},{48,52},{56,60},{64,6... | collective-permute-start | bytes 393224 | tf_op jit(solution)/shard_map/ppermute | solution.py:469
  23.5 1.3 %collective-permute-start.6 = (bf16[64,1024]{1,0:T(8,128)(2,1)S(1)}, bf16[64,1024]{1,0:T(8,128)(2,1)S(1)}, u32[]{:S(2)}, u32[]{:S(2)}) collective-permute-start(bf16[64,1024]{1,0:T(8,128)(2,1)S(1)} %collective-permute-done.5.r3), channel_id=1, source_target_pairs={{0,4},{8,12},{16,20},{24,28},{32,36},{40,44},{48,52},{56,60},{64,6... | collective-permute-start | bytes 393224 | tf_op jit(solution)/shard_map/ppermute | solution.py:469
  25.6 1.6 %collective-permute-start.7 = (bf16[128,1024]{1,0:T(8,128)(2,1)S(1)}, bf16[128,1024]{1,0:T(8,128)(2,1)S(1)}, u32[]{:S(2)}, u32[]{:S(2)}) collective-permute-start(bf16[128,1024]{1,0:T(8,128)(2,1)S(1)} %get-tuple-element.90), channel_id=1, source_target_pairs={{0,4},{8,12},{16,20},{24,28},{32,36},{40,44},{48,52},{56,60},{64,6... | collective-permute-start | bytes 786440 | tf_op jit(solution)/shard_map/ppermute | solution.py:469
  28.8 1.9 %collective-permute-start.8 = (bf16[224,1024]{1,0:T(8,128)(2,1)S(1)}, bf16[224,1024]{1,0:T(8,128)(2,1)S(1)}, u32[]{:S(2)}, u32[]{:S(2)}) collective-permute-start(bf16[224,1024]{1,0:T(8,128)(2,1)S(1)} %get-tuple-element.122), channel_id=1, source_target_pairs={{0,4},{8,12},{16,20},{24,28},{32,36},{40,44},{48,52},{56,60},{64,6... | collective-permute-start | bytes 1376264 | tf_op jit(solution)/shard_map/ppermute | solution.py:469
  30.9 16.7 %collective-permute-start.9 = (bf16[256,1024]{1,0:T(8,128)(2,1)S(1)}, bf16[256,1024]{1,0:T(8,128)(2,1)S(1)}, u32[]{:S(2)}, u32[]{:S(2)}) collective-permute-start(bf16[256,1024]{1,0:T(8,128)(2,1)S(1)} %get-tuple-element.123.after), channel_id=1, source_target_pairs={{4,8},{12,16},{20,24},{28,32},{36,40},{44,48},{52,56},{60,64},{68,... | collective-permute-start | bytes 1572872 | tf_op jit(solution)/shard_map/ppermute | solution.py:469
  33.4 12.2 %collective-permute-start.11 = (bf16[32,1024]{1,0:T(8,128)(2,1)S(1)}, bf16[32,1024]{1,0:T(8,128)(2,1)S(1)}, u32[]{:S(2)}, u32[]{:S(2)}) collective-permute-start(bf16[32,1024]{1,0:T(8,128)(2,1)S(1)} %get-tuple-element.128), channel_id=1, source_target_pairs={{0,24},{4,28},{16,40},{20,44},{32,56},{36,60},{48,72},{52,76},{64,... | collective-permute-start | bytes 196616 | tf_op jit(solution)/shard_map/ppermute | solution.py:469
  37.5 10.1 %collective-permute-start.10 = (bf16[64,1024]{1,0:T(8,128)(2,1)S(1)}, bf16[64,1024]{1,0:T(8,128)(2,1)S(1)}, u32[]{:S(2)}, u32[]{:S(2)}) collective-permute-start(bf16[64,1024]{1,0:T(8,128)(2,1)S(1)} %get-tuple-element.127), channel_id=1, source_target_pairs={{0,20},{8,28},{16,36},{24,44},{32,52},{40,60},{48,68},{56,76},{64,... | collective-permute-start | bytes 393224 | tf_op jit(solution)/shard_map/ppermute | solution.py:469
  45.6 2.5 %collective-permute-start.12 = (bf16[192,1024]{1,0:T(8,128)(2,1)S(1)}, bf16[192,1024]{1,0:T(8,128)(2,1)S(1)}, u32[]{:S(2)}, u32[]{:S(2)}) collective-permute-start(bf16[192,1024]{1,0:T(8,128)(2,1)S(1)} %get-tuple-element.130), channel_id=1, source_target_pairs={{0,4},{8,12},{16,20},{24,28},{32,36},{40,44},{48,52},{56,60},{64,6... | collective-permute-start | bytes 1179656 | tf_op jit(solution)/shard_map/ppermute | solution.py:469
  48.0 1.4 %collective-permute-start.13 = (bf16[64,1024]{1,0:T(8,128)(2,1)S(1)}, bf16[64,1024]{1,0:T(8,128)(2,1)S(1)}, u32[]{:S(2)}, u32[]{:S(2)}) collective-permute-start(bf16[64,1024]{1,0:T(8,128)(2,1)S(1)} %get-tuple-element.131), channel_id=1, source_target_pairs={{0,4},{8,12},{16,20},{24,28},{32,36},{40,44},{48,52},{56,60},{64,6... | collective-permute-start | bytes 393224 | tf_op jit(solution)/shard_map/ppermute | solution.py:469

commit v4 on v1

--- a/solution.py
+++ b/solution.py
@@ -86,8 +86,9 @@
     return jnp.broadcast_to(value, (value.shape[0], HEAD))
 
 
-def wide(value, count):
-    return value if count == 1 else jnp.concatenate([value] * count, axis=1)
+def wide(value, lanes):
+    pieces = [value[:, : min(HEAD, lanes - i)] for i in range(0, lanes, HEAD)]
+    return pieces[0] if len(pieces) == 1 else jnp.concatenate(pieces, axis=1)
 
 
 def penalty(ok):
@@ -119,7 +120,7 @@
     inners = [nt(grad, v) for _, _, v, _, grad, _ in units]
     dvs = [tn(eb, grad) for _, _, _, eb, grad, _ in units]
     dscores = [
-        (eb.astype(F32) * (inner - wide(drift, eb.shape[1] // HEAD))).astype(BF)
+        (eb.astype(F32) * (inner - wide(drift, eb.shape[1]))).astype(BF)
         for inner, (_, _, _, eb, _, drift) in zip(inners, units)
     ]
     dqs = [nn(dscore, k) * SCALE for dscore, (_, k, _, _, _, _) in zip(dscores, units)]
@@ -248,59 +249,47 @@
             )
 
 
-def second_kernel(q2, r1, got, top, zsum, ysum, win, e2, m2, top_out, z_out, y_out):
-    core, chip = place()
-    is0 = core == 0
-    win[:64] = r1[192:]
-    win[64:192] = got[...]
-    win[192:] = jnp.zeros((64, FULL), BF)
-    lane = lax.broadcasted_iota(jnp.int32, (1, 256), 1)
-    left_ok, right_ok = chip >= 1, chip <= 30
-    own_bad = penalty(jnp.where(is0, left_ok, right_ok))
-    sib_bad = penalty(jnp.where(is0, right_ok, left_ok))
-    bias = jnp.where(lane < 64, own_bad, jnp.where(lane < 192, sib_bad, NEG))
-    results = soft([(q2[:, head(h)], win[:, head(h)], win[:, head(HEADS + h)], bias) for h in range(HEADS)])
-    for h in range(HEADS):
-        e2[h], m2[h], d, n = results[h]
-        for c in range(2):
-            r, a = slice(c * 128, (c + 1) * 128), slice(c * 32, (c + 1) * 32)
-            top_out[h, r], z_out[h, r], y_out[h, r], _ = merge(
-                top[h, r], zsum[h, r], ysum[h, r], [(m2[h, a], d[a], n[a], 2)]
-            )
-
-
 def far_kernel(
-    q2, q3, g_ref, top, zsum, ysum, w2, e2, m2, r2, r3, got,
+    q2, q3, g_ref, top, zsum, ysum, r1, got2, r2, r3, got3,
     att, best_out, inv_out, delta_out, dq2, dq3, own2, own3, cross3, send,
-    w3,
+    w2, w3,
 ):
     core, chip = place()
     is0 = core == 0
+    holder = lax.rem(core + chip, 2) == 1
+    w2[:128] = got2[...]
+    w2[128:] = r1[192:]
     w3[:64] = r2[...]
-    w3[64:128] = got[:64]
-    w3[128:192] = jnp.where(lax.rem(core + chip, 2) == 1, r3[...], got[64:])
-    w3[192:] = jnp.zeros((64, FULL), BF)
-    holder = lax.rem(core + chip, 2) == 1
+    w3[64:128] = got3[:64]
+    w3[128:] = jnp.where(holder, r3[...], got3[64:])
+    left_ok, right_ok = chip >= 1, chip <= 30
     low2, high2 = chip >= 2, chip <= 29
     even = lax.rem(chip, 2) == 0
+    lane = lax.broadcasted_iota(jnp.int32, (1, 192), 1)
+    own_bad = penalty(jnp.where(is0, left_ok, right_ok))
+    sib_bad = penalty(jnp.where(is0, right_ok, left_ok))
+    bias2 = jnp.where(lane < 128, sib_bad, own_bad)
     cross_bad = penalty(jnp.where(even, chip <= 28, chip >= 3))
-    lane = lax.broadcasted_iota(jnp.int32, (1, 256), 1)
     own_bad = penalty(jnp.where(is0, high2, low2))
     sib_bad = penalty(jnp.where(is0, low2, high2))
-    bias3 = jnp.where(
-        lane < 64, own_bad, jnp.where(lane < 128, sib_bad, jnp.where(lane < 192, cross_bad, NEG))
-    )
-    third = soft([(q3[:, head(h)], w3[:, head(h)], w3[:, head(HEADS + h)], bias3) for h in range(HEADS)])
+    bias3 = jnp.where(lane < 64, own_bad, jnp.where(lane < 128, sib_bad, cross_bad))
     units = []
     for h in range(HEADS):
         kl, vl = head(h), head(HEADS + h)
-        e3, m3, d3, n3 = third[h]
+        units.append((q2[:, kl], w2[:, kl], w2[:, vl], bias2))
+        units.append((q3[:, kl], w3[:, kl], w3[:, vl], bias3))
+    results = soft(units)
+    units = []
+    for h in range(HEADS):
+        kl, vl = head(h), head(HEADS + h)
+        (e2, m2, d2, n2), (e3, m3, d3, n3) = results[2 * h : 2 * h + 2]
         grads = ([], [])
         drifts = ([], [])
         for c in range(2):
             r = slice(c * 128, (c + 1) * 128)
             a, b = slice(c * 32, (c + 1) * 32), slice(c * 16, (c + 1) * 16)
-            best, z, y, factors = merge(top[h, r], zsum[h, r], ysum[h, r], [(m3[b], d3[b], n3[b], 3)])
+            pieces = [(m2[a], d2[a], n2[a], 2), (m3[b], d3[b], n3[b], 3)]
+            best, z, y, factors = merge(top[h, r], zsum[h, r], ysum[h, r], pieces)
             inv = 1.0 / z
             y = y * inv
             att[r, kl] = y.astype(BF)
@@ -309,12 +298,11 @@
             best_out[h, r] = best
             inv_out[h, r] = inv
             delta_out[h, r] = delta
-            factors = [4.0 * jnp.exp2(expand(m2[h, a], 2) - best)] + factors
             for i in range(2):
                 share = factors[i] * inv
                 grads[i].append(fold(share * g, i + 2))
                 drifts[i].append(fold(share * delta, i + 2))
-        for i, (q, w, e) in enumerate(((q2, w2, e2[h]), (q3, w3, e3))):
+        for i, (q, w, e) in enumerate(((q2, w2, e2), (q3, w3, e3))):
             grad = jnp.concatenate(grads[i], axis=0).astype(BF)
             units.append((q[:, kl], w[:, kl], w[:, vl], e, grad, jnp.concatenate(drifts[i], axis=0)))
     results = backward(units)
@@ -324,13 +312,13 @@
             (dq2, dq3)[i][h] = dq
             for lanes, value in ((head(h), dk), (head(HEADS + h), dv)):
                 if i == 0:
-                    own2[:, lanes] = value[:64]
-                    send[:128, lanes] = value[64:192].astype(BF)
+                    send[:128, lanes] = value[:128].astype(BF)
+                    own2[:, lanes] = value[128:]
                 else:
                     own3[:, lanes] = value[:64]
                     send[128:192, lanes] = value[64:128].astype(BF)
-                    cross3[:, lanes] = jnp.where(holder, value[128:160], value[160:192])
-                    send[192:, lanes] = jnp.where(holder, value[160:192], value[128:160]).astype(BF)
+                    cross3[:, lanes] = jnp.where(holder, value[128:160], value[160:])
+                    send[192:, lanes] = jnp.where(holder, value[160:], value[128:160]).astype(BF)
 
 
 def coarse_grad(m, best, inv, g, delta):
@@ -423,28 +411,34 @@
         acc[:, lanes] = own[:, lanes] + expand(0.5 * first) + placed(r1[:128, lanes].astype(F32), is0, 128)
 
 
-def final_kernel(acc, near, got, dk, dv):
+def final_kernel(acc, near, got, dk, dv, done, sems):
     core, _ = place()
     is0 = core == 0
     matrix = order_matrix(back=True)
+    copies = []
     for j in range(2 * HEADS):
         lanes = head(j)
         first = expand(0.5 * got[:, lanes].astype(F32)) + placed(near[128:, lanes].astype(F32), is0, 64)
         total = acc[:, lanes] + expand(0.5 * first) + placed(near[:128, lanes].astype(F32), ~is0, 128)
-        (dk if j < HEADS else dv)[:, head(j % HEADS)] = reorder(matrix, total.astype(BF))
+        done[:, lanes] = reorder(matrix, total.astype(BF))
+        target = (dk if j < HEADS else dv).at[:, head(j % HEADS)]
+        copies.append(pltpu.make_async_copy(done.at[:, lanes], target, sems.at[j]))
+        copies[-1].start()
+    for copy in copies:
+        copy.wait()
 
 
 SPACES = {"v": pltpu.VMEM, "a": pl.ANY}
 
 
-def call(kernel, outs, scratch=(), flops=0, specs=None):
+def call(kernel, outs, scratch=(), flops=0, specs=None, results=pltpu.VMEM):
     extra = {"in_specs": [pl.BlockSpec(memory_space=SPACES[s]) for s in specs]} if specs else {}
     if flops:
         extra["cost_estimate"] = pl.CostEstimate(flops=flops, bytes_accessed=1 << 20, transcendentals=0)
     return pl.pallas_call(
         kernel,
         out_shape=[jax.ShapeDtypeStruct(shape, dtype) for shape, dtype in outs],
-        out_specs=[pl.BlockSpec(memory_space=pltpu.VMEM)] * len(outs),
+        out_specs=[pl.BlockSpec(memory_space=results)] * len(outs),
         scratch_shapes=[s if not isinstance(s, tuple) else pltpu.VMEM(*s) for s in scratch],
         compiler_params=pltpu.CompilerParams(vmem_limit_bytes=VMEM_LIMIT),
         **extra,
@@ -498,16 +492,11 @@
         [heads(128), heads(128)],
         flops=1 << 30,
     )(q0, q1, r1, outer1, top, zsum, ysum)
-    w2, e2, m2, top, zsum, ysum = call(
-        second_kernel,
-        [rows(256), heads(64, BF, 256), heads(64), stat, stat, stat],
-        flops=1 << 28,
-    )(q2, r1, got2, top, zsum, ysum)
     att, best, inv, delta, dq2, dq3, own2, own3, cross3, send = call(
         far_kernel,
         [out, stat, stat, stat, heads(64), heads(32), rows(64, F32), rows(64, F32), rows(32, F32), rows(224)],
-        [rows(256)],
-    )(q2, q3, g0, top, zsum, ysum, w2, e2, m2, r2, r3, got3)
+        [rows(192), rows(192)],
+    )(q2, q3, g0, top, zsum, ysum, r1, got2, r2, r3, got3)
     got = swap(send, sibling)
     dqo0, dqo1, d0, d1 = call(
         outer_back_kernel, [heads(128), heads(128), rows(128, F32), rows(128, F32)], flops=1 << 30
@@ -526,7 +515,9 @@
     near = swap(send, sibling)
     acc, send = call(add_kernel, [rows(256, F32), rows(64)], flops=1 << 34)(acc, r1, r2, r3)
     got = swap(send, sibling)
-    key_grad, value_grad = call(final_kernel, [out, out])(acc, near, got)
+    key_grad, value_grad = call(
+        final_kernel, [out, out], [rows(256), pltpu.SemaphoreType.DMA((2 * HEADS,))], results=pl.ANY
+    )(acc, near, got)
     return attended, query_grad, key_grad, value_grad
 
 

time: 49.6 us -> 49.6 us (level)
    pallas_call x2 -> x1, Pallas kernels: 1.74 us -> 1.16 us  [per_device(): call(final_kernel, [out, out], [rows(256), pltpu.SemaphoreType.DMA((2 * H...]
  transfers between devices with their start and end apart: 13 -> 13, of which waited for: 7 -> 7; matrix products, arithmetic and copies ran while one was open for 2% -> 2% of each run, Pallas kernels for 14% -> 13%
where the time goes in v4:
time: 49.6 us; the launch traced here: 49 us
  starting transfers between devices  26.3 us (53%)
  waiting for transfers between devices  10.9 us (22%)
  Pallas kernels  9.87 us (20%)
  other arithmetic  1.08 us (2%)
  between operations  0.83 us (2%)
    ppermute x13, starting transfers between devices, swap(): return lax.ppermute(value, 'seq', pairs + [(b, a) for a, b in pairs])  26.3 us
    ppermute x13, waiting for transfers between devices, swap(): return lax.ppermute(value, 'seq', pairs + [(b, a) for a, b in pairs])  10.9 us
    pallas_call x1, Pallas kernels, per_device(): call(rest_kernel, [out, out, rows(256, F32), rows(192)], [stat], flops=1...  2.68 us
    pallas_call x1, Pallas kernels, per_device(): call(far_kernel, [out, stat, stat, stat, heads(64), heads(32), rows(64, F...  1.67 us
    pallas_call x1, Pallas kernels, per_device(): call(local_kernel, [out, out, ((128, D), BF), ((64, D), BF), ((32, D), BF...  1.6 us
    pallas_call x1, Pallas kernels, per_device(): call(final_kernel, [out, out], [rows(256), pltpu.SemaphoreType.DMA((2 * H...  1.16 us
    concatenate x1, other arithmetic, per_device(): jnp.concatenate([key_rows, value_rows], axis=1)  1.08 us
  transfers between devices with their start and end apart: 13, of which 7 were waited for; matrix products, arithmetic and copies ran while one was open for 2% of the time, Pallas kernels for 13%

profile of v4, /device:TPU:11, one launch (start us, length us, event | category | flops | bytes accessed | tf_op | source)
XLA Modules:
  0.0 49.0 jit_solution(5939710445759965734)
XLA Ops:
  0.6 0.8 %collective-permute-start = (bf16[256,512]{1,0:T(8,128)(2,1)}, bf16[256,512]{1,0:T(8,128)(2,1)S(1)}, u32[]{:S(2)}, u32[]{:S(2)}) collective-permute-start(bf16[256,512]{1,0:T(8,128)(2,1)} %param.5), channel_id=1, source_target_pairs={{0,4},{8,12},{16,20},{24,28},{32,36},{40,44},{48,52},{56,60},{64,6... | collective-permute-start | bytes 786440 | tf_op jit(solution)/shard_map/ppermute | solution.py:457
  1.4 0.1 collective-permute-start.1
  1.5 1.1 %pad_maximum_fusion.raw = bf16[256,1024]{1,0:T(8,128)(2,1)S(1)} fusion(bf16[256,512]{1,0:T(8,128)(2,1)} %param.6, bf16[256,512]{1,0:T(8,128)(2,1)} %param.5), kind=kLoop, calls=%fused_computation | loop fusion | flops 1048576 | bytes 1048576 | tf_op jit(solution)/shard_map/concatenate | solution.py:470
  2.6 0.3 shard_map.75
  2.9 0.2 collective-permute-done.1.vs
  3.1 0.4 shard_map.76
  3.5 8.1 %collective-permute-start.3 = (bf16[64,1024]{1,0:T(8,128)(2,1)S(1)}, bf16[64,1024]{1,0:T(8,128)(2,1)S(1)}, u32[]{:S(2)}, u32[]{:S(2)}) collective-permute-start(bf16[64,1024]{1,0:T(8,128)(2,1)S(1)} %get-tuple-element.74), channel_id=1, source_target_pairs={{0,20},{8,28},{16,36},{24,44},{32,52},{40,60},{48,68},{56,76},{64,... | collective-permute-start | bytes 393224 | tf_op jit(solution)/shard_map/ppermute | solution.py:457
  11.6 1.9 %collective-permute-start.2 = (bf16[256,1024]{1,0:T(8,128)(2,1)S(1)}, bf16[256,1024]{1,0:T(8,128)(2,1)S(1)}, u32[]{:S(2)}, u32[]{:S(2)}) collective-permute-start(bf16[256,1024]{1,0:T(8,128)(2,1)S(1)} %get-tuple-element.73), channel_id=1, source_target_pairs={{4,8},{12,16},{20,24},{28,32},{36,40},{44,48},{52,56},{60,64},{68,... | collective-permute-start | bytes 1572872 | tf_op jit(solution)/shard_map/ppermute | solution.py:457
  13.5 1.4 %collective-permute-done.3.r2 = bf16[64,1024]{1,0:T(8,128)(2,1)S(1)} collective-permute-done((bf16[64,1024]{1,0:T(8,128)(2,1)S(1)}, bf16[64,1024]{1,0:T(8,128)(2,1)S(1)}, u32[]{:S(2)}, u32[]{:S(2)}) %collective-permute-start.3) | collective-permute-done | bytes 131104 | tf_op jit(solution)/shard_map/ppermute | solution.py:457
  14.9 2.3 %collective-permute-start.4 = (bf16[64,1024]{1,0:T(8,128)(2,1)S(1)}, bf16[64,1024]{1,0:T(8,128)(2,1)S(1)}, u32[]{:S(2)}, u32[]{:S(2)}) collective-permute-start(bf16[64,1024]{1,0:T(8,128)(2,1)S(1)} %collective-permute-done.3.r2), channel_id=1, source_target_pairs={{4,8},{20,24},{36,40},{52,56},{68,72},{84,88},{100,104},{116,120},... | collective-permute-start | bytes 393224 | tf_op jit(solution)/shard_map/ppermute | solution.py:457
  17.2 1.6 %shard_map.77 = (bf16[256,512]{1,0:T(8,128)(2,1)S(1)}, bf16[256,512]{1,0:T(8,128)(2,1)S(1)}, bf16[128,512]{1,0:T(8,128)(2,1)S(1)}, bf16[64,512]{1,0:T(8,128)(2,1...) custom-call(bf16[256,512]{1,0:T(8,128)(2,1)S(1)} %copy-done, ...), custom_call_target="tpu_custom_call" | custom-call | flops 8589934592 | bytes 1048576 | tf_op jit(solution)/shard_map/pallas_call | solution.py:478
  18.8 4.7 %collective-permute-done.4.r3 = bf16[64,1024]{1,0:T(8,128)(2,1)S(1)} collective-permute-done((bf16[64,1024]{1,0:T(8,128)(2,1)S(1)}, bf16[64,1024]{1,0:T(8,128)(2,1)S(1)}, u32[]{:S(2)}, u32[]{:S(2)}) %collective-permute-start.4) | collective-permute-done | bytes 131104 | tf_op jit(solution)/shard_map/ppermute | solution.py:457
  23.5 0.1 collective-permute-start.6
  23.6 0.0 collective-permute-done.2.r1
  23.6 0.1 shard_map.79
  23.8 0.6 %collective-permute-start.5 = (bf16[128,1024]{1,0:T(8,128)(2,1)S(1)}, bf16[128,1024]{1,0:T(8,128)(2,1)S(1)}, u32[]{:S(2)}, u32[]{:S(2)}) collective-permute-start(bf16[128,1024]{1,0:T(8,128)(2,1)S(1)} %get-tuple-element.82), channel_id=1, source_target_pairs={{0,4},{8,12},{16,20},{24,28},{32,36},{40,44},{48,52},{56,60},{64,6... | collective-permute-start | bytes 786440 | tf_op jit(solution)/shard_map/ppermute | solution.py:457
  24.3 0.8 %shard_map.80 = (f32[4,256,128]{2,1,0:T(8,128)S(1)}, f32[4,256,128]{2,1,0:T(8,128)S(1)}, f32[4,256,128]{2,1,0:T(8,128)S(1)}, bf16[4,128,128]{2,1,0:T(8,128)(2,1)...) custom-call(bf16[256,512]{1,0:T(8,128)(2,1)S(1)} %get-tuple-element.63.q0, ...), custom_call_target="tpu_custom_call" | custom-call | flops 1073741824 | bytes 1048576 | tf_op jit(solution)/shard_map/pallas_call | solution.py:489
  25.2 0.4 collective-permute-done.5.got2
  25.5 1.7 %shard_map.81 = (bf16[256,512]{1,0:T(8,128)(2,1)S(1)}, f32[4,256,128]{2,1,0:T(8,128)S(1)}, f32[4,256,128]{2,1,0:T(8,128)S(1)}, f32[4,256,128]{2,1,0:T(8,128)S(1)...) custom-call(bf16[64,512]{1,0:T(8,128)(2,1)S(1)} %get-tuple-element.7, ...), custom_call_target="tpu_custom_call" | custom-call | tf_op jit(solution)/shard_map/pallas_call | solution.py:495
  27.2 0.5 collective-permute-start.7
  27.7 0.6 %shard_map.82 = (f32[4,128,128]{2,1,0:T(8,128)S(1)}, f32[4,128,128]{2,1,0:T(8,128)S(1)}, f32[128,1024]{1,0:T(8,128)S(1)}, f32[128,1024]{1,0:T(8,128)S(1)}) custom-call(bf16[256,512]{1,0:T(8,128)(2,1)S(1)} %get-tuple-element.63.q0, bf16[128,512]{1,0:T(8,128)(2,1)S(1)} %get-tuple-element.64.q1, bf16[256,512]{1,0:T(8,128)(2,1)S(1)} %get-tuple-element.65.g_ref, ...), custom_call_target="tpu_custom_call" | custom-call | flops 1073741824 | bytes 1048576 | tf_op jit(solution)/shard_map/pallas_call | solution.py:501
  28.2 0.9 %collective-permute-done.7.got = bf16[224,1024]{1,0:T(8,128)(2,1)S(1)} collective-permute-done((bf16[224,1024]{1,0:T(8,128)(2,1)S(1)}, bf16[224,1024]{1,0:T(8,128)(2,1)S(1)}, u32[]{:S(2)}, u32[]{:S(2)}) %collective-permute-start.7) | collective-permute-done | bytes 458784 | tf_op jit(solution)/shard_map/ppermute | solution.py:457
  29.1 0.2 shard_map.83
  29.3 2.5 %collective-permute-start.8 = (bf16[256,1024]{1,0:T(8,128)(2,1)S(1)}, bf16[256,1024]{1,0:T(8,128)(2,1)S(1)}, u32[]{:S(2)}, u32[]{:S(2)}) collective-permute-start(bf16[256,1024]{1,0:T(8,128)(2,1)S(1)} %get-tuple-element.101.after), channel_id=1, source_target_pairs={{4,8},{12,16},{20,24},{28,32},{36,40},{44,48},{52,56},{60,64},{68,... | collective-permute-start | bytes 1572872 | tf_op jit(solution)/shard_map/ppermute | solution.py:457
  31.8 4.2 %collective-permute-start.10 = (bf16[32,1024]{1,0:T(8,128)(2,1)S(1)}, bf16[32,1024]{1,0:T(8,128)(2,1)S(1)}, u32[]{:S(2)}, u32[]{:S(2)}) collective-permute-start(bf16[32,1024]{1,0:T(8,128)(2,1)S(1)} %get-tuple-element.106), channel_id=1, source_target_pairs={{0,24},{4,28},{16,40},{20,44},{32,56},{36,60},{48,72},{52,76},{64,... | collective-permute-start | bytes 196616 | tf_op jit(solution)/shard_map/ppermute | solution.py:457
  36.1 5.2 %collective-permute-start.9 = (bf16[64,1024]{1,0:T(8,128)(2,1)S(1)}, bf16[64,1024]{1,0:T(8,128)(2,1)S(1)}, u32[]{:S(2)}, u32[]{:S(2)}) collective-permute-start(bf16[64,1024]{1,0:T(8,128)(2,1)S(1)} %get-tuple-element.105), channel_id=1, source_target_pairs={{0,20},{8,28},{16,36},{24,44},{32,52},{40,60},{48,68},{56,76},{64,... | collective-permute-start | bytes 393224 | tf_op jit(solution)/shard_map/ppermute | solution.py:457
  41.3 2.7 %shard_map.84 = (bf16[256,512]{1,0:T(8,128)(2,1)}, bf16[256,512]{1,0:T(8,128)(2,1)}, f32[256,1024]{1,0:T(8,128)S(1)}, bf16[192,1024]{1,0:T(8,128)(2,1)S(1)}) custom-call(bf16[256,512]{1,0:T(8,128)(2,1)S(1)} %get-tuple-element.63.q0, bf16[128,512]{1,0:T(8,128)(2,1)S(1)} %get-tuple-element.64.q1, bf16[256,512]{1,0:T(8,128)(2,1)S(1)} %get-tuple-element.65.g_ref, ...), custom_call_target="tpu_custom_call" | custom-call | flops 2147483648 | bytes 1048576 | tf_op jit(solution)/shard_map/pallas_call | solution.py:508
  44.0 2.1 %collective-permute-done.9.r2 = bf16[64,1024]{1,0:T(8,128)(2,1)S(1)} collective-permute-done((bf16[64,1024]{1,0:T(8,128)(2,1)S(1)}, bf16[64,1024]{1,0:T(8,128)(2,1)S(1)}, u32[]{:S(2)}, u32[]{:S(2)}) %collective-permute-start.9) | collective-permute-done | bytes 131104 | tf_op jit(solution)/shard_map/ppermute | solution.py:457
  46.1 0.3 shard_map.85
  46.4 0.1 collective-permute-start.12
  46.5 1.3 %collective-permute-done.12.got = bf16[64,1024]{1,0:T(8,128)(2,1)S(1)} collective-permute-done((bf16[64,1024]{1,0:T(8,128)(2,1)S(1)}, bf16[64,1024]{1,0:T(8,128)(2,1)S(1)}, u32[]{:S(2)}, u32[]{:S(2)}) %collective-permute-start.12) | collective-permute-done | bytes 131104 | tf_op jit(solution)/shard_map/ppermute | solution.py:457
  47.8 1.2 %shard_map.86 = (bf16[256,512]{1,0:T(8,128)(2,1)}, bf16[256,512]{1,0:T(8,128)(2,1)}) custom-call(f32[256,1024]{1,0:T(8,128)S(1)} %get-tuple-element.107.acc, bf16[192,1024]{1,0:T(8,128)(2,1)S(1)} %collective-permute-done.11.near, bf16[64,1024]{1,0:T(8,128)(2,1)S(1)} %collective-permute-done.12.got), custom_call_target="tpu_custom_call" | custom-call | tf_op jit(solution)/shard_map/pallas_call | solution.py:518
  (11 shorter events, 0.0 us)
Async XLA Ops:
  0.6 2.3 %collective-permute-start = (bf16[256,512]{1,0:T(8,128)(2,1)}, bf16[256,512]{1,0:T(8,128)(2,1)S(1)}, u32[]{:S(2)}, u32[]{:S(2)}) collective-permute-start(bf16[256,512]{1,0:T(8,128)(2,1)} %param.5), channel_id=1, source_target_pairs={{0,4},{8,12},{16,20},{24,28},{32,36},{40,44},{48,52},{56,60},{64,6... | collective-permute-start | bytes 786440 | tf_op jit(solution)/shard_map/ppermute | solution.py:457
  1.4 1.7 %collective-permute-start.1 = (bf16[256,512]{1,0:T(8,128)(2,1)}, bf16[256,512]{1,0:T(8,128)(2,1)S(1)}, u32[]{:S(2)}, u32[]{:S(2)}) collective-permute-start(bf16[256,512]{1,0:T(8,128)(2,1)} %param.6), channel_id=1, source_target_pairs={{0,4},{8,12},{16,20},{24,28},{32,36},{40,44},{48,52},{56,60},{64,6... | collective-permute-start | bytes 786440 | tf_op jit(solution)/shard_map/ppermute | solution.py:457
  3.1 14.0 %copy-start = (bf16[256,512]{1,0:T(8,128)(2,1)S(1)}, bf16[256,512]{1,0:T(8,128)(2,1)}, u32[]{:S(2)}) copy-start(bf16[256,512]{1,0:T(8,128)(2,1)} %q_ref.1) | copy-start | bytes 786436
  3.1 14.0 %copy-start.1 = (bf16[256,512]{1,0:T(8,128)(2,1)S(1)}, bf16[256,512]{1,0:T(8,128)(2,1)}, u32[]{:S(2)}) copy-start(bf16[256,512]{1,0:T(8,128)(2,1)} %g_ref.1) | copy-start | bytes 786436
  3.5 11.4 %collective-permute-start.3 = (bf16[64,1024]{1,0:T(8,128)(2,1)S(1)}, bf16[64,1024]{1,0:T(8,128)(2,1)S(1)}, u32[]{:S(2)}, u32[]{:S(2)}) collective-permute-start(bf16[64,1024]{1,0:T(8,128)(2,1)S(1)} %get-tuple-element.74), channel_id=1, source_target_pairs={{0,20},{8,28},{16,36},{24,44},{32,52},{40,60},{48,68},{56,76},{64,... | collective-permute-start | bytes 393224 | tf_op jit(solution)/shard_map/ppermute | solution.py:457
  11.6 12.0 %collective-permute-start.2 = (bf16[256,1024]{1,0:T(8,128)(2,1)S(1)}, bf16[256,1024]{1,0:T(8,128)(2,1)S(1)}, u32[]{:S(2)}, u32[]{:S(2)}) collective-permute-start(bf16[256,1024]{1,0:T(8,128)(2,1)S(1)} %get-tuple-element.73), channel_id=1, source_target_pairs={{4,8},{12,16},{20,24},{28,32},{36,40},{44,48},{52,56},{60,64},{68,... | collective-permute-start | bytes 1572872 | tf_op jit(solution)/shard_map/ppermute | solution.py:457
  14.9 8.6 %collective-permute-start.4 = (bf16[64,1024]{1,0:T(8,128)(2,1)S(1)}, bf16[64,1024]{1,0:T(8,128)(2,1)S(1)}, u32[]{:S(2)}, u32[]{:S(2)}) collective-permute-start(bf16[64,1024]{1,0:T(8,128)(2,1)S(1)} %collective-permute-done.3.r2), channel_id=1, source_target_pairs={{4,8},{20,24},{36,40},{52,56},{68,72},{84,88},{100,104},{116,120},... | collective-permute-start | bytes 393224 | tf_op jit(solution)/shard_map/ppermute | solution.py:457
  23.5 1.6 %collective-permute-start.6 = (bf16[128,1024]{1,0:T(8,128)(2,1)S(1)}, bf16[128,1024]{1,0:T(8,128)(2,1)S(1)}, u32[]{:S(2)}, u32[]{:S(2)}) collective-permute-start(bf16[128,1024]{1,0:T(8,128)(2,1)S(1)} %shard_map.78.after), channel_id=1, source_target_pairs={{0,4},{8,12},{16,20},{24,28},{32,36},{40,44},{48,52},{56,60},{64,6... | collective-permute-start | bytes 786440 | tf_op jit(solution)/shard_map/ppermute | solution.py:457
  23.8 1.7 %collective-permute-start.5 = (bf16[128,1024]{1,0:T(8,128)(2,1)S(1)}, bf16[128,1024]{1,0:T(8,128)(2,1)S(1)}, u32[]{:S(2)}, u32[]{:S(2)}) collective-permute-start(bf16[128,1024]{1,0:T(8,128)(2,1)S(1)} %get-tuple-element.82), channel_id=1, source_target_pairs={{0,4},{8,12},{16,20},{24,28},{32,36},{40,44},{48,52},{56,60},{64,6... | collective-permute-start | bytes 786440 | tf_op jit(solution)/shard_map/ppermute | solution.py:457
  27.2 1.9 %collective-permute-start.7 = (bf16[224,1024]{1,0:T(8,128)(2,1)S(1)}, bf16[224,1024]{1,0:T(8,128)(2,1)S(1)}, u32[]{:S(2)}, u32[]{:S(2)}) collective-permute-start(bf16[224,1024]{1,0:T(8,128)(2,1)S(1)} %get-tuple-element.100), channel_id=1, source_target_pairs={{0,4},{8,12},{16,20},{24,28},{32,36},{40,44},{48,52},{56,60},{64,6... | collective-permute-start | bytes 1376264 | tf_op jit(solution)/shard_map/ppermute | solution.py:457
  29.3 16.7 %collective-permute-start.8 = (bf16[256,1024]{1,0:T(8,128)(2,1)S(1)}, bf16[256,1024]{1,0:T(8,128)(2,1)S(1)}, u32[]{:S(2)}, u32[]{:S(2)}) collective-permute-start(bf16[256,1024]{1,0:T(8,128)(2,1)S(1)} %get-tuple-element.101.after), channel_id=1, source_target_pairs={{4,8},{12,16},{20,24},{28,32},{36,40},{44,48},{52,56},{60,64},{68,... | collective-permute-start | bytes 1572872 | tf_op jit(solution)/shard_map/ppermute | solution.py:457
  31.8 12.2 %collective-permute-start.10 = (bf16[32,1024]{1,0:T(8,128)(2,1)S(1)}, bf16[32,1024]{1,0:T(8,128)(2,1)S(1)}, u32[]{:S(2)}, u32[]{:S(2)}) collective-permute-start(bf16[32,1024]{1,0:T(8,128)(2,1)S(1)} %get-tuple-element.106), channel_id=1, source_target_pairs={{0,24},{4,28},{16,40},{20,44},{32,56},{36,60},{48,72},{52,76},{64,... | collective-permute-start | bytes 196616 | tf_op jit(solution)/shard_map/ppermute | solution.py:457
  36.1 10.0 %collective-permute-start.9 = (bf16[64,1024]{1,0:T(8,128)(2,1)S(1)}, bf16[64,1024]{1,0:T(8,128)(2,1)S(1)}, u32[]{:S(2)}, u32[]{:S(2)}) collective-permute-start(bf16[64,1024]{1,0:T(8,128)(2,1)S(1)} %get-tuple-element.105), channel_id=1, source_target_pairs={{0,20},{8,28},{16,36},{24,44},{32,52},{40,60},{48,68},{56,76},{64,... | collective-permute-start | bytes 393224 | tf_op jit(solution)/shard_map/ppermute | solution.py:457
  44.0 2.5 %collective-permute-start.11 = (bf16[192,1024]{1,0:T(8,128)(2,1)S(1)}, bf16[192,1024]{1,0:T(8,128)(2,1)S(1)}, u32[]{:S(2)}, u32[]{:S(2)}) collective-permute-start(bf16[192,1024]{1,0:T(8,128)(2,1)S(1)} %get-tuple-element.108), channel_id=1, source_target_pairs={{0,4},{8,12},{16,20},{24,28},{32,36},{40,44},{48,52},{56,60},{64,6... | collective-permute-start | bytes 1179656 | tf_op jit(solution)/shard_map/ppermute | solution.py:457
  46.4 1.4 %collective-permute-start.12 = (bf16[64,1024]{1,0:T(8,128)(2,1)S(1)}, bf16[64,1024]{1,0:T(8,128)(2,1)S(1)}, u32[]{:S(2)}, u32[]{:S(2)}) collective-permute-start(bf16[64,1024]{1,0:T(8,128)(2,1)S(1)} %get-tuple-element.109), channel_id=1, source_target_pairs={{0,4},{8,12},{16,20},{24,28},{32,36},{40,44},{48,52},{56,60},{64,6... | collective-permute-start | bytes 393224 | tf_op jit(solution)/shard_map/ppermute | solution.py:457

commit v5 on v4

--- a/solution.py
+++ b/solution.py
@@ -399,13 +399,15 @@
             send[128:, lanes] = jnp.where(is0, high, low).astype(BF)
 
 
-def add_kernel(own, r1, r2, r3, acc, send):
+def send_kernel(r1, r2, send):
+    send[...] = (r1[192:].astype(F32) + expand(0.5 * r2[32:].astype(F32))).astype(BF)
+
+
+def add_kernel(own, r1, r2, r3, after, acc):
     core, _ = place()
     is0 = core == 0
     for j in range(2 * HEADS):
         lanes = head(j)
-        sib3 = r2[32:, lanes].astype(F32)
-        send[:, lanes] = (r1[192:, lanes].astype(F32) + expand(0.5 * sib3)).astype(BF)
         own3 = r2[:32, lanes].astype(F32) + r3[:, lanes].astype(F32)
         first = expand(0.25 * own3, 2) + placed(r1[128:192, lanes].astype(F32), ~is0, 64)
         acc[:, lanes] = own[:, lanes] + expand(0.5 * first) + placed(r1[:128, lanes].astype(F32), is0, 128)
@@ -509,12 +511,13 @@
         rest_kernel,
         [out, out, rows(256, F32), rows(192)],
         [stat],
-        flops=1 << 31,
+        flops=1 << 29,
         specs="v" * 17 + "a",
     )(q0, q1, g0, win, s1, e0, e1, m0, m1, best, inv, delta, dqo0, dqo1, dq2, dq3, att, msg1)
     near = swap(send, sibling)
-    acc, send = call(add_kernel, [rows(256, F32), rows(64)], flops=1 << 34)(acc, r1, r2, r3)
+    (send,) = call(send_kernel, [rows(64)], flops=1 << 34)(r1, r2)
     got = swap(send, sibling)
+    (acc,) = call(add_kernel, [rows(256, F32)], flops=1 << 34, specs="vvvva")(acc, r1, r2, r3, send)
     key_grad, value_grad = call(
         final_kernel, [out, out], [rows(256), pltpu.SemaphoreType.DMA((2 * HEADS,))], results=pl.ANY
     )(acc, near, got)

time: 49.6 us -> 48.6 us (0.980)
  waiting for transfers between devices: 10.9 us -> 9.87 us
    ppermute x13, waiting for transfers between devices: 10.9 us -> 9.87 us  [swap(): return lax.ppermute(value, 'seq', pairs + [(b, a) for a, b in pairs])]
where the time goes in v5:
time: 48.6 us; the launch traced here: 48.2 us
  starting transfers between devices  26.6 us (55%)
  waiting for transfers between devices  9.87 us (20%)
  Pallas kernels  9.86 us (20%)
  other arithmetic  1.08 us (2%)
  between operations  0.82 us (2%)
    ppermute x13, starting transfers between devices, swap(): return lax.ppermute(value, 'seq', pairs + [(b, a) for a, b in pairs])  26.6 us
    ppermute x13, waiting for transfers between devices, swap(): return lax.ppermute(value, 'seq', pairs + [(b, a) for a, b in pairs])  9.87 us
    pallas_call x1, Pallas kernels, per_device(): call(rest_kernel, [out, out, rows(256, F32), rows(192)], [stat], flops=1...  2.69 us
    pallas_call x1, Pallas kernels, per_device(): call(far_kernel, [out, stat, stat, stat, heads(64), heads(32), rows(64, F...  1.67 us
    pallas_call x1, Pallas kernels, per_device(): call(local_kernel, [out, out, ((128, D), BF), ((64, D), BF), ((32, D), BF...  1.6 us
    pallas_call x1, Pallas kernels, per_device(): call(final_kernel, [out, out], [rows(256), pltpu.SemaphoreType.DMA((2 * H...  1.16 us
    concatenate x1, other arithmetic, per_device(): jnp.concatenate([key_rows, value_rows], axis=1)  1.08 us
  transfers between devices with their start and end apart: 13, of which 7 were waited for; matrix products, arithmetic and copies ran while one was open for 2% of the time, Pallas kernels for 13%

profile of v5, /device:TPU:11, one launch (start us, length us, event | category | flops | bytes accessed | tf_op | source)
XLA Modules:
  0.0 48.2 jit_solution(2411411584197418277)
XLA Ops:
  0.6 0.8 %collective-permute-start = (bf16[256,512]{1,0:T(8,128)(2,1)}, bf16[256,512]{1,0:T(8,128)(2,1)S(1)}, u32[]{:S(2)}, u32[]{:S(2)}) collective-permute-start(bf16[256,512]{1,0:T(8,128)(2,1)} %param.5), channel_id=1, source_target_pairs={{0,4},{8,12},{16,20},{24,28},{32,36},{40,44},{48,52},{56,60},{64,6... | collective-permute-start | bytes 786440 | tf_op jit(solution)/shard_map/ppermute | solution.py:459
  1.4 0.1 collective-permute-start.1
  1.5 1.1 %pad_maximum_fusion.raw = bf16[256,1024]{1,0:T(8,128)(2,1)S(1)} fusion(bf16[256,512]{1,0:T(8,128)(2,1)} %param.6, bf16[256,512]{1,0:T(8,128)(2,1)} %param.5), kind=kLoop, calls=%fused_computation | loop fusion | flops 1048576 | bytes 1048576 | tf_op jit(solution)/shard_map/concatenate | solution.py:472
  2.6 0.3 shard_map.75
  2.9 0.2 collective-permute-done.1.vs
  3.1 0.4 shard_map.76
  3.5 8.1 %collective-permute-start.3 = (bf16[64,1024]{1,0:T(8,128)(2,1)S(1)}, bf16[64,1024]{1,0:T(8,128)(2,1)S(1)}, u32[]{:S(2)}, u32[]{:S(2)}) collective-permute-start(bf16[64,1024]{1,0:T(8,128)(2,1)S(1)} %get-tuple-element.72), channel_id=1, source_target_pairs={{0,20},{8,28},{16,36},{24,44},{32,52},{40,60},{48,68},{56,76},{64,... | collective-permute-start | bytes 393224 | tf_op jit(solution)/shard_map/ppermute | solution.py:459
  11.6 1.9 %collective-permute-start.2 = (bf16[256,1024]{1,0:T(8,128)(2,1)S(1)}, bf16[256,1024]{1,0:T(8,128)(2,1)S(1)}, u32[]{:S(2)}, u32[]{:S(2)}) collective-permute-start(bf16[256,1024]{1,0:T(8,128)(2,1)S(1)} %get-tuple-element.71), channel_id=1, source_target_pairs={{4,8},{12,16},{20,24},{28,32},{36,40},{44,48},{52,56},{60,64},{68,... | collective-permute-start | bytes 1572872 | tf_op jit(solution)/shard_map/ppermute | solution.py:459
  13.5 1.4 %collective-permute-done.3.r2 = bf16[64,1024]{1,0:T(8,128)(2,1)S(1)} collective-permute-done((bf16[64,1024]{1,0:T(8,128)(2,1)S(1)}, bf16[64,1024]{1,0:T(8,128)(2,1)S(1)}, u32[]{:S(2)}, u32[]{:S(2)}) %collective-permute-start.3) | collective-permute-done | bytes 131104 | tf_op jit(solution)/shard_map/ppermute | solution.py:459
  14.9 2.3 %collective-permute-start.4 = (bf16[64,1024]{1,0:T(8,128)(2,1)S(1)}, bf16[64,1024]{1,0:T(8,128)(2,1)S(1)}, u32[]{:S(2)}, u32[]{:S(2)}) collective-permute-start(bf16[64,1024]{1,0:T(8,128)(2,1)S(1)} %collective-permute-done.3.r2), channel_id=1, source_target_pairs={{4,8},{20,24},{36,40},{52,56},{68,72},{84,88},{100,104},{116,120},... | collective-permute-start | bytes 393224 | tf_op jit(solution)/shard_map/ppermute | solution.py:459
  17.2 1.6 %shard_map.77 = (bf16[256,512]{1,0:T(8,128)(2,1)S(1)}, bf16[256,512]{1,0:T(8,128)(2,1)S(1)}, bf16[128,512]{1,0:T(8,128)(2,1)S(1)}, bf16[64,512]{1,0:T(8,128)(2,1...) custom-call(bf16[256,512]{1,0:T(8,128)(2,1)S(1)} %copy-done, ...), custom_call_target="tpu_custom_call" | custom-call | flops 8589934592 | bytes 1048576 | tf_op jit(solution)/shard_map/pallas_call | solution.py:480
  18.8 4.7 %collective-permute-done.4.r3 = bf16[64,1024]{1,0:T(8,128)(2,1)S(1)} collective-permute-done((bf16[64,1024]{1,0:T(8,128)(2,1)S(1)}, bf16[64,1024]{1,0:T(8,128)(2,1)S(1)}, u32[]{:S(2)}, u32[]{:S(2)}) %collective-permute-start.4) | collective-permute-done | bytes 131104 | tf_op jit(solution)/shard_map/ppermute | solution.py:459
  23.5 0.1 collective-permute-start.6
  23.6 0.1 shard_map.79
  23.8 0.6 %collective-permute-start.5 = (bf16[128,1024]{1,0:T(8,128)(2,1)S(1)}, bf16[128,1024]{1,0:T(8,128)(2,1)S(1)}, u32[]{:S(2)}, u32[]{:S(2)}) collective-permute-start(bf16[128,1024]{1,0:T(8,128)(2,1)S(1)} %get-tuple-element.80), channel_id=1, source_target_pairs={{0,4},{8,12},{16,20},{24,28},{32,36},{40,44},{48,52},{56,60},{64,6... | collective-permute-start | bytes 786440 | tf_op jit(solution)/shard_map/ppermute | solution.py:459
  24.3 0.8 %shard_map.80 = (f32[4,256,128]{2,1,0:T(8,128)S(1)}, f32[4,256,128]{2,1,0:T(8,128)S(1)}, f32[4,256,128]{2,1,0:T(8,128)S(1)}, bf16[4,128,128]{2,1,0:T(8,128)(2,1)...) custom-call(bf16[256,512]{1,0:T(8,128)(2,1)S(1)} %get-tuple-element.61.q0, ...), custom_call_target="tpu_custom_call" | custom-call | flops 1073741824 | bytes 1048576 | tf_op jit(solution)/shard_map/pallas_call | solution.py:491
  25.2 0.4 collective-permute-done.5.got2
  25.5 1.7 %shard_map.81 = (bf16[256,512]{1,0:T(8,128)(2,1)S(1)}, f32[4,256,128]{2,1,0:T(8,128)S(1)}, f32[4,256,128]{2,1,0:T(8,128)S(1)}, f32[4,256,128]{2,1,0:T(8,128)S(1)...) custom-call(bf16[64,512]{1,0:T(8,128)(2,1)S(1)} %get-tuple-element.6, ...), custom_call_target="tpu_custom_call" | custom-call | tf_op jit(solution)/shard_map/pallas_call | solution.py:497
  27.2 0.5 collective-permute-start.7
  27.7 0.6 %shard_map.82 = (f32[4,128,128]{2,1,0:T(8,128)S(1)}, f32[4,128,128]{2,1,0:T(8,128)S(1)}, f32[128,1024]{1,0:T(8,128)S(1)}, f32[128,1024]{1,0:T(8,128)S(1)}) custom-call(bf16[256,512]{1,0:T(8,128)(2,1)S(1)} %get-tuple-element.61.q0, bf16[128,512]{1,0:T(8,128)(2,1)S(1)} %get-tuple-element.62.q1, bf16[256,512]{1,0:T(8,128)(2,1)S(1)} %get-tuple-element.63.g_ref, ...), custom_call_target="tpu_custom_call" | custom-call | flops 1073741824 | bytes 1048576 | tf_op jit(solution)/shard_map/pallas_call | solution.py:503
  28.2 0.9 %collective-permute-done.7.got = bf16[224,1024]{1,0:T(8,128)(2,1)S(1)} collective-permute-done((bf16[224,1024]{1,0:T(8,128)(2,1)S(1)}, bf16[224,1024]{1,0:T(8,128)(2,1)S(1)}, u32[]{:S(2)}, u32[]{:S(2)}) %collective-permute-start.7) | collective-permute-done | bytes 458784 | tf_op jit(solution)/shard_map/ppermute | solution.py:459
  29.1 0.2 shard_map.83
  29.3 2.5 %collective-permute-start.8 = (bf16[256,1024]{1,0:T(8,128)(2,1)S(1)}, bf16[256,1024]{1,0:T(8,128)(2,1)S(1)}, u32[]{:S(2)}, u32[]{:S(2)}) collective-permute-start(bf16[256,1024]{1,0:T(8,128)(2,1)S(1)} %get-tuple-element.99.after), channel_id=1, source_target_pairs={{4,8},{12,16},{20,24},{28,32},{36,40},{44,48},{52,56},{60,64},{68,... | collective-permute-start | bytes 1572872 | tf_op jit(solution)/shard_map/ppermute | solution.py:459
  31.8 4.2 %collective-permute-start.9 = (bf16[64,1024]{1,0:T(8,128)(2,1)S(1)}, bf16[64,1024]{1,0:T(8,128)(2,1)S(1)}, u32[]{:S(2)}, u32[]{:S(2)}) collective-permute-start(bf16[64,1024]{1,0:T(8,128)(2,1)S(1)} %get-tuple-element.103), channel_id=1, source_target_pairs={{0,20},{8,28},{16,36},{24,44},{32,52},{40,60},{48,68},{56,76},{64,... | collective-permute-start | bytes 393224 | tf_op jit(solution)/shard_map/ppermute | solution.py:459
  36.1 2.8 %collective-permute-start.10 = (bf16[32,1024]{1,0:T(8,128)(2,1)S(1)}, bf16[32,1024]{1,0:T(8,128)(2,1)S(1)}, u32[]{:S(2)}, u32[]{:S(2)}) collective-permute-start(bf16[32,1024]{1,0:T(8,128)(2,1)S(1)} %get-tuple-element.104), channel_id=1, source_target_pairs={{0,24},{4,28},{16,40},{20,44},{32,56},{36,60},{48,72},{52,76},{64,... | collective-permute-start | bytes 196616 | tf_op jit(solution)/shard_map/ppermute | solution.py:459
  38.9 2.7 %shard_map.84 = (bf16[256,512]{1,0:T(8,128)(2,1)}, bf16[256,512]{1,0:T(8,128)(2,1)}, f32[256,1024]{1,0:T(8,128)S(1)}, bf16[192,1024]{1,0:T(8,128)(2,1)S(1)}) custom-call(bf16[256,512]{1,0:T(8,128)(2,1)S(1)} %get-tuple-element.61.q0, bf16[128,512]{1,0:T(8,128)(2,1)S(1)} %get-tuple-element.62.q1, bf16[256,512]{1,0:T(8,128)(2,1)S(1)} %get-tuple-element.63.g_ref, ...), custom_call_target="tpu_custom_call" | custom-call | flops 536870912 | bytes 1048576 | tf_op jit(solution)/shard_map/pallas_call | solution.py:510
  41.6 1.6 %collective-permute-start.11 = (bf16[192,1024]{1,0:T(8,128)(2,1)S(1)}, bf16[192,1024]{1,0:T(8,128)(2,1)S(1)}, u32[]{:S(2)}, u32[]{:S(2)}) collective-permute-start(bf16[192,1024]{1,0:T(8,128)(2,1)S(1)} %get-tuple-element.105), channel_id=1, source_target_pairs={{0,4},{8,12},{16,20},{24,28},{32,36},{40,44},{48,52},{56,60},{64,6... | collective-permute-start | bytes 1179656 | tf_op jit(solution)/shard_map/ppermute | solution.py:459
  43.2 1.7 %collective-permute-done.8.r1 = bf16[256,1024]{1,0:T(8,128)(2,1)S(1)} collective-permute-done((bf16[256,1024]{1,0:T(8,128)(2,1)S(1)}, bf16[256,1024]{1,0:T(8,128)(2,1)S(1)}, u32[]{:S(2)}, u32[]{:S(2)}) %collective-permute-start.8) | collective-permute-done | bytes 524320 | tf_op jit(solution)/shard_map/ppermute | solution.py:459
  44.9 1.2 %collective-permute-start.12 = (bf16[64,1024]{1,0:T(8,128)(2,1)S(1)}, bf16[64,1024]{1,0:T(8,128)(2,1)S(1)}, u32[]{:S(2)}, u32[]{:S(2)}) collective-permute-start(bf16[64,1024]{1,0:T(8,128)(2,1)S(1)} %shard_map.85.after), channel_id=1, source_target_pairs={{0,4},{8,12},{16,20},{24,28},{32,36},{40,44},{48,52},{56,60},{64,6... | collective-permute-start | bytes 393224 | tf_op jit(solution)/shard_map/ppermute | solution.py:459
  46.1 0.3 shard_map.86.acc
  46.4 0.7 %collective-permute-done.12.got = bf16[64,1024]{1,0:T(8,128)(2,1)S(1)} collective-permute-done((bf16[64,1024]{1,0:T(8,128)(2,1)S(1)}, bf16[64,1024]{1,0:T(8,128)(2,1)S(1)}, u32[]{:S(2)}, u32[]{:S(2)}) %collective-permute-start.12) | collective-permute-done | bytes 131104 | tf_op jit(solution)/shard_map/ppermute | solution.py:459
  47.1 1.2 %shard_map.87 = (bf16[256,512]{1,0:T(8,128)(2,1)}, bf16[256,512]{1,0:T(8,128)(2,1)}) custom-call(f32[256,1024]{1,0:T(8,128)S(1)} %shard_map.86.acc, bf16[192,1024]{1,0:T(8,128)(2,1)S(1)} %collective-permute-done.11.near, bf16[64,1024]{1,0:T(8,128)(2,1)S(1)} %collective-permute-done.12.got), custom_call_target="tpu_custom_call" | custom-call | tf_op jit(solution)/shard_map/pallas_call | solution.py:521
  (12 shorter events, 0.1 us)
Async XLA Ops:
  0.6 2.3 %collective-permute-start = (bf16[256,512]{1,0:T(8,128)(2,1)}, bf16[256,512]{1,0:T(8,128)(2,1)S(1)}, u32[]{:S(2)}, u32[]{:S(2)}) collective-permute-start(bf16[256,512]{1,0:T(8,128)(2,1)} %param.5), channel_id=1, source_target_pairs={{0,4},{8,12},{16,20},{24,28},{32,36},{40,44},{48,52},{56,60},{64,6... | collective-permute-start | bytes 786440 | tf_op jit(solution)/shard_map/ppermute | solution.py:459
  1.4 1.7 %collective-permute-start.1 = (bf16[256,512]{1,0:T(8,128)(2,1)}, bf16[256,512]{1,0:T(8,128)(2,1)S(1)}, u32[]{:S(2)}, u32[]{:S(2)}) collective-permute-start(bf16[256,512]{1,0:T(8,128)(2,1)} %param.6), channel_id=1, source_target_pairs={{0,4},{8,12},{16,20},{24,28},{32,36},{40,44},{48,52},{56,60},{64,6... | collective-permute-start | bytes 786440 | tf_op jit(solution)/shard_map/ppermute | solution.py:459
  3.1 14.0 %copy-start = (bf16[256,512]{1,0:T(8,128)(2,1)S(1)}, bf16[256,512]{1,0:T(8,128)(2,1)}, u32[]{:S(2)}) copy-start(bf16[256,512]{1,0:T(8,128)(2,1)} %q_ref.1) | copy-start | bytes 786436
  3.1 14.0 %copy-start.1 = (bf16[256,512]{1,0:T(8,128)(2,1)S(1)}, bf16[256,512]{1,0:T(8,128)(2,1)}, u32[]{:S(2)}) copy-start(bf16[256,512]{1,0:T(8,128)(2,1)} %g_ref.1) | copy-start | bytes 786436
  3.5 11.4 %collective-permute-start.3 = (bf16[64,1024]{1,0:T(8,128)(2,1)S(1)}, bf16[64,1024]{1,0:T(8,128)(2,1)S(1)}, u32[]{:S(2)}, u32[]{:S(2)}) collective-permute-start(bf16[64,1024]{1,0:T(8,128)(2,1)S(1)} %get-tuple-element.72), channel_id=1, source_target_pairs={{0,20},{8,28},{16,36},{24,44},{32,52},{40,60},{48,68},{56,76},{64,... | collective-permute-start | bytes 393224 | tf_op jit(solution)/shard_map/ppermute | solution.py:459
  11.6 12.0 %collective-permute-start.2 = (bf16[256,1024]{1,0:T(8,128)(2,1)S(1)}, bf16[256,1024]{1,0:T(8,128)(2,1)S(1)}, u32[]{:S(2)}, u32[]{:S(2)}) collective-permute-start(bf16[256,1024]{1,0:T(8,128)(2,1)S(1)} %get-tuple-element.71), channel_id=1, source_target_pairs={{4,8},{12,16},{20,24},{28,32},{36,40},{44,48},{52,56},{60,64},{68,... | collective-permute-start | bytes 1572872 | tf_op jit(solution)/shard_map/ppermute | solution.py:459
  14.9 8.6 %collective-permute-start.4 = (bf16[64,1024]{1,0:T(8,128)(2,1)S(1)}, bf16[64,1024]{1,0:T(8,128)(2,1)S(1)}, u32[]{:S(2)}, u32[]{:S(2)}) collective-permute-start(bf16[64,1024]{1,0:T(8,128)(2,1)S(1)} %collective-permute-done.3.r2), channel_id=1, source_target_pairs={{4,8},{20,24},{36,40},{52,56},{68,72},{84,88},{100,104},{116,120},... | collective-permute-start | bytes 393224 | tf_op jit(solution)/shard_map/ppermute | solution.py:459
  23.5 1.6 %collective-permute-start.6 = (bf16[128,1024]{1,0:T(8,128)(2,1)S(1)}, bf16[128,1024]{1,0:T(8,128)(2,1)S(1)}, u32[]{:S(2)}, u32[]{:S(2)}) collective-permute-start(bf16[128,1024]{1,0:T(8,128)(2,1)S(1)} %shard_map.78.after), channel_id=1, source_target_pairs={{0,4},{8,12},{16,20},{24,28},{32,36},{40,44},{48,52},{56,60},{64,6... | collective-permute-start | bytes 786440 | tf_op jit(solution)/shard_map/ppermute | solution.py:459
  23.8 1.7 %collective-permute-start.5 = (bf16[128,1024]{1,0:T(8,128)(2,1)S(1)}, bf16[128,1024]{1,0:T(8,128)(2,1)S(1)}, u32[]{:S(2)}, u32[]{:S(2)}) collective-permute-start(bf16[128,1024]{1,0:T(8,128)(2,1)S(1)} %get-tuple-element.80), channel_id=1, source_target_pairs={{0,4},{8,12},{16,20},{24,28},{32,36},{40,44},{48,52},{56,60},{64,6... | collective-permute-start | bytes 786440 | tf_op jit(solution)/shard_map/ppermute | solution.py:459
  27.2 1.9 %collective-permute-start.7 = (bf16[224,1024]{1,0:T(8,128)(2,1)S(1)}, bf16[224,1024]{1,0:T(8,128)(2,1)S(1)}, u32[]{:S(2)}, u32[]{:S(2)}) collective-permute-start(bf16[224,1024]{1,0:T(8,128)(2,1)S(1)} %get-tuple-element.98), channel_id=1, source_target_pairs={{0,4},{8,12},{16,20},{24,28},{32,36},{40,44},{48,52},{56,60},{64,6... | collective-permute-start | bytes 1376264 | tf_op jit(solution)/shard_map/ppermute | solution.py:459
  29.3 15.5 %collective-permute-start.8 = (bf16[256,1024]{1,0:T(8,128)(2,1)S(1)}, bf16[256,1024]{1,0:T(8,128)(2,1)S(1)}, u32[]{:S(2)}, u32[]{:S(2)}) collective-permute-start(bf16[256,1024]{1,0:T(8,128)(2,1)S(1)} %get-tuple-element.99.after), channel_id=1, source_target_pairs={{4,8},{12,16},{20,24},{28,32},{36,40},{44,48},{52,56},{60,64},{68,... | collective-permute-start | bytes 1572872 | tf_op jit(solution)/shard_map/ppermute | solution.py:459
  31.8 11.4 %collective-permute-start.9 = (bf16[64,1024]{1,0:T(8,128)(2,1)S(1)}, bf16[64,1024]{1,0:T(8,128)(2,1)S(1)}, u32[]{:S(2)}, u32[]{:S(2)}) collective-permute-start(bf16[64,1024]{1,0:T(8,128)(2,1)S(1)} %get-tuple-element.103), channel_id=1, source_target_pairs={{0,20},{8,28},{16,36},{24,44},{32,52},{40,60},{48,68},{56,76},{64,... | collective-permute-start | bytes 393224 | tf_op jit(solution)/shard_map/ppermute | solution.py:459
  36.1 10.0 %collective-permute-start.10 = (bf16[32,1024]{1,0:T(8,128)(2,1)S(1)}, bf16[32,1024]{1,0:T(8,128)(2,1)S(1)}, u32[]{:S(2)}, u32[]{:S(2)}) collective-permute-start(bf16[32,1024]{1,0:T(8,128)(2,1)S(1)} %get-tuple-element.104), channel_id=1, source_target_pairs={{0,24},{4,28},{16,40},{20,44},{32,56},{36,60},{48,72},{52,76},{64,... | collective-permute-start | bytes 196616 | tf_op jit(solution)/shard_map/ppermute | solution.py:459
  41.6 4.8 %collective-permute-start.11 = (bf16[192,1024]{1,0:T(8,128)(2,1)S(1)}, bf16[192,1024]{1,0:T(8,128)(2,1)S(1)}, u32[]{:S(2)}, u32[]{:S(2)}) collective-permute-start(bf16[192,1024]{1,0:T(8,128)(2,1)S(1)} %get-tuple-element.105), channel_id=1, source_target_pairs={{0,4},{8,12},{16,20},{24,28},{32,36},{40,44},{48,52},{56,60},{64,6... | collective-permute-start | bytes 1179656 | tf_op jit(solution)/shard_map/ppermute | solution.py:459
  44.9 2.2 %collective-permute-start.12 = (bf16[64,1024]{1,0:T(8,128)(2,1)S(1)}, bf16[64,1024]{1,0:T(8,128)(2,1)S(1)}, u32[]{:S(2)}, u32[]{:S(2)}) collective-permute-start(bf16[64,1024]{1,0:T(8,128)(2,1)S(1)} %shard_map.85.after), channel_id=1, source_target_pairs={{0,4},{8,12},{16,20},{24,28},{32,36},{40,44},{48,52},{56,60},{64,6... | collective-permute-start | bytes 393224 | tf_op jit(solution)/shard_map/ppermute | solution.py:459

commit v6 on v5

--- a/solution.py
+++ b/solution.py
@@ -249,47 +249,58 @@
             )
 
 
+def third_kernel(q3, r2, r3, got, top, zsum, ysum, w3, e3, m3, top_out, z_out, y_out):
+    core, chip = place()
+    is0 = core == 0
+    holder = lax.rem(core + chip, 2) == 1
+    w3[:64] = r2[...]
+    w3[64:128] = got[:64]
+    w3[128:] = jnp.where(holder, r3[...], got[64:])
+    low2, high2 = chip >= 2, chip <= 29
+    even = lax.rem(chip, 2) == 0
+    lane = lax.broadcasted_iota(jnp.int32, (1, 192), 1)
+    cross_bad = penalty(jnp.where(even, chip <= 28, chip >= 3))
+    own_bad = penalty(jnp.where(is0, high2, low2))
+    sib_bad = penalty(jnp.where(is0, low2, high2))
+    bias = jnp.where(lane < 64, own_bad, jnp.where(lane < 128, sib_bad, cross_bad))
+    results = soft([(q3[:, head(h)], w3[:, head(h)], w3[:, head(HEADS + h)], bias) for h in range(HEADS)])
+    for h in range(HEADS):
+        e3[h], m3[h], d, n = results[h]
+        for c in range(2):
+            r, b = slice(c * 128, (c + 1) * 128), slice(c * 16, (c + 1) * 16)
+            top_out[h, r], z_out[h, r], y_out[h, r], _ = merge(
+                top[h, r], zsum[h, r], ysum[h, r], [(m3[h, b], d[b], n[b], 3)]
+            )
+
+
 def far_kernel(
-    q2, q3, g_ref, top, zsum, ysum, r1, got2, r2, r3, got3,
-    att, best_out, inv_out, delta_out, dq2, dq3, own2, own3, cross3, send,
-    w2, w3,
+    q2, q3, g_ref, top, zsum, ysum, r1, got2, w3, e3, m3,
+    att, best_out, inv_out, delta_out, dq2, dq3, own2, own3, cross3, send2, send3,
+    w2,
 ):
     core, chip = place()
     is0 = core == 0
     holder = lax.rem(core + chip, 2) == 1
     w2[:128] = got2[...]
     w2[128:] = r1[192:]
-    w3[:64] = r2[...]
-    w3[64:128] = got3[:64]
-    w3[128:] = jnp.where(holder, r3[...], got3[64:])
     left_ok, right_ok = chip >= 1, chip <= 30
-    low2, high2 = chip >= 2, chip <= 29
-    even = lax.rem(chip, 2) == 0
     lane = lax.broadcasted_iota(jnp.int32, (1, 192), 1)
     own_bad = penalty(jnp.where(is0, left_ok, right_ok))
     sib_bad = penalty(jnp.where(is0, right_ok, left_ok))
-    bias2 = jnp.where(lane < 128, sib_bad, own_bad)
-    cross_bad = penalty(jnp.where(even, chip <= 28, chip >= 3))
-    own_bad = penalty(jnp.where(is0, high2, low2))
-    sib_bad = penalty(jnp.where(is0, low2, high2))
-    bias3 = jnp.where(lane < 64, own_bad, jnp.where(lane < 128, sib_bad, cross_bad))
-    units = []
-    for h in range(HEADS):
-        kl, vl = head(h), head(HEADS + h)
-        units.append((q2[:, kl], w2[:, kl], w2[:, vl], bias2))
-        units.append((q3[:, kl], w3[:, kl], w3[:, vl], bias3))
+    bias = jnp.where(lane < 128, sib_bad, own_bad)
+    units = [(q2[:, head(h)], w2[:, head(h)], w2[:, head(HEADS + h)], bias) for h in range(HEADS)]
     results = soft(units)
     units = []
     for h in range(HEADS):
         kl, vl = head(h), head(HEADS + h)
-        (e2, m2, d2, n2), (e3, m3, d3, n3) = results[2 * h : 2 * h + 2]
+        e2, m2, d2, n2 = results[h]
         grads = ([], [])
         drifts = ([], [])
         for c in range(2):
             r = slice(c * 128, (c + 1) * 128)
             a, b = slice(c * 32, (c + 1) * 32), slice(c * 16, (c + 1) * 16)
-            pieces = [(m2[a], d2[a], n2[a], 2), (m3[b], d3[b], n3[b], 3)]
-            best, z, y, factors = merge(top[h, r], zsum[h, r], ysum[h, r], pieces)
+            best, z, y, factors = merge(top[h, r], zsum[h, r], ysum[h, r], [(m2[a], d2[a], n2[a], 2)])
+            factors.append(8.0 * jnp.exp2(expand(m3[h, b], 3) - best))
             inv = 1.0 / z
             y = y * inv
             att[r, kl] = y.astype(BF)
@@ -302,7 +313,7 @@
                 share = factors[i] * inv
                 grads[i].append(fold(share * g, i + 2))
                 drifts[i].append(fold(share * delta, i + 2))
-        for i, (q, w, e) in enumerate(((q2, w2, e2), (q3, w3, e3))):
+        for i, (q, w, e) in enumerate(((q2, w2, e2), (q3, w3, e3[h]))):
             grad = jnp.concatenate(grads[i], axis=0).astype(BF)
             units.append((q[:, kl], w[:, kl], w[:, vl], e, grad, jnp.concatenate(drifts[i], axis=0)))
     results = backward(units)
@@ -312,13 +323,13 @@
             (dq2, dq3)[i][h] = dq
             for lanes, value in ((head(h), dk), (head(HEADS + h), dv)):
                 if i == 0:
-                    send[:128, lanes] = value[:128].astype(BF)
+                    send2[:, lanes] = value[:128].astype(BF)
                     own2[:, lanes] = value[128:]
                 else:
                     own3[:, lanes] = value[:64]
-                    send[128:192, lanes] = value[64:128].astype(BF)
+                    send3[:64, lanes] = value[64:128].astype(BF)
                     cross3[:, lanes] = jnp.where(holder, value[128:160], value[160:])
-                    send[192:, lanes] = jnp.where(holder, value[160:], value[128:160]).astype(BF)
+                    send3[64:, lanes] = jnp.where(holder, value[160:], value[128:160]).astype(BF)
 
 
 def coarse_grad(m, best, inv, g, delta):
@@ -353,18 +364,21 @@
         dq1[h], d1[:, kl], d1[:, vl] = results[2 * h + 1]
 
 
-def join_kernel(own2, own3, cross3, d0, d1, got, msg1, msg2, msg3):
+def join_kernel(own2, d0, d1, got, msg1):
     core, _ = place()
     is0 = core == 0
     for j in range(2 * HEADS):
         lanes = head(j)
-        msg1[192:, lanes] = (own2[:, lanes] + got[64:128, lanes].astype(F32)).astype(BF)
+        msg1[192:, lanes] = (own2[:, lanes] + got[64:, lanes].astype(F32)).astype(BF)
         first = d1[:, lanes] + expand(0.5 * got[:64, lanes].astype(F32))
         low, high = first[:64], first[64:]
         msg1[128:192, lanes] = jnp.where(is0, low, high).astype(BF)
         msg1[:128, lanes] = (d0[:, lanes] + expand(0.5 * jnp.where(is0, high, low))).astype(BF)
-        msg2[:, lanes] = (own3[:, lanes] + got[128:192, lanes].astype(F32)).astype(BF)
-        msg3[:, lanes] = (cross3[:, lanes] + got[192:, lanes].astype(F32)).astype(BF)
+
+
+def third_join_kernel(own3, cross3, got, msg2, msg3):
+    msg2[...] = (own3[...] + got[:64].astype(F32)).astype(BF)
+    msg3[...] = (cross3[...] + got[64:].astype(F32)).astype(BF)
 
 
 def rest_kernel(
@@ -403,24 +417,28 @@
     send[...] = (r1[192:].astype(F32) + expand(0.5 * r2[32:].astype(F32))).astype(BF)
 
 
-def add_kernel(own, r1, r2, r3, after, acc):
+def add_kernel(own, r1, r2, after, acc):
     core, _ = place()
     is0 = core == 0
     for j in range(2 * HEADS):
         lanes = head(j)
-        own3 = r2[:32, lanes].astype(F32) + r3[:, lanes].astype(F32)
-        first = expand(0.25 * own3, 2) + placed(r1[128:192, lanes].astype(F32), ~is0, 64)
+        first = expand(0.25 * r2[:32, lanes].astype(F32), 2) + placed(r1[128:192, lanes].astype(F32), ~is0, 64)
         acc[:, lanes] = own[:, lanes] + expand(0.5 * first) + placed(r1[:128, lanes].astype(F32), is0, 128)
 
 
-def final_kernel(acc, near, got, dk, dv, done, sems):
+def cross_kernel(r3, after, second):
+    second[...] = expand(0.5 * r3[...].astype(F32))
+
+
+def final_kernel(acc, near, got, cross, dk, dv, done, sems):
     core, _ = place()
     is0 = core == 0
     matrix = order_matrix(back=True)
     copies = []
     for j in range(2 * HEADS):
         lanes = head(j)
-        first = expand(0.5 * got[:, lanes].astype(F32)) + placed(near[128:, lanes].astype(F32), is0, 64)
+        second = got[:, lanes].astype(F32) + cross[:, lanes]
+        first = expand(0.5 * second) + placed(near[128:, lanes].astype(F32), is0, 64)
         total = acc[:, lanes] + expand(0.5 * first) + placed(near[:128, lanes].astype(F32), ~is0, 128)
         done[:, lanes] = reorder(matrix, total.astype(BF))
         target = (dk if j < HEADS else dv).at[:, head(j % HEADS)]
@@ -494,16 +512,21 @@
         [heads(128), heads(128)],
         flops=1 << 30,
     )(q0, q1, r1, outer1, top, zsum, ysum)
-    att, best, inv, delta, dq2, dq3, own2, own3, cross3, send = call(
+    w3, e3, m3, top, zsum, ysum = call(
+        third_kernel, [rows(192), heads(32, BF, 192), heads(32), stat, stat, stat], flops=1 << 28
+    )(q3, r2, r3, got3, top, zsum, ysum)
+    att, best, inv, delta, dq2, dq3, own2, own3, cross3, send2, send3 = call(
         far_kernel,
-        [out, stat, stat, stat, heads(64), heads(32), rows(64, F32), rows(64, F32), rows(32, F32), rows(224)],
-        [rows(192), rows(192)],
-    )(q2, q3, g0, top, zsum, ysum, r1, got2, r2, r3, got3)
-    got = swap(send, sibling)
+        [out, stat, stat, stat, heads(64), heads(32), rows(64, F32), rows(64, F32), rows(32, F32), rows(128), rows(96)],
+        [rows(192)],
+    )(q2, q3, g0, top, zsum, ysum, r1, got2, w3, e3, m3)
+    got2 = swap(send2, sibling)
+    got3 = swap(send3, sibling)
     dqo0, dqo1, d0, d1 = call(
         outer_back_kernel, [heads(128), heads(128), rows(128, F32), rows(128, F32)], flops=1 << 30
     )(q0, q1, g0, r1, outer1, eo0, eo1, mo0, mo1, best, inv, delta)
-    msg1, msg2, msg3 = call(join_kernel, [rows(256), rows(64), rows(32)])(own2, own3, cross3, d0, d1, got)
+    (msg1,) = call(join_kernel, [rows(256)])(own2, d0, d1, got2)
+    msg2, msg3 = call(third_join_kernel, [rows(64), rows(32)], flops=1 << 33)(own3, cross3, got3)
     r1 = swap(msg1, next1)
     r2 = swap(msg2, next2)
     r3 = swap(msg3, next3)
@@ -517,10 +540,11 @@
     near = swap(send, sibling)
     (send,) = call(send_kernel, [rows(64)], flops=1 << 34)(r1, r2)
     got = swap(send, sibling)
-    (acc,) = call(add_kernel, [rows(256, F32)], flops=1 << 34, specs="vvvva")(acc, r1, r2, r3, send)
+    (acc,) = call(add_kernel, [rows(256, F32)], specs="vvva")(acc, r1, r2, send)
+    (cross,) = call(cross_kernel, [rows(64, F32)], flops=1 << 34, specs="va")(r3, acc)
     key_grad, value_grad = call(
         final_kernel, [out, out], [rows(256), pltpu.SemaphoreType.DMA((2 * HEADS,))], results=pl.ANY
-    )(acc, near, got)
+    )(acc, near, got, cross)
     return attended, query_grad, key_grad, value_grad
 
 

time: 48.6 us -> 48 us (0.988)
    pallas_call x2 -> x5, Pallas kernels: 0.49 us -> 1.05 us  [the longest x1 0.59 us: per_device(): call(third_kernel, [rows(192), heads(32, BF, 192), heads(32), stat, stat,...]
    ppermute x13 -> x14, waiting for transfers between devices: 9.87 us -> 9.4 us  [swap(): return lax.ppermute(value, 'seq', pairs + [(b, a) for a, b in pairs])]
    ppermute x13 -> x14, starting transfers between devices: 26.6 us -> 26.2 us  [swap(): return lax.ppermute(value, 'seq', pairs + [(b, a) for a, b in pairs])]
  transfers between devices with their start and end apart: 13 -> 14, of which waited for: 7 -> 7; matrix products, arithmetic and copies ran while one was open for 2% -> 2% of each run, Pallas kernels for 13% -> 15%
where the time goes in v6:
time: 48 us; the launch traced here: 47.8 us
  starting transfers between devices  26.2 us (55%)
  Pallas kernels  10.2 us (21%)
  waiting for transfers between devices  9.4 us (20%)
  other arithmetic  1.08 us (2%)
  between operations  0.87 us (2%)
    ppermute x14, starting transfers between devices, swap(): return lax.ppermute(value, 'seq', pairs + [(b, a) for a, b in pairs])  26.2 us
    ppermute x14, waiting for transfers between devices, swap(): return lax.ppermute(value, 'seq', pairs + [(b, a) for a, b in pairs])  9.4 us
    pallas_call x1, Pallas kernels, per_device(): call(rest_kernel, [out, out, rows(256, F32), rows(192)], [stat], flops=1...  2.68 us
    pallas_call x1, Pallas kernels, per_device(): call(local_kernel, [out, out, ((128, D), BF), ((64, D), BF), ((32, D), BF...  1.6 us
    pallas_call x1, Pallas kernels, per_device(): call(far_kernel, [out, stat, stat, stat, heads(64), heads(32), rows(64, F...  1.43 us
    pallas_call x1, Pallas kernels, per_device(): call(final_kernel, [out, out], [rows(256), pltpu.SemaphoreType.DMA((2 * H...  1.18 us
    concatenate x1, other arithmetic, per_device(): jnp.concatenate([key_rows, value_rows], axis=1)  1.08 us
  transfers between devices with their start and end apart: 14, of which 7 were waited for; matrix products, arithmetic and copies ran while one was open for 2% of the time, Pallas kernels for 15%

profile of v6, /device:TPU:11, one launch (start us, length us, event | category | flops | bytes accessed | tf_op | source)
XLA Modules:
  0.0 47.8 jit_solution(5957496014093623334)
XLA Ops:
  0.6 0.8 %collective-permute-start = (bf16[256,512]{1,0:T(8,128)(2,1)}, bf16[256,512]{1,0:T(8,128)(2,1)S(1)}, u32[]{:S(2)}, u32[]{:S(2)}) collective-permute-start(bf16[256,512]{1,0:T(8,128)(2,1)} %param.5), channel_id=1, source_target_pairs={{0,4},{8,12},{16,20},{24,28},{32,36},{40,44},{48,52},{56,60},{64,6... | collective-permute-start | bytes 786440 | tf_op jit(solution)/shard_map/ppermute | solution.py:477
  1.5 1.1 %pad_maximum_fusion.raw = bf16[256,1024]{1,0:T(8,128)(2,1)S(1)} fusion(bf16[256,512]{1,0:T(8,128)(2,1)} %param.6, bf16[256,512]{1,0:T(8,128)(2,1)} %param.5), kind=kLoop, calls=%fused_computation | loop fusion | flops 1048576 | bytes 1048576 | tf_op jit(solution)/shard_map/concatenate | solution.py:490
  2.6 0.3 shard_map.75
  2.9 0.2 collective-permute-done.1.vs
  3.1 0.4 shard_map.76
  3.5 8.1 %collective-permute-start.2 = (bf16[64,1024]{1,0:T(8,128)(2,1)S(1)}, bf16[64,1024]{1,0:T(8,128)(2,1)S(1)}, u32[]{:S(2)}, u32[]{:S(2)}) collective-permute-start(bf16[64,1024]{1,0:T(8,128)(2,1)S(1)} %get-tuple-element.77), channel_id=1, source_target_pairs={{0,20},{8,28},{16,36},{24,44},{32,52},{40,60},{48,68},{56,76},{64,... | collective-permute-start | bytes 393224 | tf_op jit(solution)/shard_map/ppermute | solution.py:477
  11.6 1.9 %collective-permute-start.5 = (bf16[256,1024]{1,0:T(8,128)(2,1)S(1)}, bf16[256,1024]{1,0:T(8,128)(2,1)S(1)}, u32[]{:S(2)}, u32[]{:S(2)}) collective-permute-start(bf16[256,1024]{1,0:T(8,128)(2,1)S(1)} %get-tuple-element.79), channel_id=1, source_target_pairs={{4,8},{12,16},{20,24},{28,32},{36,40},{44,48},{52,56},{60,64},{68,... | collective-permute-start | bytes 1572872 | tf_op jit(solution)/shard_map/ppermute | solution.py:477
  13.5 1.4 %collective-permute-done.2.r2 = bf16[64,1024]{1,0:T(8,128)(2,1)S(1)} collective-permute-done((bf16[64,1024]{1,0:T(8,128)(2,1)S(1)}, bf16[64,1024]{1,0:T(8,128)(2,1)S(1)}, u32[]{:S(2)}, u32[]{:S(2)}) %collective-permute-start.2) | collective-permute-done | bytes 131104 | tf_op jit(solution)/shard_map/ppermute | solution.py:477
  14.9 2.3 %collective-permute-start.3 = (bf16[64,1024]{1,0:T(8,128)(2,1)S(1)}, bf16[64,1024]{1,0:T(8,128)(2,1)S(1)}, u32[]{:S(2)}, u32[]{:S(2)}) collective-permute-start(bf16[64,1024]{1,0:T(8,128)(2,1)S(1)} %collective-permute-done.2.r2), channel_id=1, source_target_pairs={{4,8},{20,24},{36,40},{52,56},{68,72},{84,88},{100,104},{116,120},... | collective-permute-start | bytes 393224 | tf_op jit(solution)/shard_map/ppermute | solution.py:477
  17.2 1.6 %shard_map.77 = (bf16[256,512]{1,0:T(8,128)(2,1)S(1)}, bf16[256,512]{1,0:T(8,128)(2,1)S(1)}, bf16[128,512]{1,0:T(8,128)(2,1)S(1)}, bf16[64,512]{1,0:T(8,128)(2,1...) custom-call(bf16[256,512]{1,0:T(8,128)(2,1)S(1)} %copy-done, ...), custom_call_target="tpu_custom_call" | custom-call | flops 8589934592 | bytes 1048576 | tf_op jit(solution)/shard_map/pallas_call | solution.py:498
  18.8 4.7 %collective-permute-done.3.r3 = bf16[64,1024]{1,0:T(8,128)(2,1)S(1)} collective-permute-done((bf16[64,1024]{1,0:T(8,128)(2,1)S(1)}, bf16[64,1024]{1,0:T(8,128)(2,1)S(1)}, u32[]{:S(2)}, u32[]{:S(2)}) %collective-permute-start.3) | collective-permute-done | bytes 131104 | tf_op jit(solution)/shard_map/ppermute | solution.py:477
  23.6 0.1 shard_map.79
  23.8 0.6 %collective-permute-start.6 = (bf16[128,1024]{1,0:T(8,128)(2,1)S(1)}, bf16[128,1024]{1,0:T(8,128)(2,1)S(1)}, u32[]{:S(2)}, u32[]{:S(2)}) collective-permute-start(bf16[128,1024]{1,0:T(8,128)(2,1)S(1)} %get-tuple-element.89), channel_id=1, source_target_pairs={{0,4},{8,12},{16,20},{24,28},{32,36},{40,44},{48,52},{56,60},{64,6... | collective-permute-start | bytes 786440 | tf_op jit(solution)/shard_map/ppermute | solution.py:477
  24.3 0.8 %shard_map.80 = (f32[4,256,128]{2,1,0:T(8,128)S(1)}, f32[4,256,128]{2,1,0:T(8,128)S(1)}, f32[4,256,128]{2,1,0:T(8,128)S(1)}, bf16[4,128,128]{2,1,0:T(8,128)(2,1)...) custom-call(bf16[256,512]{1,0:T(8,128)(2,1)S(1)} %get-tuple-element.67.q0, ...), custom_call_target="tpu_custom_call" | custom-call | flops 1073741824 | bytes 1048576 | tf_op jit(solution)/shard_map/pallas_call | solution.py:509
  25.2 0.6 %shard_map.81 = (bf16[192,1024]{1,0:T(8,128)(2,1)S(1)}, bf16[4,32,192]{2,1,0:T(8,128)(2,1)S(1)}, f32[4,32,128]{2,1,0:T(8,128)S(1)}, f32[4,256,128]{2,1,0:T(8,128...) custom-call(bf16[32,512]{1,0:T(8,128)(2,1)S(1)} %get-tuple-element.76.q3, ...), custom_call_target="tpu_custom_call" | custom-call | flops 268435456 | bytes 1048576 | tf_op jit(solution)/shard_map/pallas_call | solution.py:515
  25.8 1.4 %shard_map.82 = (bf16[256,512]{1,0:T(8,128)(2,1)S(1)}, f32[4,256,128]{2,1,0:T(8,128)S(1)}, f32[4,256,128]{2,1,0:T(8,128)S(1)}, f32[4,256,128]{2,1,0:T(8,128)S(1)...) custom-call(bf16[64,512]{1,0:T(8,128)(2,1)S(1)} %get-tuple-element.7, ...), custom_call_target="tpu_custom_call" | custom-call | tf_op jit(solution)/shard_map/pallas_call | solution.py:518
  27.2 0.2 collective-permute-start.7
  27.4 0.4 collective-permute-start.9
  27.8 0.6 %shard_map.83 = (f32[4,128,128]{2,1,0:T(8,128)S(1)}, f32[4,128,128]{2,1,0:T(8,128)S(1)}, f32[128,1024]{1,0:T(8,128)S(1)}, f32[128,1024]{1,0:T(8,128)S(1)}) custom-call(bf16[256,512]{1,0:T(8,128)(2,1)S(1)} %get-tuple-element.67.q0, bf16[128,512]{1,0:T(8,128)(2,1)S(1)} %get-tuple-element.68.q1, bf16[256,512]{1,0:T(8,128)(2,1)S(1)} %get-tuple-element.69.g_ref, ...), custom_call_target="tpu_custom_call" | custom-call | flops 1073741824 | bytes 1048576 | tf_op jit(solution)/shard_map/pallas_call | solution.py:525
  28.4 0.4 collective-permute-done.7.got
  28.8 0.2 shard_map.84.after
  29.0 2.5 %collective-permute-start.8 = (bf16[256,1024]{1,0:T(8,128)(2,1)S(1)}, bf16[256,1024]{1,0:T(8,128)(2,1)S(1)}, u32[]{:S(2)}, u32[]{:S(2)}) collective-permute-start(bf16[256,1024]{1,0:T(8,128)(2,1)S(1)} %shard_map.84.after), channel_id=1, source_target_pairs={{4,8},{12,16},{20,24},{28,32},{36,40},{44,48},{52,56},{60,64},{68,... | collective-permute-start | bytes 1572872 | tf_op jit(solution)/shard_map/ppermute | solution.py:477
  31.5 4.0 %collective-permute-start.10 = (bf16[64,1024]{1,0:T(8,128)(2,1)S(1)}, bf16[64,1024]{1,0:T(8,128)(2,1)S(1)}, u32[]{:S(2)}, u32[]{:S(2)}) collective-permute-start(bf16[64,1024]{1,0:T(8,128)(2,1)S(1)} %get-tuple-element.115), channel_id=1, source_target_pairs={{0,20},{8,28},{16,36},{24,44},{32,52},{40,60},{48,68},{56,76},{64,... | collective-permute-start | bytes 393224 | tf_op jit(solution)/shard_map/ppermute | solution.py:477
  35.6 3.1 %collective-permute-start.13 = (bf16[32,1024]{1,0:T(8,128)(2,1)S(1)}, bf16[32,1024]{1,0:T(8,128)(2,1)S(1)}, u32[]{:S(2)}, u32[]{:S(2)}) collective-permute-start(bf16[32,1024]{1,0:T(8,128)(2,1)S(1)} %get-tuple-element.117), channel_id=1, source_target_pairs={{0,24},{4,28},{16,40},{20,44},{32,56},{36,60},{48,72},{52,76},{64,... | collective-permute-start | bytes 196616 | tf_op jit(solution)/shard_map/ppermute | solution.py:477
  38.6 2.7 %shard_map.85 = (bf16[256,512]{1,0:T(8,128)(2,1)}, bf16[256,512]{1,0:T(8,128)(2,1)}, f32[256,1024]{1,0:T(8,128)S(1)}, bf16[192,1024]{1,0:T(8,128)(2,1)S(1)}) custom-call(bf16[256,512]{1,0:T(8,128)(2,1)S(1)} %get-tuple-element.67.q0, bf16[128,512]{1,0:T(8,128)(2,1)S(1)} %get-tuple-element.68.q1, bf16[256,512]{1,0:T(8,128)(2,1)S(1)} %get-tuple-element.69.g_ref, ...), custom_call_target="tpu_custom_call" | custom-call | flops 536870912 | bytes 1048576 | tf_op jit(solution)/shard_map/pallas_call | solution.py:533
  41.3 1.4 %collective-permute-start.11 = (bf16[192,1024]{1,0:T(8,128)(2,1)S(1)}, bf16[192,1024]{1,0:T(8,128)(2,1)S(1)}, u32[]{:S(2)}, u32[]{:S(2)}) collective-permute-start(bf16[192,1024]{1,0:T(8,128)(2,1)S(1)} %get-tuple-element.116), channel_id=1, source_target_pairs={{0,4},{8,12},{16,20},{24,28},{32,36},{40,44},{48,52},{56,60},{64,6... | collective-permute-start | bytes 1179656 | tf_op jit(solution)/shard_map/ppermute | solution.py:477
  42.7 0.2 collective-permute-done.10.r2
  42.8 1.8 %collective-permute-done.8.r1 = bf16[256,1024]{1,0:T(8,128)(2,1)S(1)} collective-permute-done((bf16[256,1024]{1,0:T(8,128)(2,1)S(1)}, bf16[256,1024]{1,0:T(8,128)(2,1)S(1)}, u32[]{:S(2)}, u32[]{:S(2)}) %collective-permute-start.8) | collective-permute-done | bytes 524320 | tf_op jit(solution)/shard_map/ppermute | solution.py:477
  44.7 0.9 %collective-permute-start.12 = (bf16[64,1024]{1,0:T(8,128)(2,1)S(1)}, bf16[64,1024]{1,0:T(8,128)(2,1)S(1)}, u32[]{:S(2)}, u32[]{:S(2)}) collective-permute-start(bf16[64,1024]{1,0:T(8,128)(2,1)S(1)} %shard_map.87.after), channel_id=1, source_target_pairs={{0,4},{8,12},{16,20},{24,28},{32,36},{40,44},{48,52},{56,60},{64,6... | collective-permute-start | bytes 393224 | tf_op jit(solution)/shard_map/ppermute | solution.py:477
  45.6 0.2 shard_map.88.after.acc
  45.9 0.7 %collective-permute-done.12.got = bf16[64,1024]{1,0:T(8,128)(2,1)S(1)} collective-permute-done((bf16[64,1024]{1,0:T(8,128)(2,1)S(1)}, bf16[64,1024]{1,0:T(8,128)(2,1)S(1)}, u32[]{:S(2)}, u32[]{:S(2)}) %collective-permute-start.12) | collective-permute-done | bytes 131104 | tf_op jit(solution)/shard_map/ppermute | solution.py:477
  46.6 1.2 %shard_map.90 = (bf16[256,512]{1,0:T(8,128)(2,1)}, bf16[256,512]{1,0:T(8,128)(2,1)}) custom-call(f32[256,1024]{1,0:T(8,128)S(1)} %shard_map.88.after.acc, bf16[192,1024]{1,0:T(8,128)(2,1)S(1)} %collective-permute-done.11.near, bf16[64,1024]{1,0:T(8,128)(2,1)S(1)} %collective-permute-done.12.got, f32[64,1024]{1,0:T(8,128)S(1)} %shard_map.89.cross), custom_call_target="tpu_custom_call" | custom-call | tf_op jit(solution)/shard_map/pallas_call | solution.py:545
  (17 shorter events, 0.3 us)
Async XLA Ops:
  0.6 2.3 %collective-permute-start = (bf16[256,512]{1,0:T(8,128)(2,1)}, bf16[256,512]{1,0:T(8,128)(2,1)S(1)}, u32[]{:S(2)}, u32[]{:S(2)}) collective-permute-start(bf16[256,512]{1,0:T(8,128)(2,1)} %param.5), channel_id=1, source_target_pairs={{0,4},{8,12},{16,20},{24,28},{32,36},{40,44},{48,52},{56,60},{64,6... | collective-permute-start | bytes 786440 | tf_op jit(solution)/shard_map/ppermute | solution.py:477
  1.4 1.7 %collective-permute-start.1 = (bf16[256,512]{1,0:T(8,128)(2,1)}, bf16[256,512]{1,0:T(8,128)(2,1)S(1)}, u32[]{:S(2)}, u32[]{:S(2)}) collective-permute-start(bf16[256,512]{1,0:T(8,128)(2,1)} %param.6), channel_id=1, source_target_pairs={{0,4},{8,12},{16,20},{24,28},{32,36},{40,44},{48,52},{56,60},{64,6... | collective-permute-start | bytes 786440 | tf_op jit(solution)/shard_map/ppermute | solution.py:477
  3.1 14.0 %copy-start = (bf16[256,512]{1,0:T(8,128)(2,1)S(1)}, bf16[256,512]{1,0:T(8,128)(2,1)}, u32[]{:S(2)}) copy-start(bf16[256,512]{1,0:T(8,128)(2,1)} %q_ref.1) | copy-start | bytes 786436
  3.1 14.0 %copy-start.1 = (bf16[256,512]{1,0:T(8,128)(2,1)S(1)}, bf16[256,512]{1,0:T(8,128)(2,1)}, u32[]{:S(2)}) copy-start(bf16[256,512]{1,0:T(8,128)(2,1)} %g_ref.1) | copy-start | bytes 786436
  3.5 11.4 %collective-permute-start.2 = (bf16[64,1024]{1,0:T(8,128)(2,1)S(1)}, bf16[64,1024]{1,0:T(8,128)(2,1)S(1)}, u32[]{:S(2)}, u32[]{:S(2)}) collective-permute-start(bf16[64,1024]{1,0:T(8,128)(2,1)S(1)} %get-tuple-element.77), channel_id=1, source_target_pairs={{0,20},{8,28},{16,36},{24,44},{32,52},{40,60},{48,68},{56,76},{64,... | collective-permute-start | bytes 393224 | tf_op jit(solution)/shard_map/ppermute | solution.py:477
  11.6 12.0 %collective-permute-start.5 = (bf16[256,1024]{1,0:T(8,128)(2,1)S(1)}, bf16[256,1024]{1,0:T(8,128)(2,1)S(1)}, u32[]{:S(2)}, u32[]{:S(2)}) collective-permute-start(bf16[256,1024]{1,0:T(8,128)(2,1)S(1)} %get-tuple-element.79), channel_id=1, source_target_pairs={{4,8},{12,16},{20,24},{28,32},{36,40},{44,48},{52,56},{60,64},{68,... | collective-permute-start | bytes 1572872 | tf_op jit(solution)/shard_map/ppermute | solution.py:477
  14.9 8.6 %collective-permute-start.3 = (bf16[64,1024]{1,0:T(8,128)(2,1)S(1)}, bf16[64,1024]{1,0:T(8,128)(2,1)S(1)}, u32[]{:S(2)}, u32[]{:S(2)}) collective-permute-start(bf16[64,1024]{1,0:T(8,128)(2,1)S(1)} %collective-permute-done.2.r2), channel_id=1, source_target_pairs={{4,8},{20,24},{36,40},{52,56},{68,72},{84,88},{100,104},{116,120},... | collective-permute-start | bytes 393224 | tf_op jit(solution)/shard_map/ppermute | solution.py:477
  23.5 1.6 %collective-permute-start.4 = (bf16[128,1024]{1,0:T(8,128)(2,1)S(1)}, bf16[128,1024]{1,0:T(8,128)(2,1)S(1)}, u32[]{:S(2)}, u32[]{:S(2)}) collective-permute-start(bf16[128,1024]{1,0:T(8,128)(2,1)S(1)} %shard_map.78.after), channel_id=1, source_target_pairs={{0,4},{8,12},{16,20},{24,28},{32,36},{40,44},{48,52},{56,60},{64,6... | collective-permute-start | bytes 786440 | tf_op jit(solution)/shard_map/ppermute | solution.py:477
  23.8 2.0 %collective-permute-start.6 = (bf16[128,1024]{1,0:T(8,128)(2,1)S(1)}, bf16[128,1024]{1,0:T(8,128)(2,1)S(1)}, u32[]{:S(2)}, u32[]{:S(2)}) collective-permute-start(bf16[128,1024]{1,0:T(8,128)(2,1)S(1)} %get-tuple-element.89), channel_id=1, source_target_pairs={{0,4},{8,12},{16,20},{24,28},{32,36},{40,44},{48,52},{56,60},{64,6... | collective-permute-start | bytes 786440 | tf_op jit(solution)/shard_map/ppermute | solution.py:477
  27.2 1.6 %collective-permute-start.7 = (bf16[128,1024]{1,0:T(8,128)(2,1)S(1)}, bf16[128,1024]{1,0:T(8,128)(2,1)S(1)}, u32[]{:S(2)}, u32[]{:S(2)}) collective-permute-start(bf16[128,1024]{1,0:T(8,128)(2,1)S(1)} %get-tuple-element.108), channel_id=1, source_target_pairs={{0,4},{8,12},{16,20},{24,28},{32,36},{40,44},{48,52},{56,60},{64,6... | collective-permute-start | bytes 786440 | tf_op jit(solution)/shard_map/ppermute | solution.py:477
  27.4 4.1 %collective-permute-start.9 = (bf16[96,1024]{1,0:T(8,128)(2,1)S(1)}, bf16[96,1024]{1,0:T(8,128)(2,1)S(1)}, u32[]{:S(2)}, u32[]{:S(2)}) collective-permute-start(bf16[96,1024]{1,0:T(8,128)(2,1)S(1)} %get-tuple-element.114), channel_id=1, source_target_pairs={{0,4},{8,12},{16,20},{24,28},{32,36},{40,44},{48,52},{56,60},{64,6... | collective-permute-start | bytes 589832 | tf_op jit(solution)/shard_map/ppermute | solution.py:477
  29.0 15.7 %collective-permute-start.8 = (bf16[256,1024]{1,0:T(8,128)(2,1)S(1)}, bf16[256,1024]{1,0:T(8,128)(2,1)S(1)}, u32[]{:S(2)}, u32[]{:S(2)}) collective-permute-start(bf16[256,1024]{1,0:T(8,128)(2,1)S(1)} %shard_map.84.after), channel_id=1, source_target_pairs={{4,8},{12,16},{20,24},{28,32},{36,40},{44,48},{52,56},{60,64},{68,... | collective-permute-start | bytes 1572872 | tf_op jit(solution)/shard_map/ppermute | solution.py:477
  31.5 11.3 %collective-permute-start.10 = (bf16[64,1024]{1,0:T(8,128)(2,1)S(1)}, bf16[64,1024]{1,0:T(8,128)(2,1)S(1)}, u32[]{:S(2)}, u32[]{:S(2)}) collective-permute-start(bf16[64,1024]{1,0:T(8,128)(2,1)S(1)} %get-tuple-element.115), channel_id=1, source_target_pairs={{0,20},{8,28},{16,36},{24,44},{32,52},{40,60},{48,68},{56,76},{64,... | collective-permute-start | bytes 393224 | tf_op jit(solution)/shard_map/ppermute | solution.py:477
  35.6 10.3 %collective-permute-start.13 = (bf16[32,1024]{1,0:T(8,128)(2,1)S(1)}, bf16[32,1024]{1,0:T(8,128)(2,1)S(1)}, u32[]{:S(2)}, u32[]{:S(2)}) collective-permute-start(bf16[32,1024]{1,0:T(8,128)(2,1)S(1)} %get-tuple-element.117), channel_id=1, source_target_pairs={{0,24},{4,28},{16,40},{20,44},{32,56},{36,60},{48,72},{52,76},{64,... | collective-permute-start | bytes 196616 | tf_op jit(solution)/shard_map/ppermute | solution.py:477
  41.3 4.6 %collective-permute-start.11 = (bf16[192,1024]{1,0:T(8,128)(2,1)S(1)}, bf16[192,1024]{1,0:T(8,128)(2,1)S(1)}, u32[]{:S(2)}, u32[]{:S(2)}) collective-permute-start(bf16[192,1024]{1,0:T(8,128)(2,1)S(1)} %get-tuple-element.116), channel_id=1, source_target_pairs={{0,4},{8,12},{16,20},{24,28},{32,36},{40,44},{48,52},{56,60},{64,6... | collective-permute-start | bytes 1179656 | tf_op jit(solution)/shard_map/ppermute | solution.py:477
  44.7 1.9 %collective-permute-start.12 = (bf16[64,1024]{1,0:T(8,128)(2,1)S(1)}, bf16[64,1024]{1,0:T(8,128)(2,1)S(1)}, u32[]{:S(2)}, u32[]{:S(2)}) collective-permute-start(bf16[64,1024]{1,0:T(8,128)(2,1)S(1)} %shard_map.87.after), channel_id=1, source_target_pairs={{0,4},{8,12},{16,20},{24,28},{32,36},{40,44},{48,52},{56,60},{64,6... | collective-permute-start | bytes 393224 | tf_op jit(solution)/shard_map/ppermute | solution.py:477

commit v7 on v6

--- a/solution.py
+++ b/solution.py
@@ -274,13 +274,12 @@
 
 
 def far_kernel(
-    q2, q3, g_ref, top, zsum, ysum, r1, got2, w3, e3, m3,
-    att, best_out, inv_out, delta_out, dq2, dq3, own2, own3, cross3, send2, send3,
+    q2, g_ref, top, zsum, ysum, r1, got2, m3,
+    att, best_out, inv_out, delta_out, grad3, drift3, dq2, own2, send,
     w2,
 ):
     core, chip = place()
     is0 = core == 0
-    holder = lax.rem(core + chip, 2) == 1
     w2[:128] = got2[...]
     w2[128:] = r1[192:]
     left_ok, right_ok = chip >= 1, chip <= 30
@@ -313,23 +312,30 @@
                 share = factors[i] * inv
                 grads[i].append(fold(share * g, i + 2))
                 drifts[i].append(fold(share * delta, i + 2))
-        for i, (q, w, e) in enumerate(((q2, w2, e2), (q3, w3, e3[h]))):
-            grad = jnp.concatenate(grads[i], axis=0).astype(BF)
-            units.append((q[:, kl], w[:, kl], w[:, vl], e, grad, jnp.concatenate(drifts[i], axis=0)))
-    results = backward(units)
-    for h in range(HEADS):
-        for i in range(2):
-            dq, dk, dv = results[2 * h + i]
-            (dq2, dq3)[i][h] = dq
-            for lanes, value in ((head(h), dk), (head(HEADS + h), dv)):
-                if i == 0:
-                    send2[:, lanes] = value[:128].astype(BF)
-                    own2[:, lanes] = value[128:]
-                else:
-                    own3[:, lanes] = value[:64]
-                    send3[:64, lanes] = value[64:128].astype(BF)
-                    cross3[:, lanes] = jnp.where(holder, value[128:160], value[160:])
-                    send3[64:, lanes] = jnp.where(holder, value[160:], value[128:160]).astype(BF)
+        grad = jnp.concatenate(grads[0], axis=0).astype(BF)
+        units.append((q2[:, kl], w2[:, kl], w2[:, vl], e2, grad, jnp.concatenate(drifts[0], axis=0)))
+        grad3[h] = jnp.concatenate(grads[1], axis=0).astype(BF)
+        drift3[h] = jnp.concatenate(drifts[1], axis=0)
+    for h, (dq, dk, dv) in enumerate(backward(units)):
+        dq2[h] = dq
+        for lanes, value in ((head(h), dk), (head(HEADS + h), dv)):
+            send[:, lanes] = value[:128].astype(BF)
+            own2[:, lanes] = value[128:]
+
+
+def third_back_kernel(q3, w3, e3, grad, drift, dq3, own3, cross3, send):
+    core, chip = place()
+    holder = lax.rem(core + chip, 2) == 1
+    units = []
+    for h in range(HEADS):
+        units.append((q3[:, head(h)], w3[:, head(h)], w3[:, head(HEADS + h)], e3[h], grad[h], drift[h]))
+    for h, (dq, dk, dv) in enumerate(backward(units)):
+        dq3[h] = dq
+        for lanes, value in ((head(h), dk), (head(HEADS + h), dv)):
+            own3[:, lanes] = value[:64]
+            send[:64, lanes] = value[64:128].astype(BF)
+            cross3[:, lanes] = jnp.where(holder, value[128:160], value[160:])
+            send[64:, lanes] = jnp.where(holder, value[160:], value[128:160]).astype(BF)
 
 
 def coarse_grad(m, best, inv, g, delta):
@@ -515,13 +521,16 @@
     w3, e3, m3, top, zsum, ysum = call(
         third_kernel, [rows(192), heads(32, BF, 192), heads(32), stat, stat, stat], flops=1 << 28
     )(q3, r2, r3, got3, top, zsum, ysum)
-    att, best, inv, delta, dq2, dq3, own2, own3, cross3, send2, send3 = call(
+    att, best, inv, delta, grad3, drift3, dq2, own2, send = call(
         far_kernel,
-        [out, stat, stat, stat, heads(64), heads(32), rows(64, F32), rows(64, F32), rows(32, F32), rows(128), rows(96)],
+        [out, stat, stat, stat, heads(32, BF), heads(32), heads(64), rows(64, F32), rows(128)],
         [rows(192)],
-    )(q2, q3, g0, top, zsum, ysum, r1, got2, w3, e3, m3)
-    got2 = swap(send2, sibling)
-    got3 = swap(send3, sibling)
+    )(q2, g0, top, zsum, ysum, r1, got2, m3)
+    got2 = swap(send, sibling)
+    dq3, own3, cross3, send = call(
+        third_back_kernel, [heads(32), rows(64, F32), rows(32, F32), rows(96)], flops=1 << 28
+    )(q3, w3, e3, grad3, drift3)
+    got3 = swap(send, sibling)
     dqo0, dqo1, d0, d1 = call(
         outer_back_kernel, [heads(128), heads(128), rows(128, F32), rows(128, F32)], flops=1 << 30
     )(q0, q1, g0, r1, outer1, eo0, eo1, mo0, mo1, best, inv, delta)

time: 48 us -> 48 us (level)
    pallas_call x1 -> x2, Pallas kernels: 1.43 us -> 1.73 us  [the longest x1 1.26 us: per_device(): call(far_kernel, [out, stat, stat, stat, heads(32, BF), heads(32), heads(...]
  transfers between devices with their start and end apart: 14 -> 14, of which waited for: 7 -> 6; matrix products, arithmetic and copies ran while one was open for 2% -> 2% of each run, Pallas kernels for 15% -> 16%
where the time goes in v7:
time: 48 us; the launch traced here: 47.7 us
  starting transfers between devices  26.3 us (55%)
  Pallas kernels  10.5 us (22%)
  waiting for transfers between devices  9 us (19%)
  other arithmetic  1.08 us (2%)
  between operations  0.88 us (2%)
    ppermute x14, starting transfers between devices, swap(): return lax.ppermute(value, 'seq', pairs + [(b, a) for a, b in pairs])  26.3 us
    ppermute x14, waiting for transfers between devices, swap(): return lax.ppermute(value, 'seq', pairs + [(b, a) for a, b in pairs])  9 us
    pallas_call x1, Pallas kernels, per_device(): call(rest_kernel, [out, out, rows(256, F32), rows(192)], [stat], flops=1...  2.69 us
    pallas_call x1, Pallas kernels, per_device(): call(local_kernel, [out, out, ((128, D), BF), ((64, D), BF), ((32, D), BF...  1.6 us
    pallas_call x1, Pallas kernels, per_device(): call(far_kernel, [out, stat, stat, stat, heads(32, BF), heads(32), heads(...  1.26 us
    pallas_call x1, Pallas kernels, per_device(): call(final_kernel, [out, out], [rows(256), pltpu.SemaphoreType.DMA((2 * H...  1.18 us
    concatenate x1, other arithmetic, per_device(): jnp.concatenate([key_rows, value_rows], axis=1)  1.08 us
  transfers between devices with their start and end apart: 14, of which 6 were waited for; matrix products, arithmetic and copies ran while one was open for 2% of the time, Pallas kernels for 16%

profile of v7, /device:TPU:11, one launch (start us, length us, event | category | flops | bytes accessed | tf_op | source)
XLA Modules:
  0.0 47.7 jit_solution(5660164321537645425)
XLA Ops:
  0.6 0.8 %collective-permute-start = (bf16[256,512]{1,0:T(8,128)(2,1)}, bf16[256,512]{1,0:T(8,128)(2,1)S(1)}, u32[]{:S(2)}, u32[]{:S(2)}) collective-permute-start(bf16[256,512]{1,0:T(8,128)(2,1)} %param.5), channel_id=1, source_target_pairs={{0,4},{8,12},{16,20},{24,28},{32,36},{40,44},{48,52},{56,60},{64,6... | collective-permute-start | bytes 786440 | tf_op jit(solution)/shard_map/ppermute | solution.py:483
  1.5 1.1 %pad_maximum_fusion.raw = bf16[256,1024]{1,0:T(8,128)(2,1)S(1)} fusion(bf16[256,512]{1,0:T(8,128)(2,1)} %param.6, bf16[256,512]{1,0:T(8,128)(2,1)} %param.5), kind=kLoop, calls=%fused_computation | loop fusion | flops 1048576 | bytes 1048576 | tf_op jit(solution)/shard_map/concatenate | solution.py:496
  2.6 0.3 shard_map.75
  2.9 0.2 collective-permute-done.1.vs
  3.1 0.4 shard_map.76
  3.5 8.1 %collective-permute-start.2 = (bf16[64,1024]{1,0:T(8,128)(2,1)S(1)}, bf16[64,1024]{1,0:T(8,128)(2,1)S(1)}, u32[]{:S(2)}, u32[]{:S(2)}) collective-permute-start(bf16[64,1024]{1,0:T(8,128)(2,1)S(1)} %get-tuple-element.79), channel_id=1, source_target_pairs={{0,20},{8,28},{16,36},{24,44},{32,52},{40,60},{48,68},{56,76},{64,... | collective-permute-start | bytes 393224 | tf_op jit(solution)/shard_map/ppermute | solution.py:483
  11.6 1.9 %collective-permute-start.5 = (bf16[256,1024]{1,0:T(8,128)(2,1)S(1)}, bf16[256,1024]{1,0:T(8,128)(2,1)S(1)}, u32[]{:S(2)}, u32[]{:S(2)}) collective-permute-start(bf16[256,1024]{1,0:T(8,128)(2,1)S(1)} %get-tuple-element.81), channel_id=1, source_target_pairs={{4,8},{12,16},{20,24},{28,32},{36,40},{44,48},{52,56},{60,64},{68,... | collective-permute-start | bytes 1572872 | tf_op jit(solution)/shard_map/ppermute | solution.py:483
  13.5 1.4 %collective-permute-done.2.r2 = bf16[64,1024]{1,0:T(8,128)(2,1)S(1)} collective-permute-done((bf16[64,1024]{1,0:T(8,128)(2,1)S(1)}, bf16[64,1024]{1,0:T(8,128)(2,1)S(1)}, u32[]{:S(2)}, u32[]{:S(2)}) %collective-permute-start.2) | collective-permute-done | bytes 131104 | tf_op jit(solution)/shard_map/ppermute | solution.py:483
  14.9 2.3 %collective-permute-start.3 = (bf16[64,1024]{1,0:T(8,128)(2,1)S(1)}, bf16[64,1024]{1,0:T(8,128)(2,1)S(1)}, u32[]{:S(2)}, u32[]{:S(2)}) collective-permute-start(bf16[64,1024]{1,0:T(8,128)(2,1)S(1)} %collective-permute-done.2.r2), channel_id=1, source_target_pairs={{4,8},{20,24},{36,40},{52,56},{68,72},{84,88},{100,104},{116,120},... | collective-permute-start | bytes 393224 | tf_op jit(solution)/shard_map/ppermute | solution.py:483
  17.2 1.6 %shard_map.77 = (bf16[256,512]{1,0:T(8,128)(2,1)S(1)}, bf16[256,512]{1,0:T(8,128)(2,1)S(1)}, bf16[128,512]{1,0:T(8,128)(2,1)S(1)}, bf16[64,512]{1,0:T(8,128)(2,1...) custom-call(bf16[256,512]{1,0:T(8,128)(2,1)S(1)} %copy-done, ...), custom_call_target="tpu_custom_call" | custom-call | flops 8589934592 | bytes 1048576 | tf_op jit(solution)/shard_map/pallas_call | solution.py:504
  18.8 4.7 %collective-permute-done.3.r3 = bf16[64,1024]{1,0:T(8,128)(2,1)S(1)} collective-permute-done((bf16[64,1024]{1,0:T(8,128)(2,1)S(1)}, bf16[64,1024]{1,0:T(8,128)(2,1)S(1)}, u32[]{:S(2)}, u32[]{:S(2)}) %collective-permute-start.3) | collective-permute-done | bytes 131104 | tf_op jit(solution)/shard_map/ppermute | solution.py:483
  23.6 0.1 shard_map.79
  23.8 0.6 %collective-permute-start.6 = (bf16[128,1024]{1,0:T(8,128)(2,1)S(1)}, bf16[128,1024]{1,0:T(8,128)(2,1)S(1)}, u32[]{:S(2)}, u32[]{:S(2)}) collective-permute-start(bf16[128,1024]{1,0:T(8,128)(2,1)S(1)} %get-tuple-element.91), channel_id=1, source_target_pairs={{0,4},{8,12},{16,20},{24,28},{32,36},{40,44},{48,52},{56,60},{64,6... | collective-permute-start | bytes 786440 | tf_op jit(solution)/shard_map/ppermute | solution.py:483
  24.3 0.8 %shard_map.80 = (f32[4,256,128]{2,1,0:T(8,128)S(1)}, f32[4,256,128]{2,1,0:T(8,128)S(1)}, f32[4,256,128]{2,1,0:T(8,128)S(1)}, bf16[4,128,128]{2,1,0:T(8,128)(2,1)...) custom-call(bf16[256,512]{1,0:T(8,128)(2,1)S(1)} %get-tuple-element.69.q0, ...), custom_call_target="tpu_custom_call" | custom-call | flops 1073741824 | bytes 1048576 | tf_op jit(solution)/shard_map/pallas_call | solution.py:515
  25.2 0.6 %shard_map.81 = (bf16[192,1024]{1,0:T(8,128)(2,1)S(1)}, bf16[4,32,192]{2,1,0:T(8,128)(2,1)S(1)}, f32[4,32,128]{2,1,0:T(8,128)S(1)}, f32[4,256,128]{2,1,0:T(8,128...) custom-call(bf16[32,512]{1,0:T(8,128)(2,1)S(1)} %get-tuple-element.78.q3, ...), custom_call_target="tpu_custom_call" | custom-call | flops 268435456 | bytes 1048576 | tf_op jit(solution)/shard_map/pallas_call | solution.py:521
  25.8 1.3 %shard_map.82 = (bf16[256,512]{1,0:T(8,128)(2,1)S(1)}, f32[4,256,128]{2,1,0:T(8,128)S(1)}, f32[4,256,128]{2,1,0:T(8,128)S(1)}, f32[4,256,128]{2,1,0:T(8,128)S(1)...) custom-call(bf16[64,512]{1,0:T(8,128)(2,1)S(1)} %get-tuple-element.7, ...), custom_call_target="tpu_custom_call" | custom-call | tf_op jit(solution)/shard_map/pallas_call | solution.py:524
  27.0 0.2 collective-permute-start.7
  27.2 0.5 shard_map.84
  27.7 0.5 %collective-permute-start.9 = (bf16[96,1024]{1,0:T(8,128)(2,1)S(1)}, bf16[96,1024]{1,0:T(8,128)(2,1)S(1)}, u32[]{:S(2)}, u32[]{:S(2)}) collective-permute-start(bf16[96,1024]{1,0:T(8,128)(2,1)S(1)} %get-tuple-element.118), channel_id=1, source_target_pairs={{0,4},{8,12},{16,20},{24,28},{32,36},{40,44},{48,52},{56,60},{64,6... | collective-permute-start | bytes 589832 | tf_op jit(solution)/shard_map/ppermute | solution.py:483
  28.2 0.6 %shard_map.83 = (f32[4,128,128]{2,1,0:T(8,128)S(1)}, f32[4,128,128]{2,1,0:T(8,128)S(1)}, f32[128,1024]{1,0:T(8,128)S(1)}, f32[128,1024]{1,0:T(8,128)S(1)}) custom-call(bf16[256,512]{1,0:T(8,128)(2,1)S(1)} %get-tuple-element.69.q0, bf16[128,512]{1,0:T(8,128)(2,1)S(1)} %get-tuple-element.70.q1, bf16[256,512]{1,0:T(8,128)(2,1)S(1)} %get-tuple-element.71.g_ref, ...), custom_call_target="tpu_custom_call" | custom-call | flops 1073741824 | bytes 1048576 | tf_op jit(solution)/shard_map/pallas_call | solution.py:534
  28.8 0.2 shard_map.85.after
  29.0 2.5 %collective-permute-start.8 = (bf16[256,1024]{1,0:T(8,128)(2,1)S(1)}, bf16[256,1024]{1,0:T(8,128)(2,1)S(1)}, u32[]{:S(2)}, u32[]{:S(2)}) collective-permute-start(bf16[256,1024]{1,0:T(8,128)(2,1)S(1)} %shard_map.85.after), channel_id=1, source_target_pairs={{4,8},{12,16},{20,24},{28,32},{36,40},{44,48},{52,56},{60,64},{68,... | collective-permute-start | bytes 1572872 | tf_op jit(solution)/shard_map/ppermute | solution.py:483
  31.5 4.0 %collective-permute-start.10 = (bf16[64,1024]{1,0:T(8,128)(2,1)S(1)}, bf16[64,1024]{1,0:T(8,128)(2,1)S(1)}, u32[]{:S(2)}, u32[]{:S(2)}) collective-permute-start(bf16[64,1024]{1,0:T(8,128)(2,1)S(1)} %get-tuple-element.119), channel_id=1, source_target_pairs={{0,20},{8,28},{16,36},{24,44},{32,52},{40,60},{48,68},{56,76},{64,... | collective-permute-start | bytes 393224 | tf_op jit(solution)/shard_map/ppermute | solution.py:483
  35.5 3.1 %collective-permute-start.13 = (bf16[32,1024]{1,0:T(8,128)(2,1)S(1)}, bf16[32,1024]{1,0:T(8,128)(2,1)S(1)}, u32[]{:S(2)}, u32[]{:S(2)}) collective-permute-start(bf16[32,1024]{1,0:T(8,128)(2,1)S(1)} %get-tuple-element.121), channel_id=1, source_target_pairs={{0,24},{4,28},{16,40},{20,44},{32,56},{36,60},{48,72},{52,76},{64,... | collective-permute-start | bytes 196616 | tf_op jit(solution)/shard_map/ppermute | solution.py:483
  38.6 2.7 %shard_map.86 = (bf16[256,512]{1,0:T(8,128)(2,1)}, bf16[256,512]{1,0:T(8,128)(2,1)}, f32[256,1024]{1,0:T(8,128)S(1)}, bf16[192,1024]{1,0:T(8,128)(2,1)S(1)}) custom-call(bf16[256,512]{1,0:T(8,128)(2,1)S(1)} %get-tuple-element.69.q0, bf16[128,512]{1,0:T(8,128)(2,1)S(1)} %get-tuple-element.70.q1, bf16[256,512]{1,0:T(8,128)(2,1)S(1)} %get-tuple-element.71.g_ref, ...), custom_call_target="tpu_custom_call" | custom-call | flops 536870912 | bytes 1048576 | tf_op jit(solution)/shard_map/pallas_call | solution.py:542
  41.3 1.3 %collective-permute-start.11 = (bf16[192,1024]{1,0:T(8,128)(2,1)S(1)}, bf16[192,1024]{1,0:T(8,128)(2,1)S(1)}, u32[]{:S(2)}, u32[]{:S(2)}) collective-permute-start(bf16[192,1024]{1,0:T(8,128)(2,1)S(1)} %get-tuple-element.120), channel_id=1, source_target_pairs={{0,4},{8,12},{16,20},{24,28},{32,36},{40,44},{48,52},{56,60},{64,6... | collective-permute-start | bytes 1179656 | tf_op jit(solution)/shard_map/ppermute | solution.py:483
  42.6 0.3 collective-permute-done.10.r2
  42.9 1.7 %collective-permute-done.8.r1 = bf16[256,1024]{1,0:T(8,128)(2,1)S(1)} collective-permute-done((bf16[256,1024]{1,0:T(8,128)(2,1)S(1)}, bf16[256,1024]{1,0:T(8,128)(2,1)S(1)}, u32[]{:S(2)}, u32[]{:S(2)}) %collective-permute-start.8) | collective-permute-done | bytes 524320 | tf_op jit(solution)/shard_map/ppermute | solution.py:483
  44.7 0.9 %collective-permute-start.12 = (bf16[64,1024]{1,0:T(8,128)(2,1)S(1)}, bf16[64,1024]{1,0:T(8,128)(2,1)S(1)}, u32[]{:S(2)}, u32[]{:S(2)}) collective-permute-start(bf16[64,1024]{1,0:T(8,128)(2,1)S(1)} %shard_map.88.after), channel_id=1, source_target_pairs={{0,4},{8,12},{16,20},{24,28},{32,36},{40,44},{48,52},{56,60},{64,6... | collective-permute-start | bytes 393224 | tf_op jit(solution)/shard_map/ppermute | solution.py:483
  45.6 0.2 shard_map.89.after.acc
  45.9 0.7 %collective-permute-done.12.got = bf16[64,1024]{1,0:T(8,128)(2,1)S(1)} collective-permute-done((bf16[64,1024]{1,0:T(8,128)(2,1)S(1)}, bf16[64,1024]{1,0:T(8,128)(2,1)S(1)}, u32[]{:S(2)}, u32[]{:S(2)}) %collective-permute-start.12) | collective-permute-done | bytes 131104 | tf_op jit(solution)/shard_map/ppermute | solution.py:483
  46.6 1.2 %shard_map.91 = (bf16[256,512]{1,0:T(8,128)(2,1)}, bf16[256,512]{1,0:T(8,128)(2,1)}) custom-call(f32[256,1024]{1,0:T(8,128)S(1)} %shard_map.89.after.acc, bf16[192,1024]{1,0:T(8,128)(2,1)S(1)} %collective-permute-done.11.near, bf16[64,1024]{1,0:T(8,128)(2,1)S(1)} %collective-permute-done.12.got, f32[64,1024]{1,0:T(8,128)S(1)} %shard_map.90.cross), custom_call_target="tpu_custom_call" | custom-call | tf_op jit(solution)/shard_map/pallas_call | solution.py:554
  (18 shorter events, 0.3 us)
Async XLA Ops:
  0.6 2.3 %collective-permute-start = (bf16[256,512]{1,0:T(8,128)(2,1)}, bf16[256,512]{1,0:T(8,128)(2,1)S(1)}, u32[]{:S(2)}, u32[]{:S(2)}) collective-permute-start(bf16[256,512]{1,0:T(8,128)(2,1)} %param.5), channel_id=1, source_target_pairs={{0,4},{8,12},{16,20},{24,28},{32,36},{40,44},{48,52},{56,60},{64,6... | collective-permute-start | bytes 786440 | tf_op jit(solution)/shard_map/ppermute | solution.py:483
  1.4 1.7 %collective-permute-start.1 = (bf16[256,512]{1,0:T(8,128)(2,1)}, bf16[256,512]{1,0:T(8,128)(2,1)S(1)}, u32[]{:S(2)}, u32[]{:S(2)}) collective-permute-start(bf16[256,512]{1,0:T(8,128)(2,1)} %param.6), channel_id=1, source_target_pairs={{0,4},{8,12},{16,20},{24,28},{32,36},{40,44},{48,52},{56,60},{64,6... | collective-permute-start | bytes 786440 | tf_op jit(solution)/shard_map/ppermute | solution.py:483
  3.1 14.0 %copy-start = (bf16[256,512]{1,0:T(8,128)(2,1)S(1)}, bf16[256,512]{1,0:T(8,128)(2,1)}, u32[]{:S(2)}) copy-start(bf16[256,512]{1,0:T(8,128)(2,1)} %q_ref.1) | copy-start | bytes 786436
  3.1 14.0 %copy-start.1 = (bf16[256,512]{1,0:T(8,128)(2,1)S(1)}, bf16[256,512]{1,0:T(8,128)(2,1)}, u32[]{:S(2)}) copy-start(bf16[256,512]{1,0:T(8,128)(2,1)} %g_ref.1) | copy-start | bytes 786436
  3.5 11.4 %collective-permute-start.2 = (bf16[64,1024]{1,0:T(8,128)(2,1)S(1)}, bf16[64,1024]{1,0:T(8,128)(2,1)S(1)}, u32[]{:S(2)}, u32[]{:S(2)}) collective-permute-start(bf16[64,1024]{1,0:T(8,128)(2,1)S(1)} %get-tuple-element.79), channel_id=1, source_target_pairs={{0,20},{8,28},{16,36},{24,44},{32,52},{40,60},{48,68},{56,76},{64,... | collective-permute-start | bytes 393224 | tf_op jit(solution)/shard_map/ppermute | solution.py:483
  11.6 12.0 %collective-permute-start.5 = (bf16[256,1024]{1,0:T(8,128)(2,1)S(1)}, bf16[256,1024]{1,0:T(8,128)(2,1)S(1)}, u32[]{:S(2)}, u32[]{:S(2)}) collective-permute-start(bf16[256,1024]{1,0:T(8,128)(2,1)S(1)} %get-tuple-element.81), channel_id=1, source_target_pairs={{4,8},{12,16},{20,24},{28,32},{36,40},{44,48},{52,56},{60,64},{68,... | collective-permute-start | bytes 1572872 | tf_op jit(solution)/shard_map/ppermute | solution.py:483
  14.9 8.6 %collective-permute-start.3 = (bf16[64,1024]{1,0:T(8,128)(2,1)S(1)}, bf16[64,1024]{1,0:T(8,128)(2,1)S(1)}, u32[]{:S(2)}, u32[]{:S(2)}) collective-permute-start(bf16[64,1024]{1,0:T(8,128)(2,1)S(1)} %collective-permute-done.2.r2), channel_id=1, source_target_pairs={{4,8},{20,24},{36,40},{52,56},{68,72},{84,88},{100,104},{116,120},... | collective-permute-start | bytes 393224 | tf_op jit(solution)/shard_map/ppermute | solution.py:483
  23.5 1.6 %collective-permute-start.4 = (bf16[128,1024]{1,0:T(8,128)(2,1)S(1)}, bf16[128,1024]{1,0:T(8,128)(2,1)S(1)}, u32[]{:S(2)}, u32[]{:S(2)}) collective-permute-start(bf16[128,1024]{1,0:T(8,128)(2,1)S(1)} %shard_map.78.after), channel_id=1, source_target_pairs={{0,4},{8,12},{16,20},{24,28},{32,36},{40,44},{48,52},{56,60},{64,6... | collective-permute-start | bytes 786440 | tf_op jit(solution)/shard_map/ppermute | solution.py:483
  23.8 2.0 %collective-permute-start.6 = (bf16[128,1024]{1,0:T(8,128)(2,1)S(1)}, bf16[128,1024]{1,0:T(8,128)(2,1)S(1)}, u32[]{:S(2)}, u32[]{:S(2)}) collective-permute-start(bf16[128,1024]{1,0:T(8,128)(2,1)S(1)} %get-tuple-element.91), channel_id=1, source_target_pairs={{0,4},{8,12},{16,20},{24,28},{32,36},{40,44},{48,52},{56,60},{64,6... | collective-permute-start | bytes 786440 | tf_op jit(solution)/shard_map/ppermute | solution.py:483
  27.0 1.7 %collective-permute-start.7 = (bf16[128,1024]{1,0:T(8,128)(2,1)S(1)}, bf16[128,1024]{1,0:T(8,128)(2,1)S(1)}, u32[]{:S(2)}, u32[]{:S(2)}) collective-permute-start(bf16[128,1024]{1,0:T(8,128)(2,1)S(1)} %get-tuple-element.112), channel_id=1, source_target_pairs={{0,4},{8,12},{16,20},{24,28},{32,36},{40,44},{48,52},{56,60},{64,6... | collective-permute-start | bytes 786440 | tf_op jit(solution)/shard_map/ppermute | solution.py:483
  27.7 3.7 %collective-permute-start.9 = (bf16[96,1024]{1,0:T(8,128)(2,1)S(1)}, bf16[96,1024]{1,0:T(8,128)(2,1)S(1)}, u32[]{:S(2)}, u32[]{:S(2)}) collective-permute-start(bf16[96,1024]{1,0:T(8,128)(2,1)S(1)} %get-tuple-element.118), channel_id=1, source_target_pairs={{0,4},{8,12},{16,20},{24,28},{32,36},{40,44},{48,52},{56,60},{64,6... | collective-permute-start | bytes 589832 | tf_op jit(solution)/shard_map/ppermute | solution.py:483
  29.0 15.7 %collective-permute-start.8 = (bf16[256,1024]{1,0:T(8,128)(2,1)S(1)}, bf16[256,1024]{1,0:T(8,128)(2,1)S(1)}, u32[]{:S(2)}, u32[]{:S(2)}) collective-permute-start(bf16[256,1024]{1,0:T(8,128)(2,1)S(1)} %shard_map.85.after), channel_id=1, source_target_pairs={{4,8},{12,16},{20,24},{28,32},{36,40},{44,48},{52,56},{60,64},{68,... | collective-permute-start | bytes 1572872 | tf_op jit(solution)/shard_map/ppermute | solution.py:483
  31.5 11.4 %collective-permute-start.10 = (bf16[64,1024]{1,0:T(8,128)(2,1)S(1)}, bf16[64,1024]{1,0:T(8,128)(2,1)S(1)}, u32[]{:S(2)}, u32[]{:S(2)}) collective-permute-start(bf16[64,1024]{1,0:T(8,128)(2,1)S(1)} %get-tuple-element.119), channel_id=1, source_target_pairs={{0,20},{8,28},{16,36},{24,44},{32,52},{40,60},{48,68},{56,76},{64,... | collective-permute-start | bytes 393224 | tf_op jit(solution)/shard_map/ppermute | solution.py:483
  35.5 10.3 %collective-permute-start.13 = (bf16[32,1024]{1,0:T(8,128)(2,1)S(1)}, bf16[32,1024]{1,0:T(8,128)(2,1)S(1)}, u32[]{:S(2)}, u32[]{:S(2)}) collective-permute-start(bf16[32,1024]{1,0:T(8,128)(2,1)S(1)} %get-tuple-element.121), channel_id=1, source_target_pairs={{0,24},{4,28},{16,40},{20,44},{32,56},{36,60},{48,72},{52,76},{64,... | collective-permute-start | bytes 196616 | tf_op jit(solution)/shard_map/ppermute | solution.py:483
  41.3 4.6 %collective-permute-start.11 = (bf16[192,1024]{1,0:T(8,128)(2,1)S(1)}, bf16[192,1024]{1,0:T(8,128)(2,1)S(1)}, u32[]{:S(2)}, u32[]{:S(2)}) collective-permute-start(bf16[192,1024]{1,0:T(8,128)(2,1)S(1)} %get-tuple-element.120), channel_id=1, source_target_pairs={{0,4},{8,12},{16,20},{24,28},{32,36},{40,44},{48,52},{56,60},{64,6... | collective-permute-start | bytes 1179656 | tf_op jit(solution)/shard_map/ppermute | solution.py:483
  44.7 1.9 %collective-permute-start.12 = (bf16[64,1024]{1,0:T(8,128)(2,1)S(1)}, bf16[64,1024]{1,0:T(8,128)(2,1)S(1)}, u32[]{:S(2)}, u32[]{:S(2)}) collective-permute-start(bf16[64,1024]{1,0:T(8,128)(2,1)S(1)} %shard_map.88.after), channel_id=1, source_target_pairs={{0,4},{8,12},{16,20},{24,28},{32,36},{40,44},{48,52},{56,60},{64,6... | collective-permute-start | bytes 393224 | tf_op jit(solution)/shard_map/ppermute | solution.py:483

commit v8 on v7

--- a/solution.py
+++ b/solution.py
@@ -111,17 +111,17 @@
     mixes = [nn(eb, v) for eb, (_, _, v, _) in zip(rounded, units)]
     sums = [jnp.sum(e, axis=1, keepdims=True) for e in weights]
     return [
-        (eb, lanes128(peak * EXP_SCALE), lanes128(den), mix)
-        for eb, peak, den, mix in zip(rounded, peaks, sums, mixes)
+        (e, lanes128(peak * EXP_SCALE), lanes128(den), mix)
+        for e, peak, den, mix in zip(weights, peaks, sums, mixes)
     ]
 
 
 def backward(units):
     inners = [nt(grad, v) for _, _, v, _, grad, _ in units]
-    dvs = [tn(eb, grad) for _, _, _, eb, grad, _ in units]
+    dvs = [tn(e.astype(BF), grad) for _, _, _, e, grad, _ in units]
     dscores = [
-        (eb.astype(F32) * (inner - wide(drift, eb.shape[1]))).astype(BF)
-        for inner, (_, _, _, eb, _, drift) in zip(inners, units)
+        (e * (inner - wide(drift, e.shape[1]))).astype(BF)
+        for inner, (_, _, _, e, _, drift) in zip(inners, units)
     ]
     dqs = [nn(dscore, k) * SCALE for dscore, (_, k, _, _, _, _) in zip(dscores, units)]
     dks = [tn(dscore, q) * SCALE for dscore, (q, _, _, _, _, _) in zip(dscores, units)]
@@ -504,7 +504,7 @@
     q0, g0, q1, q2, q3, win, e0, e1, m0, m1, top, zsum, ysum = call(
         local_kernel,
         [out, out, ((128, D), BF), ((64, D), BF), ((32, D), BF), rows(384)]
-        + [heads(256, BF, 384), heads(128, BF), stat, heads(128), stat, stat, stat],
+        + [heads(256, F32, 384), heads(128), stat, heads(128), stat, stat, stat],
         [heads(128), heads(128)],
         flops=1 << 33,
     )(query, out_grad, kv, near, s1)
@@ -514,12 +514,12 @@
     got2 = swap(send, sibling)
     top, zsum, ysum, eo0, eo1, mo0, mo1 = call(
         outer_kernel,
-        [stat] * 3 + [heads(128, BF), heads(128, BF), heads(128), heads(128)],
+        [stat] * 3 + [heads(128), heads(128), heads(128), heads(128)],
         [heads(128), heads(128)],
         flops=1 << 30,
     )(q0, q1, r1, outer1, top, zsum, ysum)
     w3, e3, m3, top, zsum, ysum = call(
-        third_kernel, [rows(192), heads(32, BF, 192), heads(32), stat, stat, stat], flops=1 << 28
+        third_kernel, [rows(192), heads(32, F32, 192), heads(32), stat, stat, stat], flops=1 << 28
     )(q3, r2, r3, got3, top, zsum, ysum)
     att, best, inv, delta, grad3, drift3, dq2, own2, send = call(
         far_kernel,

time: 48 us -> 48 us (level)
  no operation moved by 1% of the time
where the time goes in v8:
time: 48 us; the launch traced here: 47.8 us
  starting transfers between devices  26.3 us (55%)
  Pallas kernels  10.5 us (22%)
  waiting for transfers between devices  9.04 us (19%)
  other arithmetic  1.08 us (2%)
  between operations  0.89 us (2%)
    ppermute x14, starting transfers between devices, swap(): return lax.ppermute(value, 'seq', pairs + [(b, a) for a, b in pairs])  26.3 us
    ppermute x14, waiting for transfers between devices, swap(): return lax.ppermute(value, 'seq', pairs + [(b, a) for a, b in pairs])  9.04 us
    pallas_call x1, Pallas kernels, per_device(): call(rest_kernel, [out, out, rows(256, F32), rows(192)], [stat], flops=1...  2.67 us
    pallas_call x1, Pallas kernels, per_device(): call(local_kernel, [out, out, ((128, D), BF), ((64, D), BF), ((32, D), BF...  1.59 us
    pallas_call x1, Pallas kernels, per_device(): call(far_kernel, [out, stat, stat, stat, heads(32, BF), heads(32), heads(...  1.25 us
    pallas_call x1, Pallas kernels, per_device(): call(final_kernel, [out, out], [rows(256), pltpu.SemaphoreType.DMA((2 * H...  1.18 us
    concatenate x1, other arithmetic, per_device(): jnp.concatenate([key_rows, value_rows], axis=1)  1.08 us
  transfers between devices with their start and end apart: 14, of which 6 were waited for; matrix products, arithmetic and copies ran while one was open for 2% of the time, Pallas kernels for 16%

profile of v8, /device:TPU:11, one launch (start us, length us, event | category | flops | bytes accessed | tf_op | source)
XLA Modules:
  0.0 47.8 jit_solution(6695109263107222679)
XLA Ops:
  0.7 0.8 %collective-permute-start = (bf16[256,512]{1,0:T(8,128)(2,1)}, bf16[256,512]{1,0:T(8,128)(2,1)S(1)}, u32[]{:S(2)}, u32[]{:S(2)}) collective-permute-start(bf16[256,512]{1,0:T(8,128)(2,1)} %param.5), channel_id=1, source_target_pairs={{0,4},{8,12},{16,20},{24,28},{32,36},{40,44},{48,52},{56,60},{64,6... | collective-permute-start | bytes 786440 | tf_op jit(solution)/shard_map/ppermute | solution.py:483
  1.5 1.1 %pad_maximum_fusion.raw = bf16[256,1024]{1,0:T(8,128)(2,1)S(1)} fusion(bf16[256,512]{1,0:T(8,128)(2,1)} %param.6, bf16[256,512]{1,0:T(8,128)(2,1)} %param.5), kind=kLoop, calls=%fused_computation | loop fusion | flops 1048576 | bytes 1048576 | tf_op jit(solution)/shard_map/concatenate | solution.py:496
  2.6 0.3 shard_map.75
  2.9 0.2 collective-permute-done.1.vs
  3.2 0.4 shard_map.76
  3.5 8.1 %collective-permute-start.2 = (bf16[64,1024]{1,0:T(8,128)(2,1)S(1)}, bf16[64,1024]{1,0:T(8,128)(2,1)S(1)}, u32[]{:S(2)}, u32[]{:S(2)}) collective-permute-start(bf16[64,1024]{1,0:T(8,128)(2,1)S(1)} %get-tuple-element.79), channel_id=1, source_target_pairs={{0,20},{8,28},{16,36},{24,44},{32,52},{40,60},{48,68},{56,76},{64,... | collective-permute-start | bytes 393224 | tf_op jit(solution)/shard_map/ppermute | solution.py:483
  11.6 1.9 %collective-permute-start.5 = (bf16[256,1024]{1,0:T(8,128)(2,1)S(1)}, bf16[256,1024]{1,0:T(8,128)(2,1)S(1)}, u32[]{:S(2)}, u32[]{:S(2)}) collective-permute-start(bf16[256,1024]{1,0:T(8,128)(2,1)S(1)} %get-tuple-element.81), channel_id=1, source_target_pairs={{4,8},{12,16},{20,24},{28,32},{36,40},{44,48},{52,56},{60,64},{68,... | collective-permute-start | bytes 1572872 | tf_op jit(solution)/shard_map/ppermute | solution.py:483
  13.5 1.4 %collective-permute-done.2.r2 = bf16[64,1024]{1,0:T(8,128)(2,1)S(1)} collective-permute-done((bf16[64,1024]{1,0:T(8,128)(2,1)S(1)}, bf16[64,1024]{1,0:T(8,128)(2,1)S(1)}, u32[]{:S(2)}, u32[]{:S(2)}) %collective-permute-start.2) | collective-permute-done | bytes 131104 | tf_op jit(solution)/shard_map/ppermute | solution.py:483
  14.9 2.3 %collective-permute-start.3 = (bf16[64,1024]{1,0:T(8,128)(2,1)S(1)}, bf16[64,1024]{1,0:T(8,128)(2,1)S(1)}, u32[]{:S(2)}, u32[]{:S(2)}) collective-permute-start(bf16[64,1024]{1,0:T(8,128)(2,1)S(1)} %collective-permute-done.2.r2), channel_id=1, source_target_pairs={{4,8},{20,24},{36,40},{52,56},{68,72},{84,88},{100,104},{116,120},... | collective-permute-start | bytes 393224 | tf_op jit(solution)/shard_map/ppermute | solution.py:483
  17.2 1.6 %shard_map.77 = (bf16[256,512]{1,0:T(8,128)(2,1)S(1)}, bf16[256,512]{1,0:T(8,128)(2,1)S(1)}, bf16[128,512]{1,0:T(8,128)(2,1)S(1)}, bf16[64,512]{1,0:T(8,128)(2,1...) custom-call(bf16[256,512]{1,0:T(8,128)(2,1)S(1)} %copy-done, ...), custom_call_target="tpu_custom_call" | custom-call | flops 8589934592 | bytes 1048576 | tf_op jit(solution)/shard_map/pallas_call | solution.py:504
  18.8 4.7 %collective-permute-done.3.r3 = bf16[64,1024]{1,0:T(8,128)(2,1)S(1)} collective-permute-done((bf16[64,1024]{1,0:T(8,128)(2,1)S(1)}, bf16[64,1024]{1,0:T(8,128)(2,1)S(1)}, u32[]{:S(2)}, u32[]{:S(2)}) %collective-permute-start.3) | collective-permute-done | bytes 131104 | tf_op jit(solution)/shard_map/ppermute | solution.py:483
  23.6 0.1 shard_map.79
  23.8 0.6 %collective-permute-start.6 = (bf16[128,1024]{1,0:T(8,128)(2,1)S(1)}, bf16[128,1024]{1,0:T(8,128)(2,1)S(1)}, u32[]{:S(2)}, u32[]{:S(2)}) collective-permute-start(bf16[128,1024]{1,0:T(8,128)(2,1)S(1)} %get-tuple-element.91), channel_id=1, source_target_pairs={{0,4},{8,12},{16,20},{24,28},{32,36},{40,44},{48,52},{56,60},{64,6... | collective-permute-start | bytes 786440 | tf_op jit(solution)/shard_map/ppermute | solution.py:483
  24.4 0.8 %shard_map.80 = (f32[4,256,128]{2,1,0:T(8,128)S(1)}, f32[4,256,128]{2,1,0:T(8,128)S(1)}, f32[4,256,128]{2,1,0:T(8,128)S(1)}, f32[4,128,128]{2,1,0:T(8,128)S(1)},...) custom-call(bf16[256,512]{1,0:T(8,128)(2,1)S(1)} %get-tuple-element.69.q0, ...), custom_call_target="tpu_custom_call" | custom-call | flops 1073741824 | bytes 1048576 | tf_op jit(solution)/shard_map/pallas_call | solution.py:515
  25.2 0.6 %shard_map.81 = (bf16[192,1024]{1,0:T(8,128)(2,1)S(1)}, f32[4,32,192]{2,1,0:T(8,128)S(1)}, f32[4,32,128]{2,1,0:T(8,128)S(1)}, f32[4,256,128]{2,1,0:T(8,128)S(1)}...) custom-call(bf16[32,512]{1,0:T(8,128)(2,1)S(1)} %get-tuple-element.78.q3, ...), custom_call_target="tpu_custom_call" | custom-call | flops 268435456 | bytes 1048576 | tf_op jit(solution)/shard_map/pallas_call | solution.py:521
  25.8 1.3 %shard_map.82 = (bf16[256,512]{1,0:T(8,128)(2,1)S(1)}, f32[4,256,128]{2,1,0:T(8,128)S(1)}, f32[4,256,128]{2,1,0:T(8,128)S(1)}, f32[4,256,128]{2,1,0:T(8,128)S(1)...) custom-call(bf16[64,512]{1,0:T(8,128)(2,1)S(1)} %get-tuple-element.7, ...), custom_call_target="tpu_custom_call" | custom-call | tf_op jit(solution)/shard_map/pallas_call | solution.py:524
  27.0 0.2 collective-permute-start.7
  27.2 0.5 shard_map.84
  27.7 0.5 %collective-permute-start.9 = (bf16[96,1024]{1,0:T(8,128)(2,1)S(1)}, bf16[96,1024]{1,0:T(8,128)(2,1)S(1)}, u32[]{:S(2)}, u32[]{:S(2)}) collective-permute-start(bf16[96,1024]{1,0:T(8,128)(2,1)S(1)} %get-tuple-element.118), channel_id=1, source_target_pairs={{0,4},{8,12},{16,20},{24,28},{32,36},{40,44},{48,52},{56,60},{64,6... | collective-permute-start | bytes 589832 | tf_op jit(solution)/shard_map/ppermute | solution.py:483
  28.2 0.6 %shard_map.83 = (f32[4,128,128]{2,1,0:T(8,128)S(1)}, f32[4,128,128]{2,1,0:T(8,128)S(1)}, f32[128,1024]{1,0:T(8,128)S(1)}, f32[128,1024]{1,0:T(8,128)S(1)}) custom-call(bf16[256,512]{1,0:T(8,128)(2,1)S(1)} %get-tuple-element.69.q0, bf16[128,512]{1,0:T(8,128)(2,1)S(1)} %get-tuple-element.70.q1, bf16[256,512]{1,0:T(8,128)(2,1)S(1)} %get-tuple-element.71.g_ref, ...), custom_call_target="tpu_custom_call" | custom-call | flops 1073741824 | bytes 1048576 | tf_op jit(solution)/shard_map/pallas_call | solution.py:534
  28.8 0.2 shard_map.85.after
  29.0 2.5 %collective-permute-start.8 = (bf16[256,1024]{1,0:T(8,128)(2,1)S(1)}, bf16[256,1024]{1,0:T(8,128)(2,1)S(1)}, u32[]{:S(2)}, u32[]{:S(2)}) collective-permute-start(bf16[256,1024]{1,0:T(8,128)(2,1)S(1)} %shard_map.85.after), channel_id=1, source_target_pairs={{4,8},{12,16},{20,24},{28,32},{36,40},{44,48},{52,56},{60,64},{68,... | collective-permute-start | bytes 1572872 | tf_op jit(solution)/shard_map/ppermute | solution.py:483
  31.5 4.0 %collective-permute-start.10 = (bf16[64,1024]{1,0:T(8,128)(2,1)S(1)}, bf16[64,1024]{1,0:T(8,128)(2,1)S(1)}, u32[]{:S(2)}, u32[]{:S(2)}) collective-permute-start(bf16[64,1024]{1,0:T(8,128)(2,1)S(1)} %get-tuple-element.119), channel_id=1, source_target_pairs={{0,20},{8,28},{16,36},{24,44},{32,52},{40,60},{48,68},{56,76},{64,... | collective-permute-start | bytes 393224 | tf_op jit(solution)/shard_map/ppermute | solution.py:483
  35.5 3.1 %collective-permute-start.13 = (bf16[32,1024]{1,0:T(8,128)(2,1)S(1)}, bf16[32,1024]{1,0:T(8,128)(2,1)S(1)}, u32[]{:S(2)}, u32[]{:S(2)}) collective-permute-start(bf16[32,1024]{1,0:T(8,128)(2,1)S(1)} %get-tuple-element.121), channel_id=1, source_target_pairs={{0,24},{4,28},{16,40},{20,44},{32,56},{36,60},{48,72},{52,76},{64,... | collective-permute-start | bytes 196616 | tf_op jit(solution)/shard_map/ppermute | solution.py:483
  38.6 2.7 %shard_map.86 = (bf16[256,512]{1,0:T(8,128)(2,1)}, bf16[256,512]{1,0:T(8,128)(2,1)}, f32[256,1024]{1,0:T(8,128)S(1)}, bf16[192,1024]{1,0:T(8,128)(2,1)S(1)}) custom-call(bf16[256,512]{1,0:T(8,128)(2,1)S(1)} %get-tuple-element.69.q0, bf16[128,512]{1,0:T(8,128)(2,1)S(1)} %get-tuple-element.70.q1, bf16[256,512]{1,0:T(8,128)(2,1)S(1)} %get-tuple-element.71.g_ref, ...), custom_call_target="tpu_custom_call" | custom-call | flops 536870912 | bytes 1048576 | tf_op jit(solution)/shard_map/pallas_call | solution.py:542
  41.3 1.3 %collective-permute-start.11 = (bf16[192,1024]{1,0:T(8,128)(2,1)S(1)}, bf16[192,1024]{1,0:T(8,128)(2,1)S(1)}, u32[]{:S(2)}, u32[]{:S(2)}) collective-permute-start(bf16[192,1024]{1,0:T(8,128)(2,1)S(1)} %get-tuple-element.120), channel_id=1, source_target_pairs={{0,4},{8,12},{16,20},{24,28},{32,36},{40,44},{48,52},{56,60},{64,6... | collective-permute-start | bytes 1179656 | tf_op jit(solution)/shard_map/ppermute | solution.py:483
  42.6 0.3 collective-permute-done.10.r2
  42.9 1.8 %collective-permute-done.8.r1 = bf16[256,1024]{1,0:T(8,128)(2,1)S(1)} collective-permute-done((bf16[256,1024]{1,0:T(8,128)(2,1)S(1)}, bf16[256,1024]{1,0:T(8,128)(2,1)S(1)}, u32[]{:S(2)}, u32[]{:S(2)}) %collective-permute-start.8) | collective-permute-done | bytes 524320 | tf_op jit(solution)/shard_map/ppermute | solution.py:483
  44.7 0.9 %collective-permute-start.12 = (bf16[64,1024]{1,0:T(8,128)(2,1)S(1)}, bf16[64,1024]{1,0:T(8,128)(2,1)S(1)}, u32[]{:S(2)}, u32[]{:S(2)}) collective-permute-start(bf16[64,1024]{1,0:T(8,128)(2,1)S(1)} %shard_map.88.after), channel_id=1, source_target_pairs={{0,4},{8,12},{16,20},{24,28},{32,36},{40,44},{48,52},{56,60},{64,6... | collective-permute-start | bytes 393224 | tf_op jit(solution)/shard_map/ppermute | solution.py:483
  45.6 0.2 shard_map.89.after.acc
  45.9 0.7 %collective-permute-done.12.got = bf16[64,1024]{1,0:T(8,128)(2,1)S(1)} collective-permute-done((bf16[64,1024]{1,0:T(8,128)(2,1)S(1)}, bf16[64,1024]{1,0:T(8,128)(2,1)S(1)}, u32[]{:S(2)}, u32[]{:S(2)}) %collective-permute-start.12) | collective-permute-done | bytes 131104 | tf_op jit(solution)/shard_map/ppermute | solution.py:483
  46.6 1.2 %shard_map.91 = (bf16[256,512]{1,0:T(8,128)(2,1)}, bf16[256,512]{1,0:T(8,128)(2,1)}) custom-call(f32[256,1024]{1,0:T(8,128)S(1)} %shard_map.89.after.acc, bf16[192,1024]{1,0:T(8,128)(2,1)S(1)} %collective-permute-done.11.near, bf16[64,1024]{1,0:T(8,128)(2,1)S(1)} %collective-permute-done.12.got, f32[64,1024]{1,0:T(8,128)S(1)} %shard_map.90.cross), custom_call_target="tpu_custom_call" | custom-call | tf_op jit(solution)/shard_map/pallas_call | solution.py:554
  (18 shorter events, 0.3 us)
Async XLA Ops:
  0.6 16.6 %copy-start.1 = (bf16[256,512]{1,0:T(8,128)(2,1)S(1)}, bf16[256,512]{1,0:T(8,128)(2,1)}, u32[]{:S(2)}) copy-start(bf16[256,512]{1,0:T(8,128)(2,1)} %g_ref.1) | copy-start | bytes 786436
  0.6 16.6 %copy-start = (bf16[256,512]{1,0:T(8,128)(2,1)S(1)}, bf16[256,512]{1,0:T(8,128)(2,1)}, u32[]{:S(2)}) copy-start(bf16[256,512]{1,0:T(8,128)(2,1)} %q_ref.1) | copy-start | bytes 786436
  0.7 2.3 %collective-permute-start = (bf16[256,512]{1,0:T(8,128)(2,1)}, bf16[256,512]{1,0:T(8,128)(2,1)S(1)}, u32[]{:S(2)}, u32[]{:S(2)}) collective-permute-start(bf16[256,512]{1,0:T(8,128)(2,1)} %param.5), channel_id=1, source_target_pairs={{0,4},{8,12},{16,20},{24,28},{32,36},{40,44},{48,52},{56,60},{64,6... | collective-permute-start | bytes 786440 | tf_op jit(solution)/shard_map/ppermute | solution.py:483
  1.4 1.7 %collective-permute-start.1 = (bf16[256,512]{1,0:T(8,128)(2,1)}, bf16[256,512]{1,0:T(8,128)(2,1)S(1)}, u32[]{:S(2)}, u32[]{:S(2)}) collective-permute-start(bf16[256,512]{1,0:T(8,128)(2,1)} %param.6), channel_id=1, source_target_pairs={{0,4},{8,12},{16,20},{24,28},{32,36},{40,44},{48,52},{56,60},{64,6... | collective-permute-start | bytes 786440 | tf_op jit(solution)/shard_map/ppermute | solution.py:483
  3.5 11.4 %collective-permute-start.2 = (bf16[64,1024]{1,0:T(8,128)(2,1)S(1)}, bf16[64,1024]{1,0:T(8,128)(2,1)S(1)}, u32[]{:S(2)}, u32[]{:S(2)}) collective-permute-start(bf16[64,1024]{1,0:T(8,128)(2,1)S(1)} %get-tuple-element.79), channel_id=1, source_target_pairs={{0,20},{8,28},{16,36},{24,44},{32,52},{40,60},{48,68},{56,76},{64,... | collective-permute-start | bytes 393224 | tf_op jit(solution)/shard_map/ppermute | solution.py:483
  11.6 12.0 %collective-permute-start.5 = (bf16[256,1024]{1,0:T(8,128)(2,1)S(1)}, bf16[256,1024]{1,0:T(8,128)(2,1)S(1)}, u32[]{:S(2)}, u32[]{:S(2)}) collective-permute-start(bf16[256,1024]{1,0:T(8,128)(2,1)S(1)} %get-tuple-element.81), channel_id=1, source_target_pairs={{4,8},{12,16},{20,24},{28,32},{36,40},{44,48},{52,56},{60,64},{68,... | collective-permute-start | bytes 1572872 | tf_op jit(solution)/shard_map/ppermute | solution.py:483
  14.9 8.6 %collective-permute-start.3 = (bf16[64,1024]{1,0:T(8,128)(2,1)S(1)}, bf16[64,1024]{1,0:T(8,128)(2,1)S(1)}, u32[]{:S(2)}, u32[]{:S(2)}) collective-permute-start(bf16[64,1024]{1,0:T(8,128)(2,1)S(1)} %collective-permute-done.2.r2), channel_id=1, source_target_pairs={{4,8},{20,24},{36,40},{52,56},{68,72},{84,88},{100,104},{116,120},... | collective-permute-start | bytes 393224 | tf_op jit(solution)/shard_map/ppermute | solution.py:483
  23.5 1.6 %collective-permute-start.4 = (bf16[128,1024]{1,0:T(8,128)(2,1)S(1)}, bf16[128,1024]{1,0:T(8,128)(2,1)S(1)}, u32[]{:S(2)}, u32[]{:S(2)}) collective-permute-start(bf16[128,1024]{1,0:T(8,128)(2,1)S(1)} %shard_map.78.after), channel_id=1, source_target_pairs={{0,4},{8,12},{16,20},{24,28},{32,36},{40,44},{48,52},{56,60},{64,6... | collective-permute-start | bytes 786440 | tf_op jit(solution)/shard_map/ppermute | solution.py:483
  23.8 2.0 %collective-permute-start.6 = (bf16[128,1024]{1,0:T(8,128)(2,1)S(1)}, bf16[128,1024]{1,0:T(8,128)(2,1)S(1)}, u32[]{:S(2)}, u32[]{:S(2)}) collective-permute-start(bf16[128,1024]{1,0:T(8,128)(2,1)S(1)} %get-tuple-element.91), channel_id=1, source_target_pairs={{0,4},{8,12},{16,20},{24,28},{32,36},{40,44},{48,52},{56,60},{64,6... | collective-permute-start | bytes 786440 | tf_op jit(solution)/shard_map/ppermute | solution.py:483
  27.0 1.8 %collective-permute-start.7 = (bf16[128,1024]{1,0:T(8,128)(2,1)S(1)}, bf16[128,1024]{1,0:T(8,128)(2,1)S(1)}, u32[]{:S(2)}, u32[]{:S(2)}) collective-permute-start(bf16[128,1024]{1,0:T(8,128)(2,1)S(1)} %get-tuple-element.112), channel_id=1, source_target_pairs={{0,4},{8,12},{16,20},{24,28},{32,36},{40,44},{48,52},{56,60},{64,6... | collective-permute-start | bytes 786440 | tf_op jit(solution)/shard_map/ppermute | solution.py:483
  27.7 3.8 %collective-permute-start.9 = (bf16[96,1024]{1,0:T(8,128)(2,1)S(1)}, bf16[96,1024]{1,0:T(8,128)(2,1)S(1)}, u32[]{:S(2)}, u32[]{:S(2)}) collective-permute-start(bf16[96,1024]{1,0:T(8,128)(2,1)S(1)} %get-tuple-element.118), channel_id=1, source_target_pairs={{0,4},{8,12},{16,20},{24,28},{32,36},{40,44},{48,52},{56,60},{64,6... | collective-permute-start | bytes 589832 | tf_op jit(solution)/shard_map/ppermute | solution.py:483
  29.0 15.7 %collective-permute-start.8 = (bf16[256,1024]{1,0:T(8,128)(2,1)S(1)}, bf16[256,1024]{1,0:T(8,128)(2,1)S(1)}, u32[]{:S(2)}, u32[]{:S(2)}) collective-permute-start(bf16[256,1024]{1,0:T(8,128)(2,1)S(1)} %shard_map.85.after), channel_id=1, source_target_pairs={{4,8},{12,16},{20,24},{28,32},{36,40},{44,48},{52,56},{60,64},{68,... | collective-permute-start | bytes 1572872 | tf_op jit(solution)/shard_map/ppermute | solution.py:483
  31.5 11.4 %collective-permute-start.10 = (bf16[64,1024]{1,0:T(8,128)(2,1)S(1)}, bf16[64,1024]{1,0:T(8,128)(2,1)S(1)}, u32[]{:S(2)}, u32[]{:S(2)}) collective-permute-start(bf16[64,1024]{1,0:T(8,128)(2,1)S(1)} %get-tuple-element.119), channel_id=1, source_target_pairs={{0,20},{8,28},{16,36},{24,44},{32,52},{40,60},{48,68},{56,76},{64,... | collective-permute-start | bytes 393224 | tf_op jit(solution)/shard_map/ppermute | solution.py:483
  35.5 10.3 %collective-permute-start.13 = (bf16[32,1024]{1,0:T(8,128)(2,1)S(1)}, bf16[32,1024]{1,0:T(8,128)(2,1)S(1)}, u32[]{:S(2)}, u32[]{:S(2)}) collective-permute-start(bf16[32,1024]{1,0:T(8,128)(2,1)S(1)} %get-tuple-element.121), channel_id=1, source_target_pairs={{0,24},{4,28},{16,40},{20,44},{32,56},{36,60},{48,72},{52,76},{64,... | collective-permute-start | bytes 196616 | tf_op jit(solution)/shard_map/ppermute | solution.py:483
  41.3 4.6 %collective-permute-start.11 = (bf16[192,1024]{1,0:T(8,128)(2,1)S(1)}, bf16[192,1024]{1,0:T(8,128)(2,1)S(1)}, u32[]{:S(2)}, u32[]{:S(2)}) collective-permute-start(bf16[192,1024]{1,0:T(8,128)(2,1)S(1)} %get-tuple-element.120), channel_id=1, source_target_pairs={{0,4},{8,12},{16,20},{24,28},{32,36},{40,44},{48,52},{56,60},{64,6... | collective-permute-start | bytes 1179656 | tf_op jit(solution)/shard_map/ppermute | solution.py:483
  44.7 1.9 %collective-permute-start.12 = (bf16[64,1024]{1,0:T(8,128)(2,1)S(1)}, bf16[64,1024]{1,0:T(8,128)(2,1)S(1)}, u32[]{:S(2)}, u32[]{:S(2)}) collective-permute-start(bf16[64,1024]{1,0:T(8,128)(2,1)S(1)} %shard_map.88.after), channel_id=1, source_target_pairs={{0,4},{8,12},{16,20},{24,28},{32,36},{40,44},{48,52},{56,60},{64,6... | collective-permute-start | bytes 393224 | tf_op jit(solution)/shard_map/ppermute | solution.py:483

commit v9 on v8

--- a/solution.py
+++ b/solution.py
@@ -508,9 +508,9 @@
         [heads(128), heads(128)],
         flops=1 << 33,
     )(query, out_grad, kv, near, s1)
-    (send,) = call(third_split_kernel, [rows(128)], specs="vva")(r2, r3, top)
-    got3 = swap(send, sibling)
-    outer1, send = call(second_split_kernel, [rows(128), rows(128)], specs="va")(r1, send)
+    outer1, send = call(second_split_kernel, [rows(128), rows(128)], specs="va")(r1, top)
+    (send3,) = call(third_split_kernel, [rows(128)], specs="vva")(r2, r3, send)
+    got3 = swap(send3, sibling)
     got2 = swap(send, sibling)
     top, zsum, ysum, eo0, eo1, mo0, mo1 = call(
         outer_kernel,

time: 48 us -> 47.9 us (level)
  transfers between devices with their start and end apart: 14 -> 14, of which waited for: 6 -> 8; matrix products, arithmetic and copies ran while one was open for 2% -> 2% of each run, Pallas kernels for 16% -> 16%
where the time goes in v9:
time: 47.9 us; the launch traced here: 47.6 us
  starting transfers between devices  26.2 us (55%)
  Pallas kernels  10.5 us (22%)
  waiting for transfers between devices  8.93 us (19%)
  other arithmetic  1.08 us (2%)
  between operations  0.88 us (2%)
    ppermute x14, starting transfers between devices, swap(): return lax.ppermute(value, 'seq', pairs + [(b, a) for a, b in pairs])  26.2 us
    ppermute x14, waiting for transfers between devices, swap(): return lax.ppermute(value, 'seq', pairs + [(b, a) for a, b in pairs])  8.93 us
    pallas_call x1, Pallas kernels, per_device(): call(rest_kernel, [out, out, rows(256, F32), rows(192)], [stat], flops=1...  2.67 us
    pallas_call x1, Pallas kernels, per_device(): call(local_kernel, [out, out, ((128, D), BF), ((64, D), BF), ((32, D), BF...  1.59 us
    pallas_call x1, Pallas kernels, per_device(): call(far_kernel, [out, stat, stat, stat, heads(32, BF), heads(32), heads(...  1.25 us
    pallas_call x1, Pallas kernels, per_device(): call(final_kernel, [out, out], [rows(256), pltpu.SemaphoreType.DMA((2 * H...  1.18 us
    concatenate x1, other arithmetic, per_device(): jnp.concatenate([key_rows, value_rows], axis=1)  1.08 us
  transfers between devices with their start and end apart: 14, of which 8 were waited for; matrix products, arithmetic and copies ran while one was open for 2% of the time, Pallas kernels for 16%

profile of v9, /device:TPU:11, one launch (start us, length us, event | category | flops | bytes accessed | tf_op | source)
XLA Modules:
  0.0 47.6 jit_solution(8258058707166538528)
XLA Ops:
  0.7 0.8 %collective-permute-start = (bf16[256,512]{1,0:T(8,128)(2,1)}, bf16[256,512]{1,0:T(8,128)(2,1)S(1)}, u32[]{:S(2)}, u32[]{:S(2)}) collective-permute-start(bf16[256,512]{1,0:T(8,128)(2,1)} %param.5), channel_id=1, source_target_pairs={{0,4},{8,12},{16,20},{24,28},{32,36},{40,44},{48,52},{56,60},{64,6... | collective-permute-start | bytes 786440 | tf_op jit(solution)/shard_map/ppermute | solution.py:483
  1.5 1.1 %pad_maximum_fusion.raw = bf16[256,1024]{1,0:T(8,128)(2,1)S(1)} fusion(bf16[256,512]{1,0:T(8,128)(2,1)} %param.6, bf16[256,512]{1,0:T(8,128)(2,1)} %param.5), kind=kLoop, calls=%fused_computation | loop fusion | flops 1048576 | bytes 1048576 | tf_op jit(solution)/shard_map/concatenate | solution.py:496
  2.6 0.3 shard_map.75
  2.9 0.2 collective-permute-done.1.vs
  3.2 0.4 shard_map.76
  3.5 8.1 %collective-permute-start.2 = (bf16[64,1024]{1,0:T(8,128)(2,1)S(1)}, bf16[64,1024]{1,0:T(8,128)(2,1)S(1)}, u32[]{:S(2)}, u32[]{:S(2)}) collective-permute-start(bf16[64,1024]{1,0:T(8,128)(2,1)S(1)} %get-tuple-element.79), channel_id=1, source_target_pairs={{0,20},{8,28},{16,36},{24,44},{32,52},{40,60},{48,68},{56,76},{64,... | collective-permute-start | bytes 393224 | tf_op jit(solution)/shard_map/ppermute | solution.py:483
  11.6 1.9 %collective-permute-start.4 = (bf16[256,1024]{1,0:T(8,128)(2,1)S(1)}, bf16[256,1024]{1,0:T(8,128)(2,1)S(1)}, u32[]{:S(2)}, u32[]{:S(2)}) collective-permute-start(bf16[256,1024]{1,0:T(8,128)(2,1)S(1)} %get-tuple-element.80), channel_id=1, source_target_pairs={{4,8},{12,16},{20,24},{28,32},{36,40},{44,48},{52,56},{60,64},{68,... | collective-permute-start | bytes 1572872 | tf_op jit(solution)/shard_map/ppermute | solution.py:483
  13.5 1.4 %collective-permute-done.2.r2 = bf16[64,1024]{1,0:T(8,128)(2,1)S(1)} collective-permute-done((bf16[64,1024]{1,0:T(8,128)(2,1)S(1)}, bf16[64,1024]{1,0:T(8,128)(2,1)S(1)}, u32[]{:S(2)}, u32[]{:S(2)}) %collective-permute-start.2) | collective-permute-done | bytes 131104 | tf_op jit(solution)/shard_map/ppermute | solution.py:483
  14.9 2.3 %collective-permute-start.3 = (bf16[64,1024]{1,0:T(8,128)(2,1)S(1)}, bf16[64,1024]{1,0:T(8,128)(2,1)S(1)}, u32[]{:S(2)}, u32[]{:S(2)}) collective-permute-start(bf16[64,1024]{1,0:T(8,128)(2,1)S(1)} %collective-permute-done.2.r2), channel_id=1, source_target_pairs={{4,8},{20,24},{36,40},{52,56},{68,72},{84,88},{100,104},{116,120},... | collective-permute-start | bytes 393224 | tf_op jit(solution)/shard_map/ppermute | solution.py:483
  17.2 1.6 %shard_map.77 = (bf16[256,512]{1,0:T(8,128)(2,1)S(1)}, bf16[256,512]{1,0:T(8,128)(2,1)S(1)}, bf16[128,512]{1,0:T(8,128)(2,1)S(1)}, bf16[64,512]{1,0:T(8,128)(2,1...) custom-call(bf16[256,512]{1,0:T(8,128)(2,1)S(1)} %copy-done, ...), custom_call_target="tpu_custom_call" | custom-call | flops 8589934592 | bytes 1048576 | tf_op jit(solution)/shard_map/pallas_call | solution.py:504
  18.8 3.3 %collective-permute-done.4.r1 = bf16[256,1024]{1,0:T(8,128)(2,1)S(1)} collective-permute-done((bf16[256,1024]{1,0:T(8,128)(2,1)S(1)}, bf16[256,1024]{1,0:T(8,128)(2,1)S(1)}, u32[]{:S(2)}, u32[]{:S(2)}) %collective-permute-start.4) | collective-permute-done | bytes 524320 | tf_op jit(solution)/shard_map/ppermute | solution.py:483
  22.2 1.3 %collective-permute-done.3.r3 = bf16[64,1024]{1,0:T(8,128)(2,1)S(1)} collective-permute-done((bf16[64,1024]{1,0:T(8,128)(2,1)S(1)}, bf16[64,1024]{1,0:T(8,128)(2,1)S(1)}, u32[]{:S(2)}, u32[]{:S(2)}) %collective-permute-start.3) | collective-permute-done | bytes 131104 | tf_op jit(solution)/shard_map/ppermute | solution.py:483
  23.6 0.5 %collective-permute-start.6 = (bf16[128,1024]{1,0:T(8,128)(2,1)S(1)}, bf16[128,1024]{1,0:T(8,128)(2,1)S(1)}, u32[]{:S(2)}, u32[]{:S(2)}) collective-permute-start(bf16[128,1024]{1,0:T(8,128)(2,1)S(1)} %get-tuple-element.82.after), channel_id=1, source_target_pairs={{0,4},{8,12},{16,20},{24,28},{32,36},{40,44},{48,52},{56,60},{64,6... | collective-permute-start | bytes 786440 | tf_op jit(solution)/shard_map/ppermute | solution.py:483
  24.1 0.8 %shard_map.80 = (f32[4,256,128]{2,1,0:T(8,128)S(1)}, f32[4,256,128]{2,1,0:T(8,128)S(1)}, f32[4,256,128]{2,1,0:T(8,128)S(1)}, f32[4,128,128]{2,1,0:T(8,128)S(1)},...) custom-call(bf16[256,512]{1,0:T(8,128)(2,1)S(1)} %get-tuple-element.69.q0, ...), custom_call_target="tpu_custom_call" | custom-call | flops 1073741824 | bytes 1048576 | tf_op jit(solution)/shard_map/pallas_call | solution.py:515
  24.9 0.2 collective-permute-done.5.got
  25.2 0.6 %shard_map.81 = (bf16[192,1024]{1,0:T(8,128)(2,1)S(1)}, f32[4,32,192]{2,1,0:T(8,128)S(1)}, f32[4,32,128]{2,1,0:T(8,128)S(1)}, f32[4,256,128]{2,1,0:T(8,128)S(1)}...) custom-call(bf16[32,512]{1,0:T(8,128)(2,1)S(1)} %get-tuple-element.78.q3, ...), custom_call_target="tpu_custom_call" | custom-call | flops 268435456 | bytes 1048576 | tf_op jit(solution)/shard_map/pallas_call | solution.py:521
  25.8 1.3 %shard_map.82 = (bf16[256,512]{1,0:T(8,128)(2,1)S(1)}, f32[4,256,128]{2,1,0:T(8,128)S(1)}, f32[4,256,128]{2,1,0:T(8,128)S(1)}, f32[4,256,128]{2,1,0:T(8,128)S(1)...) custom-call(bf16[64,512]{1,0:T(8,128)(2,1)S(1)} %get-tuple-element.7, ...), custom_call_target="tpu_custom_call" | custom-call | tf_op jit(solution)/shard_map/pallas_call | solution.py:524
  27.0 0.2 collective-permute-start.7
  27.2 0.5 shard_map.84
  27.7 0.5 collective-permute-start.9
  28.2 0.6 %shard_map.83 = (f32[4,128,128]{2,1,0:T(8,128)S(1)}, f32[4,128,128]{2,1,0:T(8,128)S(1)}, f32[128,1024]{1,0:T(8,128)S(1)}, f32[128,1024]{1,0:T(8,128)S(1)}) custom-call(bf16[256,512]{1,0:T(8,128)(2,1)S(1)} %get-tuple-element.69.q0, bf16[128,512]{1,0:T(8,128)(2,1)S(1)} %get-tuple-element.70.q1, bf16[256,512]{1,0:T(8,128)(2,1)S(1)} %get-tuple-element.71.g_ref, ...), custom_call_target="tpu_custom_call" | custom-call | flops 1073741824 | bytes 1048576 | tf_op jit(solution)/shard_map/pallas_call | solution.py:534
  29.0 2.5 %collective-permute-start.8 = (bf16[256,1024]{1,0:T(8,128)(2,1)S(1)}, bf16[256,1024]{1,0:T(8,128)(2,1)S(1)}, u32[]{:S(2)}, u32[]{:S(2)}) collective-permute-start(bf16[256,1024]{1,0:T(8,128)(2,1)S(1)} %shard_map.85.after), channel_id=1, source_target_pairs={{4,8},{12,16},{20,24},{28,32},{36,40},{44,48},{52,56},{60,64},{68,... | collective-permute-start | bytes 1572872 | tf_op jit(solution)/shard_map/ppermute | solution.py:483
  31.5 4.0 %collective-permute-start.10 = (bf16[64,1024]{1,0:T(8,128)(2,1)S(1)}, bf16[64,1024]{1,0:T(8,128)(2,1)S(1)}, u32[]{:S(2)}, u32[]{:S(2)}) collective-permute-start(bf16[64,1024]{1,0:T(8,128)(2,1)S(1)} %get-tuple-element.119), channel_id=1, source_target_pairs={{0,20},{8,28},{16,36},{24,44},{32,52},{40,60},{48,68},{56,76},{64,... | collective-permute-start | bytes 393224 | tf_op jit(solution)/shard_map/ppermute | solution.py:483
  35.5 3.1 %collective-permute-start.13 = (bf16[32,1024]{1,0:T(8,128)(2,1)S(1)}, bf16[32,1024]{1,0:T(8,128)(2,1)S(1)}, u32[]{:S(2)}, u32[]{:S(2)}) collective-permute-start(bf16[32,1024]{1,0:T(8,128)(2,1)S(1)} %get-tuple-element.121), channel_id=1, source_target_pairs={{0,24},{4,28},{16,40},{20,44},{32,56},{36,60},{48,72},{52,76},{64,... | collective-permute-start | bytes 196616 | tf_op jit(solution)/shard_map/ppermute | solution.py:483
  38.6 2.7 %shard_map.86 = (bf16[256,512]{1,0:T(8,128)(2,1)}, bf16[256,512]{1,0:T(8,128)(2,1)}, f32[256,1024]{1,0:T(8,128)S(1)}, bf16[192,1024]{1,0:T(8,128)(2,1)S(1)}) custom-call(bf16[256,512]{1,0:T(8,128)(2,1)S(1)} %get-tuple-element.69.q0, bf16[128,512]{1,0:T(8,128)(2,1)S(1)} %get-tuple-element.70.q1, bf16[256,512]{1,0:T(8,128)(2,1)S(1)} %get-tuple-element.71.g_ref, ...), custom_call_target="tpu_custom_call" | custom-call | flops 536870912 | bytes 1048576 | tf_op jit(solution)/shard_map/pallas_call | solution.py:542
  41.3 1.4 %collective-permute-start.11 = (bf16[192,1024]{1,0:T(8,128)(2,1)S(1)}, bf16[192,1024]{1,0:T(8,128)(2,1)S(1)}, u32[]{:S(2)}, u32[]{:S(2)}) collective-permute-start(bf16[192,1024]{1,0:T(8,128)(2,1)S(1)} %get-tuple-element.120), channel_id=1, source_target_pairs={{0,4},{8,12},{16,20},{24,28},{32,36},{40,44},{48,52},{56,60},{64,6... | collective-permute-start | bytes 1179656 | tf_op jit(solution)/shard_map/ppermute | solution.py:483
  42.6 0.6 %collective-permute-done.10.r2 = bf16[64,1024]{1,0:T(8,128)(2,1)S(1)} collective-permute-done((bf16[64,1024]{1,0:T(8,128)(2,1)S(1)}, bf16[64,1024]{1,0:T(8,128)(2,1)S(1)}, u32[]{:S(2)}, u32[]{:S(2)}) %collective-permute-start.10) | collective-permute-done | bytes 131104 | tf_op jit(solution)/shard_map/ppermute | solution.py:483
  43.3 1.2 %collective-permute-done.8.r1 = bf16[256,1024]{1,0:T(8,128)(2,1)S(1)} collective-permute-done((bf16[256,1024]{1,0:T(8,128)(2,1)S(1)}, bf16[256,1024]{1,0:T(8,128)(2,1)S(1)}, u32[]{:S(2)}, u32[]{:S(2)}) %collective-permute-start.8) | collective-permute-done | bytes 524320 | tf_op jit(solution)/shard_map/ppermute | solution.py:483
  44.5 0.9 %collective-permute-start.12 = (bf16[64,1024]{1,0:T(8,128)(2,1)S(1)}, bf16[64,1024]{1,0:T(8,128)(2,1)S(1)}, u32[]{:S(2)}, u32[]{:S(2)}) collective-permute-start(bf16[64,1024]{1,0:T(8,128)(2,1)S(1)} %shard_map.88.after), channel_id=1, source_target_pairs={{0,4},{8,12},{16,20},{24,28},{32,36},{40,44},{48,52},{56,60},{64,6... | collective-permute-start | bytes 393224 | tf_op jit(solution)/shard_map/ppermute | solution.py:483
  45.4 0.2 shard_map.89.after.acc
  45.7 0.7 %collective-permute-done.12.got = bf16[64,1024]{1,0:T(8,128)(2,1)S(1)} collective-permute-done((bf16[64,1024]{1,0:T(8,128)(2,1)S(1)}, bf16[64,1024]{1,0:T(8,128)(2,1)S(1)}, u32[]{:S(2)}, u32[]{:S(2)}) %collective-permute-start.12) | collective-permute-done | bytes 131104 | tf_op jit(solution)/shard_map/ppermute | solution.py:483
  46.4 1.2 %shard_map.91 = (bf16[256,512]{1,0:T(8,128)(2,1)}, bf16[256,512]{1,0:T(8,128)(2,1)}) custom-call(f32[256,1024]{1,0:T(8,128)S(1)} %shard_map.89.after.acc, bf16[192,1024]{1,0:T(8,128)(2,1)S(1)} %collective-permute-done.11.near, bf16[64,1024]{1,0:T(8,128)(2,1)S(1)} %collective-permute-done.12.got, f32[64,1024]{1,0:T(8,128)S(1)} %shard_map.90.cross), custom_call_target="tpu_custom_call" | custom-call | tf_op jit(solution)/shard_map/pallas_call | solution.py:554
  (18 shorter events, 0.6 us)
Async XLA Ops:
  0.6 16.6 %copy-start.1 = (bf16[256,512]{1,0:T(8,128)(2,1)S(1)}, bf16[256,512]{1,0:T(8,128)(2,1)}, u32[]{:S(2)}) copy-start(bf16[256,512]{1,0:T(8,128)(2,1)} %g_ref.1) | copy-start | bytes 786436
  0.6 16.6 %copy-start = (bf16[256,512]{1,0:T(8,128)(2,1)S(1)}, bf16[256,512]{1,0:T(8,128)(2,1)}, u32[]{:S(2)}) copy-start(bf16[256,512]{1,0:T(8,128)(2,1)} %q_ref.1) | copy-start | bytes 786436
  0.7 2.3 %collective-permute-start = (bf16[256,512]{1,0:T(8,128)(2,1)}, bf16[256,512]{1,0:T(8,128)(2,1)S(1)}, u32[]{:S(2)}, u32[]{:S(2)}) collective-permute-start(bf16[256,512]{1,0:T(8,128)(2,1)} %param.5), channel_id=1, source_target_pairs={{0,4},{8,12},{16,20},{24,28},{32,36},{40,44},{48,52},{56,60},{64,6... | collective-permute-start | bytes 786440 | tf_op jit(solution)/shard_map/ppermute | solution.py:483
  1.4 1.7 %collective-permute-start.1 = (bf16[256,512]{1,0:T(8,128)(2,1)}, bf16[256,512]{1,0:T(8,128)(2,1)S(1)}, u32[]{:S(2)}, u32[]{:S(2)}) collective-permute-start(bf16[256,512]{1,0:T(8,128)(2,1)} %param.6), channel_id=1, source_target_pairs={{0,4},{8,12},{16,20},{24,28},{32,36},{40,44},{48,52},{56,60},{64,6... | collective-permute-start | bytes 786440 | tf_op jit(solution)/shard_map/ppermute | solution.py:483
  3.5 11.4 %collective-permute-start.2 = (bf16[64,1024]{1,0:T(8,128)(2,1)S(1)}, bf16[64,1024]{1,0:T(8,128)(2,1)S(1)}, u32[]{:S(2)}, u32[]{:S(2)}) collective-permute-start(bf16[64,1024]{1,0:T(8,128)(2,1)S(1)} %get-tuple-element.79), channel_id=1, source_target_pairs={{0,20},{8,28},{16,36},{24,44},{32,52},{40,60},{48,68},{56,76},{64,... | collective-permute-start | bytes 393224 | tf_op jit(solution)/shard_map/ppermute | solution.py:483
  11.6 10.5 %collective-permute-start.4 = (bf16[256,1024]{1,0:T(8,128)(2,1)S(1)}, bf16[256,1024]{1,0:T(8,128)(2,1)S(1)}, u32[]{:S(2)}, u32[]{:S(2)}) collective-permute-start(bf16[256,1024]{1,0:T(8,128)(2,1)S(1)} %get-tuple-element.80), channel_id=1, source_target_pairs={{4,8},{12,16},{20,24},{28,32},{36,40},{44,48},{52,56},{60,64},{68,... | collective-permute-start | bytes 1572872 | tf_op jit(solution)/shard_map/ppermute | solution.py:483
  14.9 8.6 %collective-permute-start.3 = (bf16[64,1024]{1,0:T(8,128)(2,1)S(1)}, bf16[64,1024]{1,0:T(8,128)(2,1)S(1)}, u32[]{:S(2)}, u32[]{:S(2)}) collective-permute-start(bf16[64,1024]{1,0:T(8,128)(2,1)S(1)} %collective-permute-done.2.r2), channel_id=1, source_target_pairs={{4,8},{20,24},{36,40},{52,56},{68,72},{84,88},{100,104},{116,120},... | collective-permute-start | bytes 393224 | tf_op jit(solution)/shard_map/ppermute | solution.py:483
  23.5 1.6 %collective-permute-start.5 = (bf16[128,1024]{1,0:T(8,128)(2,1)S(1)}, bf16[128,1024]{1,0:T(8,128)(2,1)S(1)}, u32[]{:S(2)}, u32[]{:S(2)}) collective-permute-start(bf16[128,1024]{1,0:T(8,128)(2,1)S(1)} %shard_map.79), channel_id=1, source_target_pairs={{0,4},{8,12},{16,20},{24,28},{32,36},{40,44},{48,52},{56,60},{64,6... | collective-permute-start | bytes 786440 | tf_op jit(solution)/shard_map/ppermute | solution.py:483
  23.6 2.1 %collective-permute-start.6 = (bf16[128,1024]{1,0:T(8,128)(2,1)S(1)}, bf16[128,1024]{1,0:T(8,128)(2,1)S(1)}, u32[]{:S(2)}, u32[]{:S(2)}) collective-permute-start(bf16[128,1024]{1,0:T(8,128)(2,1)S(1)} %get-tuple-element.82.after), channel_id=1, source_target_pairs={{0,4},{8,12},{16,20},{24,28},{32,36},{40,44},{48,52},{56,60},{64,6... | collective-permute-start | bytes 786440 | tf_op jit(solution)/shard_map/ppermute | solution.py:483
  27.0 1.8 %collective-permute-start.7 = (bf16[128,1024]{1,0:T(8,128)(2,1)S(1)}, bf16[128,1024]{1,0:T(8,128)(2,1)S(1)}, u32[]{:S(2)}, u32[]{:S(2)}) collective-permute-start(bf16[128,1024]{1,0:T(8,128)(2,1)S(1)} %get-tuple-element.112), channel_id=1, source_target_pairs={{0,4},{8,12},{16,20},{24,28},{32,36},{40,44},{48,52},{56,60},{64,6... | collective-permute-start | bytes 786440 | tf_op jit(solution)/shard_map/ppermute | solution.py:483
  27.7 3.7 %collective-permute-start.9 = (bf16[96,1024]{1,0:T(8,128)(2,1)S(1)}, bf16[96,1024]{1,0:T(8,128)(2,1)S(1)}, u32[]{:S(2)}, u32[]{:S(2)}) collective-permute-start(bf16[96,1024]{1,0:T(8,128)(2,1)S(1)} %get-tuple-element.118), channel_id=1, source_target_pairs={{0,4},{8,12},{16,20},{24,28},{32,36},{40,44},{48,52},{56,60},{64,6... | collective-permute-start | bytes 589832 | tf_op jit(solution)/shard_map/ppermute | solution.py:483
  29.0 15.5 %collective-permute-start.8 = (bf16[256,1024]{1,0:T(8,128)(2,1)S(1)}, bf16[256,1024]{1,0:T(8,128)(2,1)S(1)}, u32[]{:S(2)}, u32[]{:S(2)}) collective-permute-start(bf16[256,1024]{1,0:T(8,128)(2,1)S(1)} %shard_map.85.after), channel_id=1, source_target_pairs={{4,8},{12,16},{20,24},{28,32},{36,40},{44,48},{52,56},{60,64},{68,... | collective-permute-start | bytes 1572872 | tf_op jit(solution)/shard_map/ppermute | solution.py:483
  31.5 11.8 %collective-permute-start.10 = (bf16[64,1024]{1,0:T(8,128)(2,1)S(1)}, bf16[64,1024]{1,0:T(8,128)(2,1)S(1)}, u32[]{:S(2)}, u32[]{:S(2)}) collective-permute-start(bf16[64,1024]{1,0:T(8,128)(2,1)S(1)} %get-tuple-element.119), channel_id=1, source_target_pairs={{0,20},{8,28},{16,36},{24,44},{32,52},{40,60},{48,68},{56,76},{64,... | collective-permute-start | bytes 393224 | tf_op jit(solution)/shard_map/ppermute | solution.py:483
  35.5 10.1 %collective-permute-start.13 = (bf16[32,1024]{1,0:T(8,128)(2,1)S(1)}, bf16[32,1024]{1,0:T(8,128)(2,1)S(1)}, u32[]{:S(2)}, u32[]{:S(2)}) collective-permute-start(bf16[32,1024]{1,0:T(8,128)(2,1)S(1)} %get-tuple-element.121), channel_id=1, source_target_pairs={{0,24},{4,28},{16,40},{20,44},{32,56},{36,60},{48,72},{52,76},{64,... | collective-permute-start | bytes 196616 | tf_op jit(solution)/shard_map/ppermute | solution.py:483
  41.3 4.4 %collective-permute-start.11 = (bf16[192,1024]{1,0:T(8,128)(2,1)S(1)}, bf16[192,1024]{1,0:T(8,128)(2,1)S(1)}, u32[]{:S(2)}, u32[]{:S(2)}) collective-permute-start(bf16[192,1024]{1,0:T(8,128)(2,1)S(1)} %get-tuple-element.120), channel_id=1, source_target_pairs={{0,4},{8,12},{16,20},{24,28},{32,36},{40,44},{48,52},{56,60},{64,6... | collective-permute-start | bytes 1179656 | tf_op jit(solution)/shard_map/ppermute | solution.py:483
  44.5 1.8 %collective-permute-start.12 = (bf16[64,1024]{1,0:T(8,128)(2,1)S(1)}, bf16[64,1024]{1,0:T(8,128)(2,1)S(1)}, u32[]{:S(2)}, u32[]{:S(2)}) collective-permute-start(bf16[64,1024]{1,0:T(8,128)(2,1)S(1)} %shard_map.88.after), channel_id=1, source_target_pairs={{0,4},{8,12},{16,20},{24,28},{32,36},{40,44},{48,52},{56,60},{64,6... | collective-permute-start | bytes 393224 | tf_op jit(solution)/shard_map/ppermute | solution.py:483
